TPU v7x, 32 devices: a whole 2x2x4 slice. The times are simulated.
32 devices in a mesh: fsdp: 4 (over z), ctx: 2 (over x), tp: 4 (over y, core).
Axes of the slice: x: 2, y: 2, z: 4, core: 2. Of those that a mesh axis runs over, the one named last changes fastest.
Arguments:
- tokens: bfloat16 [4, 2048, 1024], P(None, ('fsdp', 'ctx'), 'tp'), may hold values from -6 to 6
- time_embed: bfloat16 [4, 2048, 1024], P(None, ('fsdp', 'ctx'), 'tp'), may hold values from -3 to 3
- cotangent: bfloat16 [4, 2048, 1024], P(None, ('fsdp', 'ctx'), 'tp'), may hold values from -6 to 6
- segment_ids: int32 [4, 2048], P(None, 'fsdp'), may hold values from 0 to 31, as said below
- to_owner: int32 [4, 2048], P(None, ('fsdp', 'ctx')), may hold values from 0 to 2047, as said below
- from_owner: int32 [4, 2048], P(None, ('fsdp', 'ctx')), may hold values from 0 to 2047, as said below
- w_qkv: bfloat16 [2, 3, 1024, 1024], P(None, None, ('fsdp', 'ctx'), 'tp'), may hold values from -0.1875 to 0.1875
- w_out: bfloat16 [2, 1024, 1024], P(None, ('fsdp', 'ctx'), 'tp'), may hold values from -1.5 to 1.5
- w_up: bfloat16 [2, 1024, 4096], P(None, ('fsdp', 'ctx'), 'tp'), may hold values from -0.1875 to 0.1875
- w_down: bfloat16 [2, 1024, 4096], P(None, ('fsdp', 'ctx'), 'tp'), may hold values from -0.125 to 0.125
- biases: float32 [2, 4, 1024], P(None, None, 'tp'), may hold values from -3 to 3
- norm_gain: float32 [2, 2, 1024], P(None, None, 'tp'), may hold values from 0.5 to 1.5
- norm_bias: float32 [2, 2, 1024], P(None, None, 'tp'), may hold values from -3 to 3
- up_bias: float32 [2, 4096], P(None, 'tp'), may hold values from -3 to 3
Outputs:
- outputs: float32 [4, 2048, 1024], P(None, ('fsdp', 'ctx'), 'tp')
- input_grad: float32 [4, 2048, 1024], P(None, ('fsdp', 'ctx'), 'tp')
- w_qkv_grad: float32 [2, 3, 1024, 1024], P(None, None, ('fsdp', 'ctx'), 'tp')
- w_out_grad: float32 [2, 1024, 1024], P(None, ('fsdp', 'ctx'), 'tp')
- w_up_grad: float32 [2, 1024, 4096], P(None, ('fsdp', 'ctx'), 'tp')
- w_down_grad: float32 [2, 1024, 4096], P(None, ('fsdp', 'ctx'), 'tp')
- biases_grad: float32 [2, 4, 1024], P(None, None, 'tp')
- norm_gain_grad: float32 [2, 2, 1024], P(None, None, 'tp')
- norm_bias_grad: float32 [2, 2, 1024], P(None, None, 'tp')
- up_bias_grad: float32 [2, 4096], P(None, 'tp')
Inputs may be any that keep to these rules, and one draw needn't show every extreme that they name: `to_owner`: for each micro-batch a permutation of the 2048 positions; every aligned block of 256 given positions sends exactly 32 tokens into every aligned block of 256 balanced positions. `from_owner`: for each micro-batch the inverse of to_owner. `segment_ids`: within the b-th aligned block of 512 tokens the numbers lie in 8 * b to 8 * b + 7, never fall, and the block's last token has 8 * b + 7; a sequence has 64 tokens or more; in every micro-batch some block other than the first is one sequence of 512 tokens, and every other block begins with number 8 * b.
All inputs are finite; a program needn't handle non-finite values.
Results may differ from a plain program's by a relative error of at most 0.025.
Values may be sent and summed in bfloat16 or wider, within the bound.
A program may use at most 256 MiB of HBM per device.

v0:
```python
import functools
import math

import jax
import jax.numpy as jnp
from jax import lax
from jax.sharding import PartitionSpec as P

D = 1024
HD = 64


NEG = -1e30
EPS = 1e-05


def features_full(values):
    return lax.all_gather(values, "tp", axis=1, tiled=True)


def partial_total(values):
    return lax.psum_scatter(
        values.astype(jnp.bfloat16), "tp", scatter_dimension=1, tiled=True
    ).astype(jnp.float32)


def gradient_full(values):
    return lax.all_gather(values, "tp", axis=1, tiled=True)


def gradient_total(values):
    return lax.psum_scatter(
        values.astype(jnp.bfloat16), "tp", scatter_dimension=1, tiled=True
    ).astype(jnp.float32)


def norm_forward(residual, gain_row, offset):
    row_stats = lax.psum((jnp.sum(residual, axis=1), jnp.sum(residual * residual, axis=1)), "tp")
    row_mean = row_stats[0] / D
    row_var = row_stats[1] / D - row_mean * row_mean
    row_scale = lax.rsqrt(row_var + EPS)[:, None]
    normed = (residual - row_mean[:, None]) * row_scale
    return (normed * gain_row + offset, normed, row_scale)


def norm_backward(upstream, normed, row_scale, gain_row):
    scaled = upstream * gain_row
    row_stats = lax.psum((jnp.sum(scaled, axis=1), jnp.sum(scaled * normed, axis=1)), "tp")
    downstream = row_scale * (
        scaled - row_stats[0][:, None] / D - normed * (row_stats[1][:, None] / D)
    )
    return (downstream, jnp.sum(upstream * normed, axis=0), jnp.sum(upstream, axis=0))


def block_scores(queries, key_rows, query_seg, key_seg, block_index, block_rows):
    first_row = block_index * block_rows
    key_block = key_rows[first_row : first_row + block_rows]
    raw_scores = jnp.einsum(
        "qhd,khd->hqk", queries, key_block, preferred_element_type=jnp.float32
    ) * (1.0 / math.sqrt(HD))
    same_seq = (query_seg[:, None] == key_seg[first_row : first_row + block_rows][None, :])[None]
    return (jnp.where(same_seq, raw_scores, NEG), same_seq)


def first_pass(queries, key_rows, query_seg, key_seg, block_index, block_rows, carried):
    row_top, row_total = carried
    masked, same_seq = block_scores(queries, key_rows, query_seg, key_seg, block_index, block_rows)
    new_top = jnp.maximum(row_top, jnp.max(masked, axis=2))
    weighted = jnp.where(same_seq, jnp.exp(masked - new_top[:, :, None]), 0.0)
    return (new_top, row_total * jnp.exp(row_top - new_top) + jnp.sum(weighted, axis=2))


def second_pass(
    queries, key_rows, value_rows, query_seg, key_seg, log_total, block_index, block_rows, gathered
):
    masked, same_seq = block_scores(queries, key_rows, query_seg, key_seg, block_index, block_rows)
    soft_low = jnp.where(same_seq, jnp.exp(masked - log_total[:, :, None]), 0.0).astype(
        jnp.bfloat16
    )
    first_row = block_index * block_rows
    value_block = value_rows[first_row : first_row + block_rows]
    return gathered + jnp.einsum(
        "hqk,khd->qhd", soft_low, value_block, preferred_element_type=jnp.float32
    )


def delta_pass(
    queries,
    key_rows,
    value_rows,
    query_seg,
    key_seg,
    log_total,
    grad_heads,
    block_index,
    block_rows,
    row_delta,
):
    masked, same_seq = block_scores(queries, key_rows, query_seg, key_seg, block_index, block_rows)
    soft_rows = jnp.where(same_seq, jnp.exp(masked - log_total[:, :, None]), 0.0)
    first_row = block_index * block_rows
    grad_soft = jnp.einsum(
        "qhd,khd->hqk",
        grad_heads,
        value_rows[first_row : first_row + block_rows],
        preferred_element_type=jnp.float32,
    )
    return row_delta + jnp.sum(soft_rows * grad_soft, axis=2)


def gradient_pass(
    queries,
    key_rows,
    value_rows,
    query_seg,
    key_seg,
    log_total,
    grad_heads,
    row_delta,
    block_index,
    block_rows,
    carried,
):
    masked, same_seq = block_scores(queries, key_rows, query_seg, key_seg, block_index, block_rows)
    soft_rows = jnp.where(same_seq, jnp.exp(masked - log_total[:, :, None]), 0.0)
    first_row = block_index * block_rows
    key_block = key_rows[first_row : first_row + block_rows]
    value_block = value_rows[first_row : first_row + block_rows]
    grad_soft = jnp.einsum(
        "qhd,khd->hqk", grad_heads, value_block, preferred_element_type=jnp.float32
    )
    grad_scores = (soft_rows * (grad_soft - row_delta[:, :, None])).astype(jnp.bfloat16)
    score_scale = 1.0 / math.sqrt(HD)
    grad_queries = (
        carried[0]
        + jnp.einsum("hqk,khd->qhd", grad_scores, key_block, preferred_element_type=jnp.float32)
        * score_scale
    )
    grad_keys = (
        jnp.einsum("hqk,qhd->khd", grad_scores, queries, preferred_element_type=jnp.float32)
        * score_scale
    )
    grad_values = jnp.einsum(
        "hqk,qhd->khd",
        soft_rows.astype(jnp.bfloat16),
        grad_heads,
        preferred_element_type=jnp.float32,
    )
    return (grad_queries, grad_keys, grad_values)


def split_heads(values):
    return values.reshape(values.shape[0], values.shape[1] // HD, HD)


def attend_forward(query_low, key_pack, value_pack, query_seg, key_seg):
    queries = split_heads(query_low)
    key_rows = split_heads(key_pack)
    value_rows = split_heads(value_pack)
    row_count, head_count = (queries.shape[0], queries.shape[1])
    block_rows = key_rows.shape[0] // 4
    carried = (
        jnp.full((head_count, row_count), NEG, jnp.float32),
        jnp.zeros((head_count, row_count), jnp.float32),
    )
    for block_index in range(4):
        block_work = functools.partial(
            first_pass, queries, key_rows, query_seg, key_seg, block_index, block_rows
        )
        carried = block_work(carried)
    log_total = carried[0] + jnp.log(carried[1])
    gathered = jnp.zeros((row_count, head_count, HD), jnp.float32)
    for block_index in range(4):
        block_work = functools.partial(
            second_pass,
            queries,
            key_rows,
            value_rows,
            query_seg,
            key_seg,
            log_total,
            block_index,
            block_rows,
        )
        gathered = block_work(gathered)
    return (log_total, gathered.reshape(row_count, head_count * HD))


def attend_backward(grad_low, query_low, key_pack, value_pack, log_total, query_seg, key_seg):
    queries = split_heads(query_low)
    key_rows = split_heads(key_pack)
    value_rows = split_heads(value_pack)
    grad_heads = split_heads(grad_low)
    row_count, head_count = (queries.shape[0], queries.shape[1])
    block_rows = key_rows.shape[0] // 4
    row_delta = jnp.zeros((head_count, row_count), jnp.float32)
    for block_index in range(4):
        block_work = functools.partial(
            delta_pass,
            queries,
            key_rows,
            value_rows,
            query_seg,
            key_seg,
            log_total,
            grad_heads,
            block_index,
            block_rows,
        )
        row_delta = block_work(row_delta)
    grad_queries = jnp.zeros((row_count, head_count, HD), jnp.float32)
    empty_block = jnp.zeros((block_rows, head_count, HD), jnp.float32)
    key_parts = []
    value_parts = []
    for block_index in range(4):
        block_work = functools.partial(
            gradient_pass,
            queries,
            key_rows,
            value_rows,
            query_seg,
            key_seg,
            log_total,
            grad_heads,
            row_delta,
            block_index,
            block_rows,
        )
        carried = block_work((grad_queries, empty_block, empty_block))
        grad_queries = carried[0]
        key_parts.append(carried[1])
        value_parts.append(carried[2])
    key_grads = jnp.concatenate(key_parts, axis=0)
    value_grads = jnp.concatenate(value_parts, axis=0)
    width_heads = head_count * HD
    return (
        grad_queries.reshape(row_count, width_heads),
        key_grads.reshape(-1, width_heads),
        value_grads.reshape(-1, width_heads),
    )


def exact_gelu(values):
    return jax.nn.gelu(values, approximate=False)


def layer_forward(residual, weights, vector_set, query_seg, key_seg):
    w_qkv, w_out, w_up, w_down = weights
    bias_rows, gain_rows, offsets, up_offset = vector_set
    act_full = features_full(residual.astype(jnp.bfloat16))
    projected = jnp.einsum("td,cdh->cth", act_full, w_qkv, preferred_element_type=jnp.float32)
    query_low = (projected[0] + bias_rows[0]).astype(jnp.bfloat16)
    key_low = projected[1].astype(jnp.bfloat16)
    value_low = (projected[2] + bias_rows[1]).astype(jnp.bfloat16)
    key_pack, value_pack = (
        lax.all_gather(key_low, "ctx", axis=0, tiled=True),
        lax.all_gather(value_low, "ctx", axis=0, tiled=True),
    )
    log_total, attended = attend_forward(query_low, key_pack, value_pack, query_seg, key_seg)
    attended_low = attended.astype(jnp.bfloat16)
    mixed = jnp.einsum("th,dh->td", attended_low, w_out, preferred_element_type=jnp.float32)
    resid_one = partial_total(mixed) + bias_rows[2] + residual
    hidden, normed_one, scale_one = norm_forward(resid_one, gain_rows[0], offsets[0])
    hidden_full = features_full(hidden.astype(jnp.bfloat16))
    upper = jnp.dot(hidden_full, w_up, preferred_element_type=jnp.float32) + up_offset
    gelu_low = exact_gelu(upper).astype(jnp.bfloat16)
    lowered = jnp.einsum("tf,df->td", gelu_low, w_down, preferred_element_type=jnp.float32)
    resid_two = partial_total(lowered) + bias_rows[3] + hidden
    output, normed_two, scale_two = norm_forward(resid_two, gain_rows[1], offsets[1])
    saved = (
        act_full,
        query_low,
        key_pack,
        value_pack,
        log_total,
        attended_low,
        normed_one,
        scale_one,
        hidden_full,
        upper,
        gelu_low,
        normed_two,
        scale_two,
    )
    return (output, saved)


def layer_backward(upstream, saved, weights, vector_set, query_seg, key_seg):
    w_qkv, w_out, w_up, w_down = weights
    bias_rows, gain_rows, offsets, up_offset = vector_set
    (
        act_full,
        query_low,
        key_pack,
        value_pack,
        log_total,
        attended_low,
        normed_one,
        scale_one,
        hidden_full,
        upper,
        gelu_low,
        normed_two,
        scale_two,
    ) = saved
    grad_two, gain_two, offset_two = norm_backward(upstream, normed_two, scale_two, gain_rows[1])
    grad_lowered = gradient_full(grad_two.astype(jnp.bfloat16))
    grad_w_down = jnp.einsum(
        "td,tf->df", grad_lowered, gelu_low, preferred_element_type=jnp.float32
    )
    grad_gelu = jnp.dot(grad_lowered, w_down, preferred_element_type=jnp.float32).astype(
        jnp.bfloat16
    )
    gelu_value, gelu_pull = jax.vjp(exact_gelu, upper)
    grad_upper = gelu_pull(grad_gelu.astype(jnp.float32))[0].astype(jnp.bfloat16)
    grad_up_offset = jnp.sum(grad_upper, axis=0, dtype=jnp.float32)
    grad_w_up = jnp.einsum("td,tf->df", hidden_full, grad_upper, preferred_element_type=jnp.float32)
    grad_hidden = (
        gradient_total(
            jnp.einsum("tf,df->td", grad_upper, w_up, preferred_element_type=jnp.float32)
        )
        + grad_two
    )
    grad_one, gain_one, offset_one = norm_backward(grad_hidden, normed_one, scale_one, gain_rows[0])
    grad_mixed = gradient_full(grad_one.astype(jnp.bfloat16))
    grad_w_out = jnp.einsum(
        "td,th->dh", grad_mixed, attended_low, preferred_element_type=jnp.float32
    )
    grad_attended = jnp.dot(grad_mixed, w_out, preferred_element_type=jnp.float32).astype(
        jnp.bfloat16
    )
    grad_queries, key_grads, value_grads = attend_backward(
        grad_attended, query_low, key_pack, value_pack, log_total, query_seg, key_seg
    )
    grad_keys, grad_values = (
        lax.psum_scatter(
            key_grads.astype(jnp.bfloat16), "ctx", scatter_dimension=0, tiled=True
        ).astype(jnp.float32),
        lax.psum_scatter(
            value_grads.astype(jnp.bfloat16), "ctx", scatter_dimension=0, tiled=True
        ).astype(jnp.float32),
    )
    grad_proj = jnp.stack([grad_queries, grad_keys, grad_values]).astype(jnp.bfloat16)
    grad_w_qkv = jnp.einsum("td,cth->cdh", act_full, grad_proj, preferred_element_type=jnp.float32)
    grad_act = gradient_total(
        jnp.einsum("cth,cdh->td", grad_proj, w_qkv, preferred_element_type=jnp.float32)
    )
    grad_bias_rows = jnp.stack(
        [
            jnp.sum(grad_proj[0], axis=0, dtype=jnp.float32),
            jnp.sum(grad_proj[2], axis=0, dtype=jnp.float32),
            jnp.sum(grad_one, axis=0),
            jnp.sum(grad_two, axis=0),
        ]
    )
    matrices = (grad_w_qkv, grad_w_out, grad_w_up, grad_w_down)
    vectors = (
        grad_bias_rows,
        jnp.stack([gain_one, gain_two]),
        jnp.stack([offset_one, offset_two]),
        grad_up_offset,
    )
    return (grad_act + grad_one, matrices, vectors)


def reduce_grads(matrices, vectors):
    shards = (
        lax.psum_scatter(matrices[0], ("fsdp", "ctx"), scatter_dimension=2, tiled=True),
        lax.psum_scatter(matrices[1], ("fsdp", "ctx"), scatter_dimension=1, tiled=True),
        lax.psum_scatter(matrices[2], ("fsdp", "ctx"), scatter_dimension=1, tiled=True),
        lax.psum_scatter(matrices[3], ("fsdp", "ctx"), scatter_dimension=1, tiled=True),
    )
    summed = lax.psum(vectors, ("fsdp", "ctx"))
    return (shards, summed)


def add_trees(first_tree, second_tree):
    return jax.tree.map(
        lambda left_value, right_value: left_value + right_value, first_tree, second_tree
    )


def local(
    tokens,
    time_embed,
    cotangent,
    segment_ids,
    to_owner,
    from_owner,
    w_qkv,
    w_out,
    w_up,
    w_down,
    biases,
    norm_gain,
    norm_bias,
    up_bias,
):
    micro_count, row_count, width_local = tokens.shape
    layers = w_qkv.shape[0]
    groups = lax.axis_size(("fsdp", "ctx"))
    send_rows = row_count // groups
    embedded = (tokens.astype(jnp.float32) + time_embed.astype(jnp.float32)).astype(jnp.bfloat16)
    send_order = jnp.argsort(to_owner // row_count, axis=1, stable=True)
    owner_order = jnp.argsort(from_owner, axis=1, stable=True)
    arrive_rank = jnp.argsort(owner_order, axis=1, stable=True)
    return_rank = jnp.argsort(send_order, axis=1, stable=True)

    def grouped(values, row_order):
        picked = jnp.take_along_axis(values, row_order[:, :, None], axis=1)
        return picked.reshape(micro_count, groups, send_rows, values.shape[2])

    def placed(values, row_rank):
        flat_rows = values.reshape(micro_count, row_count, values.shape[3])
        return jnp.take_along_axis(flat_rows, row_rank[:, :, None], axis=1)

    arrived = (
        lax.all_to_all(
            grouped(embedded, send_order), ("fsdp", "ctx"), split_axis=1, concat_axis=1, tiled=True
        ),
        lax.all_to_all(
            grouped(cotangent, send_order), ("fsdp", "ctx"), split_axis=1, concat_axis=1, tiled=True
        ),
    )
    balanced = placed(arrived[0], arrive_rank)
    cot_balanced = placed(arrived[1], arrive_rank)
    full_weights = []
    vector_sets = []
    for layer_index in range(layers):
        full_weights.append(
            (
                lax.all_gather(w_qkv[layer_index], ("fsdp", "ctx"), axis=1, tiled=True),
                lax.all_gather(w_out[layer_index], ("fsdp", "ctx"), axis=0, tiled=True),
                lax.all_gather(w_up[layer_index], ("fsdp", "ctx"), axis=0, tiled=True),
                lax.all_gather(w_down[layer_index], ("fsdp", "ctx"), axis=0, tiled=True),
            )
        )
        vector_sets.append(
            (
                biases[layer_index],
                norm_gain[layer_index],
                norm_bias[layer_index],
                up_bias[layer_index],
            )
        )
    ctx_start = lax.axis_index("ctx") * row_count
    final_rows = []
    input_rows = []
    matrix_total = None
    vector_total = None
    for micro_index in range(micro_count):
        key_seg = segment_ids[micro_index]
        query_seg = lax.dynamic_slice_in_dim(key_seg, ctx_start, row_count)
        residual = balanced[micro_index].astype(jnp.float32)
        saved_layers = []
        for layer_index in range(layers):
            residual, saved = layer_forward(
                residual, full_weights[layer_index], vector_sets[layer_index], query_seg, key_seg
            )
            saved_layers.append(saved)
        final_rows.append(residual)
        upstream = cot_balanced[micro_index].astype(jnp.float32)
        matrix_parts = [None] * layers
        vector_parts = [None] * layers
        for layer_index in reversed(range(layers)):
            upstream, matrix_parts[layer_index], vector_parts[layer_index] = layer_backward(
                upstream,
                saved_layers[layer_index],
                full_weights[layer_index],
                vector_sets[layer_index],
                query_seg,
                key_seg,
            )
        input_rows.append(upstream)
        matrices = tuple(
            (jnp.stack([layer_part[member] for layer_part in matrix_parts]) for member in range(4))
        )
        vectors = tuple(
            (jnp.stack([layer_part[member] for layer_part in vector_parts]) for member in range(4))
        )
        matrices, vectors = (matrices, vectors)
        if micro_index == 0:
            matrix_total = matrices
            vector_total = vectors
        else:
            matrix_total = add_trees(matrix_total, matrices)
            vector_total = add_trees(vector_total, vectors)
    matrix_total, vector_total = reduce_grads(matrix_total, vector_total)
    final_stack = jnp.stack(final_rows)
    input_stack = jnp.stack(input_rows)
    returned = (
        lax.all_to_all(
            grouped(final_stack, owner_order).astype(jnp.bfloat16),
            ("fsdp", "ctx"),
            split_axis=1,
            concat_axis=1,
            tiled=True,
        ).astype(jnp.float32),
        lax.all_to_all(
            grouped(input_stack, owner_order).astype(jnp.bfloat16),
            ("fsdp", "ctx"),
            split_axis=1,
            concat_axis=1,
            tiled=True,
        ).astype(jnp.float32),
    )
    outputs = placed(returned[0], return_rank)
    input_grad = placed(returned[1], return_rank)
    return (
        outputs,
        input_grad,
        matrix_total[0],
        matrix_total[1],
        matrix_total[2],
        matrix_total[3],
        vector_total[0],
        vector_total[1],
        vector_total[2],
        vector_total[3],
    )


def solution(mesh):
    placed = (
        P(None, ("fsdp", "ctx"), "tp"),
        P(None, ("fsdp", "ctx"), "tp"),
        P(None, ("fsdp", "ctx"), "tp"),
        P(None, "fsdp"),
        P(None, ("fsdp", "ctx")),
        P(None, ("fsdp", "ctx")),
        P(None, None, ("fsdp", "ctx"), "tp"),
        P(None, ("fsdp", "ctx"), "tp"),
        P(None, ("fsdp", "ctx"), "tp"),
        P(None, ("fsdp", "ctx"), "tp"),
        P(None, None, "tp"),
        P(None, None, "tp"),
        P(None, None, "tp"),
        P(None, "tp"),
    )
    return jax.shard_map(
        local,
        mesh=mesh,
        in_specs=placed,
        out_specs=(
            P(None, ("fsdp", "ctx"), "tp"),
            P(None, ("fsdp", "ctx"), "tp"),
            P(None, None, ("fsdp", "ctx"), "tp"),
            P(None, ("fsdp", "ctx"), "tp"),
            P(None, ("fsdp", "ctx"), "tp"),
            P(None, ("fsdp", "ctx"), "tp"),
            P(None, None, "tp"),
            P(None, None, "tp"),
            P(None, None, "tp"),
            P(None, "tp"),
        ),
        check_vma=False,
    )
```

profile of v0, /device:TPU:8, one launch (start us, length us, event | category | flops | bytes accessed | tf_op | source)
XLA Modules:
  0.0 2150.3 jit_solution(3790419329910080398)
XLA Ops:
  43.5 18.4 all-to-all-done.2
  69.2 34.7 %all-gather.3 = bf16[1,1024,256]{2,1,0:T(8,128)(2,1)S(1)} all-gather(bf16[1,128,256]{2,1,0:T(8,128)(2,1)S(1)} %get-tuple-element.460), channel_id=5, replica_groups=mesh['fsdp'=4,'ctx'=2,'tp'=4] {'fsdp','ctx'}, dimensions={1}, use_global_device_ids=true | all-gather | bytes 589824 | tf_op jit(solution)/shard_map/all_gather | solution.py:433
  139.8 7.7 all-gather
  233.1 24.6 %reduce-scatter.69.cloned.1.call-done = bf16[256,256]{1,0:T(8,128)(2,1)} async-done(((bf16[256,1024]{1,0:T(8,128)(2,1)}), bf16[256,256]{1,0:T(8,128)(2,1)}) %reduce-scatter.69.cloned.1.call-update) | async-done | bytes 131088 | tf_op jit(solution)/shard_map/reduce_scatter | solution.py:22
  257.7 24.9 %reduce-scatter.77.cloned.1.call-done = bf16[256,256]{1,0:T(8,128)(2,1)} async-done(((bf16[256,1024]{1,0:T(8,128)(2,1)}), bf16[256,256]{1,0:T(8,128)(2,1)}) %reduce-scatter.77.cloned.1.call-update) | async-done | bytes 131088 | tf_op jit(solution)/shard_map/reduce_scatter | solution.py:22
  304.5 23.0 %all-gather.31.cloned.1.call-done = bf16[1,1024,1024]{2,1,0:T(8,128)(2,1)} async-done(((bf16[1,128,1024]{2,1,0:T(8,128)(2,1)}), bf16[1,1024,1024]{2,1,0:T(8,128)(2,1)}) %all-gather.31.cloned.1.call-update) | async-done | bytes 2097168 | tf_op jit(solution)/shard_map/all_gather | solution.py:435
  337.8 7.7 all_gather.203
  360.3 14.9 reduce-scatter.63.cloned.1.call-done
  390.5 29.6 %all-gather.8 = bf16[1,1024,256]{2,1,0:T(8,128)(2,1)S(1)} all-gather(bf16[1,128,256]{2,1,0:T(8,128)(2,1)S(1)} %get-tuple-element.459), channel_id=10, replica_groups=mesh['fsdp'=4,'ctx'=2,'tp'=4] {'fsdp','ctx'}, dimensions={1}, use_global_device_ids=true | all-gather | bytes 589824 | tf_op jit(solution)/shard_map/all_gather | solution.py:433
  526.9 12.1 reduce-scatter.65.cloned.1.call-done
  539.0 24.0 %reduce-scatter.73.cloned.1.call-done = bf16[256,256]{1,0:T(8,128)(2,1)} async-done(((bf16[256,1024]{1,0:T(8,128)(2,1)}), bf16[256,256]{1,0:T(8,128)(2,1)}) %reduce-scatter.73.cloned.1.call-update) | async-done | bytes 131088 | tf_op jit(solution)/shard_map/reduce_scatter | solution.py:22
  594.0 20.4 reduce-scatter.81.cloned.1.call-done
  628.4 7.6 all_gather.181
  636.0 9.4 all-gather.35.cloned.1.call-done
  651.5 44.0 %all-gather.37.cloned.1.call-done = bf16[1,1024,1024]{2,1,0:T(8,128)(2,1)} async-done(((bf16[1,128,1024]{2,1,0:T(8,128)(2,1)}), bf16[1,1024,1024]{2,1,0:T(8,128)(2,1)}) %all-gather.37.cloned.1.call-update) | async-done | bytes 2097168 | tf_op jit(solution)/shard_map/all_gather | solution.py:435
  706.2 8.6 all_gather.199
  732.5 10.8 reduce-scatter.67.cloned.1.call-done
  743.3 24.0 %reduce-scatter.75.cloned.1.call-done = bf16[256,256]{1,0:T(8,128)(2,1)} async-done(((bf16[256,1024]{1,0:T(8,128)(2,1)}), bf16[256,256]{1,0:T(8,128)(2,1)}) %reduce-scatter.75.cloned.1.call-update) | async-done | bytes 131088 | tf_op jit(solution)/shard_map/reduce_scatter | solution.py:22
  784.3 22.2 %reduce-scatter.83.cloned.1.call-done = bf16[256,256]{1,0:T(8,128)(2,1)} async-done(((bf16[256,1024]{1,0:T(8,128)(2,1)}), bf16[256,256]{1,0:T(8,128)(2,1)}) %reduce-scatter.83.cloned.1.call-update) | async-done | bytes 131088 | tf_op jit(solution)/shard_map/reduce_scatter | solution.py:22
  864.9 7.5 all_gather.220
  878.9 7.7 all_gather.212
  894.9 20.5 reduce-scatter.133.cloned.1.call-done
  915.4 24.3 %reduce-scatter.101.cloned.1.call-done = bf16[256,256]{1,0:T(8,128)(2,1)} async-done(((bf16[256,1024]{1,0:T(8,128)(2,1)}), bf16[256,256]{1,0:T(8,128)(2,1)}) %reduce-scatter.101.cloned.1.call-update) | async-done | bytes 131088 | tf_op jit(solution)/shard_map/reduce_scatter | solution.py:32
  967.9 7.4 all_gather.217
  1085.4 13.9 reduce-scatter.135.cloned.1.call-done
  1103.1 10.0 reduce-scatter.105.cloned.1.call-done
  1113.1 13.9 reduce-scatter.103.cloned.1.call-done
  1129.5 21.5 %reduce-scatter.91.cloned.1.call-done = bf16[256,256]{1,0:T(8,128)(2,1)} async-done(((bf16[256,1024]{1,0:T(8,128)(2,1)}), bf16[256,256]{1,0:T(8,128)(2,1)}) %reduce-scatter.91.cloned.1.call-update) | async-done | bytes 131088 | tf_op jit(solution)/shard_map/reduce_scatter | solution.py:32
  1153.0 22.3 %reduce-scatter.123.cloned.1.call-done = bf16[256,256]{1,0:T(8,128)(2,1)} async-done(((bf16[256,1024]{1,0:T(8,128)(2,1)}), bf16[256,256]{1,0:T(8,128)(2,1)}) %reduce-scatter.123.cloned.1.call-update) | async-done | bytes 131088 | tf_op jit(solution)/shard_map/reduce_scatter | solution.py:32
  1175.3 24.1 %reduce-scatter.139.cloned.1.call-done = bf16[256,256]{1,0:T(8,128)(2,1)} async-done(((bf16[256,1024]{1,0:T(8,128)(2,1)}), bf16[256,256]{1,0:T(8,128)(2,1)}) %reduce-scatter.139.cloned.1.call-update) | async-done | bytes 131088 | tf_op jit(solution)/shard_map/reduce_scatter | solution.py:32
  1199.5 24.2 %reduce-scatter.107.cloned.1.call-done = bf16[256,256]{1,0:T(8,128)(2,1)} async-done(((bf16[256,1024]{1,0:T(8,128)(2,1)}), bf16[256,256]{1,0:T(8,128)(2,1)}) %reduce-scatter.107.cloned.1.call-update) | async-done | bytes 131088 | tf_op jit(solution)/shard_map/reduce_scatter | solution.py:32
  1259.4 9.7 all_gather.214
  1296.8 22.5 %reduce-scatter.109.cloned.1.call-done = bf16[256,256]{1,0:T(8,128)(2,1)} async-done(((bf16[256,1024]{1,0:T(8,128)(2,1)}), bf16[256,256]{1,0:T(8,128)(2,1)}) %reduce-scatter.109.cloned.1.call-update) | async-done | bytes 131088 | tf_op jit(solution)/shard_map/reduce_scatter | solution.py:32
  1319.3 24.7 %reduce-scatter.125.cloned.1.call-done = bf16[256,256]{1,0:T(8,128)(2,1)} async-done(((bf16[256,1024]{1,0:T(8,128)(2,1)}), bf16[256,256]{1,0:T(8,128)(2,1)}) %reduce-scatter.125.cloned.1.call-update) | async-done | bytes 131088 | tf_op jit(solution)/shard_map/reduce_scatter | solution.py:32
  1370.9 7.4 all_gather.219
  1486.1 14.0 reduce-scatter.111.cloned.1.call-done
  1505.7 8.0 reduce-scatter.97.cloned.1.call-done
  1513.7 14.0 reduce-scatter.95.cloned.1.call-done
  1569.2 11.3 fusion.1
  1598.8 11.2 fusion.3
  1646.6 23.1 %all-to-all-done.3 = bf16[4,8,32,256]{3,2,0,1:T(8,128)(2,1)S(1)} async-done(((bf16[4,8,32,256]{3,2,0,1:T(8,128)(2,1)}), bf16[4,8,32,256]{3,2,0,1:T(8,128)(2,1)S(1)}, u32[]{:S(2)}, u32[]{:S(2)}) %all-to-all-start.3) | async-done | bytes 524320 | tf_op jit(solution)/shard_map/all_to_all | solution.py:499
  1669.7 8.2 all-to-all-start.1
  1678.2 49.1 %all-reduce = (f32[2,4,256]{2,1,0:T(4,128)}, f32[2,2,256]{2,1,0:T(2,128)}, f32[2,2,256]{2,1,0:T(2,128)}, f32[2,1024]{1,0:T(2,128)}) all-reduce(f32[2,4,256]{2,1,0:T(4,128)S(1)} %fusion.749, f32[2,2,256]{2,1,0:T(2,128)S(1)} %fusion.754, f32[2,2,256]{2,1,0:T(2,128)S(1)} %fusion.756, ...), channel_id=1, replica_groups=mesh['fsdp'=4,'ctx'=2,'tp'=4] {'fsdp','ctx'}, use_global_device_ids=true, to_apply=%region_312.315 | all-reduce | flops 6144 | bytes 49152 | tf_op jit(solution)/shard_map/psum | solution.py:373
  1734.9 12.2 gather_fusion.3
  1749.9 20.7 reduce-scatter.149.cloned.1.call-done
  1772.9 69.0 %reduce-scatter.151.cloned.1.call-done = f32[2,128,256]{2,1,0:T(8,128)} async-done(((f32[2,1024,256]{2,1,0:T(8,128)}), f32[2,128,256]{2,1,0:T(8,128)}) %reduce-scatter.151.cloned.1.call-update) | async-done | bytes 262160 | tf_op jit(solution)/shard_map/reduce_scatter | solution.py:369
  1841.9 150.3 %reduce-scatter.153.cloned.1.call-done = f32[2,128,1024]{2,1,0:T(8,128)} async-done(((f32[2,1024,1024]{2,1,0:T(8,128)}), f32[2,128,1024]{2,1,0:T(8,128)}) %reduce-scatter.153.cloned.1.call-update) | async-done | bytes 1048592 | tf_op jit(solution)/shard_map/reduce_scatter | solution.py:370
  1992.2 150.2 %reduce-scatter.155.cloned.1.call-done = f32[2,128,1024]{2,1,0:T(8,128)} async-done(((f32[2,1024,1024]{2,1,0:T(8,128)}), f32[2,128,1024]{2,1,0:T(8,128)}) %reduce-scatter.155.cloned.1.call-update) | async-done | bytes 1048592 | tf_op jit(solution)/shard_map/reduce_scatter | solution.py:371
  (2268 shorter events, 951.6 us)
Async XLA Ops:
  15.9 131.7 %all-gather.27.cloned.1.call-start = ((), (), s32[]{:S(2)}) async-start(), calls=%async_computation.108 | async-start | bytes 1769472 | tf_op jit(solution)/shard_map/all_gather | solution.py:432
  61.9 49.3 %all-to-all-start = ((bf16[4,8,32,256]{3,2,0,1:T(8,128)(2,1)}), bf16[4,8,32,256]{3,2,0,1:T(8,128)(2,1)S(1)}, u32[]{:S(2)}, u32[]{:S(2)}) async-start(bf16[4,8,32,256]{3,2,0,1:T(8,128)(2,1)} %copy.370), calls=%async_computation | async-start | bytes 1048576 | tf_op jit(solution)/shard_map/all_to_all | solution.py:418
  68.5 161.2 %reduce-scatter.53.cloned.1.call-start = ((), (), s32[]{:S(2)}) async-start(), calls=%async_computation.56 | async-start | bytes 655360 | tf_op jit(solution)/shard_map/reduce_scatter | solution.py:22
  169.2 63.9 %reduce-scatter.61.cloned.1.call-start = ((), (), s32[]{:S(2)}) async-start(), calls=%async_computation.60 | async-start | bytes 655360 | tf_op jit(solution)/shard_map/reduce_scatter | solution.py:22
  218.4 64.2 %reduce-scatter.77.cloned.1.call-start = ((), (), s32[]{:S(2)}) async-start(), calls=%async_computation.68 | async-start | bytes 655360 | tf_op jit(solution)/shard_map/reduce_scatter | solution.py:22
  226.0 72.9 %all-gather.29.cloned.1.call-start = ((), (), s32[]{:S(2)}) async-start(), calls=%async_computation.109 | async-start | bytes 2359296 | tf_op jit(solution)/shard_map/all_gather | solution.py:434
  226.9 100.6 %all-gather.31.cloned.1.call-start = ((), (), s32[]{:S(2)}) async-start(), calls=%async_computation.110 | async-start | bytes 2359296 | tf_op jit(solution)/shard_map/all_gather | solution.py:435
  227.8 132.5 %reduce-scatter.55.cloned.1.call-start = ((), (), s32[]{:S(2)}) async-start(), calls=%async_computation.57 | async-start | bytes 655360 | tf_op jit(solution)/shard_map/reduce_scatter | solution.py:22
  352.8 67.2 %reduce-scatter.79.cloned.1.call-start = ((), (), s32[]{:S(2)}) async-start(), calls=%async_computation.69 | async-start | bytes 655360 | tf_op jit(solution)/shard_map/reduce_scatter | solution.py:22
  360.2 63.3 %reduce-scatter.71.cloned.1.call-start = ((), (), s32[]{:S(2)}) async-start(), calls=%async_computation.65 | async-start | bytes 655360 | tf_op jit(solution)/shard_map/reduce_scatter | solution.py:22
  389.4 51.2 %all-gather.33.cloned.1.call-start = ((), (), s32[]{:S(2)}) async-start(), calls=%async_computation.111 | async-start | bytes 1769472 | tf_op jit(solution)/shard_map/all_gather | solution.py:432
  390.3 136.5 %reduce-scatter.57.cloned.1.call-start = ((), (), s32[]{:S(2)}) async-start(), calls=%async_computation.58 | async-start | bytes 655360 | tf_op jit(solution)/shard_map/reduce_scatter | solution.py:22
  478.4 60.6 %reduce-scatter.65.cloned.1.call-start = ((), (), s32[]{:S(2)}) async-start(), calls=%async_computation.62 | async-start | bytes 655360 | tf_op jit(solution)/shard_map/reduce_scatter | solution.py:22
  525.5 88.9 %reduce-scatter.81.cloned.1.call-start = ((), (), s32[]{:S(2)}) async-start(), calls=%async_computation.70 | async-start | bytes 655360 | tf_op jit(solution)/shard_map/reduce_scatter | solution.py:22
  592.2 53.2 %all-gather.35.cloned.1.call-start = ((), (), s32[]{:S(2)}) async-start(), calls=%async_computation.112 | async-start | bytes 2359296 | tf_op jit(solution)/shard_map/all_gather | solution.py:434
  593.0 102.5 %all-gather.37.cloned.1.call-start = ((), (), s32[]{:S(2)}) async-start(), calls=%async_computation.113 | async-start | bytes 2359296 | tf_op jit(solution)/shard_map/all_gather | solution.py:435
  593.7 138.7 %reduce-scatter.59.cloned.1.call-start = ((), (), s32[]{:S(2)}) async-start(), calls=%async_computation.59 | async-start | bytes 655360 | tf_op jit(solution)/shard_map/reduce_scatter | solution.py:22
  731.2 75.3 %reduce-scatter.83.cloned.1.call-start = ((), (), s32[]{:S(2)}) async-start(), calls=%async_computation.71 | async-start | bytes 655360 | tf_op jit(solution)/shard_map/reduce_scatter | solution.py:22
  784.3 108.7 %reduce-scatter.85.cloned.1.call-start = ((), (), s32[]{:S(2)}) async-start(), calls=%async_computation.72 | async-start | bytes 655360 | tf_op jit(solution)/shard_map/reduce_scatter | solution.py:32
  844.8 50.2 %reduce-scatter.117.cloned.1.call-start = ((), (), s32[]{:S(2)}) async-start(), calls=%async_computation.88 | async-start | bytes 655360 | tf_op jit(solution)/shard_map/reduce_scatter | solution.py:32
  864.8 50.6 %reduce-scatter.133.cloned.1.call-start = ((), (), s32[]{:S(2)}) async-start(), calls=%async_computation.96 | async-start | bytes 655360 | tf_op jit(solution)/shard_map/reduce_scatter | solution.py:32
  878.8 61.0 %reduce-scatter.101.cloned.1.call-start = ((), (), s32[]{:S(2)}) async-start(), calls=%async_computation.80 | async-start | bytes 655360 | tf_op jit(solution)/shard_map/reduce_scatter | solution.py:32
  892.9 178.1 %reduce-scatter.89.cloned.1.call-start = ((), (), s32[]{:S(2)}) async-start(), calls=%async_computation.74 | async-start | bytes 393216 | tf_op jit(solution)/shard_map/reduce_scatter | solution.py:339
  1005.1 65.9 %reduce-scatter.87.cloned.1.call-start = ((), (), s32[]{:S(2)}) async-start(), calls=%async_computation.73 | async-start | bytes 393216 | tf_op jit(solution)/shard_map/reduce_scatter | solution.py:336
  1059.4 53.6 %reduce-scatter.105.cloned.1.call-start = ((), (), s32[]{:S(2)}) async-start(), calls=%async_computation.82 | async-start | bytes 393216 | tf_op jit(solution)/shard_map/reduce_scatter | solution.py:339
  1063.0 64.0 %reduce-scatter.103.cloned.1.call-start = ((), (), s32[]{:S(2)}) async-start(), calls=%async_computation.81 | async-start | bytes 393216 | tf_op jit(solution)/shard_map/reduce_scatter | solution.py:336
  1069.4 81.7 %reduce-scatter.91.cloned.1.call-start = ((), (), s32[]{:S(2)}) async-start(), calls=%async_computation.75 | async-start | bytes 655360 | tf_op jit(solution)/shard_map/reduce_scatter | solution.py:32
  1074.1 101.2 %reduce-scatter.123.cloned.1.call-start = ((), (), s32[]{:S(2)}) async-start(), calls=%async_computation.91 | async-start | bytes 655360 | tf_op jit(solution)/shard_map/reduce_scatter | solution.py:32
  1080.8 118.6 %reduce-scatter.139.cloned.1.call-start = ((), (), s32[]{:S(2)}) async-start(), calls=%async_computation.99 | async-start | bytes 655360 | tf_op jit(solution)/shard_map/reduce_scatter | solution.py:32
  1101.8 121.9 %reduce-scatter.107.cloned.1.call-start = ((), (), s32[]{:S(2)}) async-start(), calls=%async_computation.83 | async-start | bytes 655360 | tf_op jit(solution)/shard_map/reduce_scatter | solution.py:32
  1129.5 158.6 %reduce-scatter.93.cloned.1.call-start = ((), (), s32[]{:S(2)}) async-start(), calls=%async_computation.76 | async-start | bytes 655360 | tf_op jit(solution)/shard_map/reduce_scatter | solution.py:32
  1245.7 49.0 %reduce-scatter.141.cloned.1.call-start = ((), (), s32[]{:S(2)}) async-start(), calls=%async_computation.100 | async-start | bytes 655360 | tf_op jit(solution)/shard_map/reduce_scatter | solution.py:32
  1259.3 60.0 %reduce-scatter.109.cloned.1.call-start = ((), (), s32[]{:S(2)}) async-start(), calls=%async_computation.84 | async-start | bytes 655360 | tf_op jit(solution)/shard_map/reduce_scatter | solution.py:32
  1274.7 69.3 %reduce-scatter.125.cloned.1.call-start = ((), (), s32[]{:S(2)}) async-start(), calls=%async_computation.92 | async-start | bytes 655360 | tf_op jit(solution)/shard_map/reduce_scatter | solution.py:32
  1287.8 173.0 %reduce-scatter.145.cloned.1.call-start = ((), (), s32[]{:S(2)}) async-start(), calls=%async_computation.102 | async-start | bytes 393216 | tf_op jit(solution)/shard_map/reduce_scatter | solution.py:339
  1410.2 50.6 %reduce-scatter.143.cloned.1.call-start = ((), (), s32[]{:S(2)}) async-start(), calls=%async_computation.101 | async-start | bytes 393216 | tf_op jit(solution)/shard_map/reduce_scatter | solution.py:336
  1439.2 60.8 %reduce-scatter.111.cloned.1.call-start = ((), (), s32[]{:S(2)}) async-start(), calls=%async_computation.85 | async-start | bytes 393216 | tf_op jit(solution)/shard_map/reduce_scatter | solution.py:336
  1442.0 71.8 %reduce-scatter.97.cloned.1.call-start = ((), (), s32[]{:S(2)}) async-start(), calls=%async_computation.78 | async-start | bytes 393216 | tf_op jit(solution)/shard_map/reduce_scatter | solution.py:339
  1446.9 80.8 %reduce-scatter.95.cloned.1.call-start = ((), (), s32[]{:S(2)}) async-start(), calls=%async_computation.77 | async-start | bytes 393216 | tf_op jit(solution)/shard_map/reduce_scatter | solution.py:336
  1449.1 179.7 %reduce-scatter.147.cloned.1.call-start = ((), (), s32[]{:S(2)}) async-start(), calls=%async_computation.103 | async-start | bytes 655360 | tf_op jit(solution)/shard_map/reduce_scatter | solution.py:32
  1463.9 165.9 %reduce-scatter.131.cloned.1.call-start = ((), (), s32[]{:S(2)}) async-start(), calls=%async_computation.95 | async-start | bytes 655360 | tf_op jit(solution)/shard_map/reduce_scatter | solution.py:32
  1474.9 155.8 %reduce-scatter.115.cloned.1.call-start = ((), (), s32[]{:S(2)}) async-start(), calls=%async_computation.87 | async-start | bytes 655360 | tf_op jit(solution)/shard_map/reduce_scatter | solution.py:32
  1502.4 129.3 %reduce-scatter.99.cloned.1.call-start = ((), (), s32[]{:S(2)}) async-start(), calls=%async_computation.79 | async-start | bytes 655360 | tf_op jit(solution)/shard_map/reduce_scatter | solution.py:32
  1532.4 238.2 %reduce-scatter.149.cloned.1.call-start = ((), (), s32[]{:S(2)}) async-start(), calls=%async_computation.104 | async-start | bytes 7077888 | tf_op jit(solution)/shard_map/reduce_scatter | solution.py:368
  1543.7 298.2 %reduce-scatter.151.cloned.1.call-start = ((), (), s32[]{:S(2)}) async-start(), calls=%async_computation.105 | async-start | bytes 2359296 | tf_op jit(solution)/shard_map/reduce_scatter | solution.py:369
  1550.6 441.6 %reduce-scatter.153.cloned.1.call-start = ((), (), s32[]{:S(2)}) async-start(), calls=%async_computation.106 | async-start | bytes 9437184 | tf_op jit(solution)/shard_map/reduce_scatter | solution.py:370
  1580.5 561.9 %reduce-scatter.155.cloned.1.call-start = ((), (), s32[]{:S(2)}) async-start(), calls=%async_computation.107 | async-start | bytes 9437184 | tf_op jit(solution)/shard_map/reduce_scatter | solution.py:371
  1669.7 65.1 %all-to-all-start.1 = ((bf16[4,8,32,256]{3,2,0,1:T(8,128)(2,1)}), bf16[4,8,32,256]{3,2,0,1:T(8,128)(2,1)S(1)}, u32[]{:S(2)}, u32[]{:S(2)}) async-start(bf16[4,8,32,256]{3,2,0,1:T(8,128)(2,1)} %copy.406), calls=%async_computation.17 | async-start | bytes 1048576 | tf_op jit(solution)/shard_map/all_to_all | solution.py:492
  (738 other events, 11458.3 us)
Sparse Core Ops, SparseCore 0:
  12.4 2.6 sort.62.cloned.1.call-done
  18.9 2.3 sort.60.cloned.1.call-done
  25.0 2.5 sort.64.cloned.1.call-done
  169.3 20.9 reduce-scatter.52
  211.8 21.2 reduce-scatter.60
  236.0 21.6 reduce-scatter.68
  261.0 21.6 reduce-scatter.76
  330.7 20.1 reduce-scatter.54
  353.6 21.6 reduce-scatter.62
  377.6 21.6 reduce-scatter.78
  401.9 21.6 reduce-scatter.70
  478.5 21.9 reduce-scatter.56
  517.0 21.8 reduce-scatter.64
  541.3 21.6 reduce-scatter.72
  592.4 22.0 reduce-scatter.80
  698.9 20.1 reduce-scatter.58
  722.9 20.3 reduce-scatter.66
  745.6 21.6 reduce-scatter.74
  784.4 22.0 reduce-scatter.82
  844.9 21.9 reduce-scatter.84
  869.6 21.6 reduce-scatter.116
  893.8 21.6 reduce-scatter.132
  918.1 21.6 reduce-scatter.100
  1245.8 23.7 reduce-scatter.92
  1272.7 21.9 reduce-scatter.140
  1297.6 21.6 reduce-scatter.108
  1322.4 21.6 reduce-scatter.124
  1451.5 2.6 sort.66.cloned.1.call-done
  (4 shorter events, 0.1 us)
Sparse Core Ops, SparseCore 1:
  19.0 50.8 all-gather.26
  228.6 48.9 all-gather.28
  279.6 47.8 all-gather.30
  392.3 45.7 all-gather.32
  595.7 49.7 all-gather.34
  647.6 47.8 all-gather.36
  1005.2 11.8 reduce-scatter.88
  1032.2 11.8 reduce-scatter.86
  1046.2 11.6 reduce-scatter.120
  1060.1 11.5 reduce-scatter.118
  1073.8 11.6 reduce-scatter.136
  1087.8 11.5 reduce-scatter.134
  1101.5 11.6 reduce-scatter.104
  1115.4 11.5 reduce-scatter.102
  1129.5 21.5 reduce-scatter.90
  1153.8 21.5 reduce-scatter.122
  1177.9 21.6 reduce-scatter.138
  1202.1 21.5 reduce-scatter.106
  1410.3 11.8 reduce-scatter.144
  1431.9 11.8 reduce-scatter.142
  1446.5 11.5 reduce-scatter.128
  1460.8 11.6 reduce-scatter.126
  1474.5 11.5 reduce-scatter.112
  1488.4 11.6 reduce-scatter.110
  1502.1 11.5 reduce-scatter.96
  1516.1 11.6 reduce-scatter.94
  1530.8 21.6 reduce-scatter.146
  1555.5 21.5 reduce-scatter.130
  1579.4 21.6 reduce-scatter.114
  1603.7 21.5 reduce-scatter.98
  1629.2 141.4 reduce-scatter.148
  1775.0 66.9 reduce-scatter.150
  1846.6 145.6 reduce-scatter.152
  1996.3 146.1 reduce-scatter.154
where the time goes:
time: 2170 us; the launch traced here: 2150 us
  waiting for transfers between devices  970 us (45%)
  blocking collectives  500 us (23%)
  matrix products  335 us (15%)
  other arithmetic  156 us (7%)
  local copies, waits for them, and re-layouts  132 us (6%)
  starting transfers between devices  31 us (1%)
  between operations  26.9 us (1%)
    reduce_scatter x16, waiting for transfers between devices, gradient_total(): lax.psum_scatter(values.astype(jnp.bfloat16), 'tp', scatter_dimension=1,...  191 us
    reduce_scatter x16, waiting for transfers between devices, partial_total(): lax.psum_scatter(values.astype(jnp.bfloat16), 'tp', scatter_dimension=1,...  185 us
    reduce_scatter x1, waiting for transfers between devices, reduce_grads(): lax.psum_scatter(matrices[2], ('fsdp', 'ctx'), scatter_dimension=1, tiled...  150 us
    reduce_scatter x1, waiting for transfers between devices, reduce_grads(): lax.psum_scatter(matrices[3], ('fsdp', 'ctx'), scatter_dimension=1, tiled...  150 us
    all_gather x16, blocking collectives, gradient_full(): return lax.all_gather(values, 'tp', axis=1, tiled=True)  120 us
    all_gather x16, blocking collectives, features_full(): return lax.all_gather(values, 'tp', axis=1, tiled=True)  118 us
    reduce_scatter x1, waiting for transfers between devices, reduce_grads(): lax.psum_scatter(matrices[1], ('fsdp', 'ctx'), scatter_dimension=1, tiled...  69 us
    all_gather x2, waiting for transfers between devices, local(): lax.all_gather(w_down[layer_index], ('fsdp', 'ctx'), axis=0, tiled=True)  67 us
  transfers between devices with their start and end apart: 62, of which 38 were waited for; matrix products, arithmetic and copies ran while one was open for 21% of the time, Pallas kernels for 0%

commit v1 on v0

v1 whole, which is shorter than its diff:
```python
import functools
import math

import jax
import jax.numpy as jnp
from jax import lax
from jax.experimental import pallas as pl
from jax.experimental.pallas import tpu as pltpu
from jax.sharding import PartitionSpec as P

HD = 64
NEG = -1e30
EPS = 1e-05
BF = jnp.bfloat16
F32 = jnp.float32
GRP = ("fsdp", "ctx")


def dot(left, right, dims):
    return lax.dot_general(left, right, (dims, ((), ())), preferred_element_type=F32)


NN = ((1,), (0,))
NT = ((1,), (1,))
TN = ((0,), (0,))


def head_probs(query, key_rows, same_seq):
    scores = jnp.where(same_seq, dot(query, key_rows, NT) * (1.0 / math.sqrt(HD)), NEG)
    top = jnp.max(scores, axis=1, keepdims=True)
    weighted = jnp.exp(scores - top)
    return weighted * (1.0 / jnp.sum(weighted, axis=1, keepdims=True))


def attend_kernel(qkv_ref, seg_col, seg_row, out_ref):
    same_seq = seg_col[0] == seg_row[0]
    for head in range(qkv_ref.shape[3] // HD):
        cols = slice(head * HD, (head + 1) * HD)
        probs = head_probs(qkv_ref[0, 0, :, cols], qkv_ref[1, 0, :, cols], same_seq)
        out_ref[0, :, cols] = dot(probs.astype(BF), qkv_ref[2, 0, :, cols], NN).astype(BF)


def attend_back_kernel(qkv_ref, grad_ref, seg_col, seg_row, out_ref):
    same_seq = seg_col[0] == seg_row[0]
    scale = 1.0 / math.sqrt(HD)
    for head in range(qkv_ref.shape[3] // HD):
        cols = slice(head * HD, (head + 1) * HD)
        query, key_rows, value_rows = (qkv_ref[c, 0, :, cols] for c in range(3))
        grad = grad_ref[0, :, cols]
        probs = head_probs(query, key_rows, same_seq)
        grad_probs = dot(grad, value_rows, NT)
        delta = jnp.sum(probs * grad_probs, axis=1, keepdims=True)
        grad_scores = (probs * (grad_probs - delta)).astype(BF)
        out_ref[0, 0, :, cols] = (dot(grad_scores, key_rows, NN) * scale).astype(BF)
        out_ref[1, 0, :, cols] = (dot(grad_scores, query, TN) * scale).astype(BF)
        out_ref[2, 0, :, cols] = dot(probs.astype(BF), grad, TN).astype(BF)


def attend(qkv, seg_col, seg_row):
    _, packs, rows, width = qkv.shape
    return pl.pallas_call(
        attend_kernel,
        grid=(packs,),
        in_specs=[
            pl.BlockSpec((3, 1, rows, width), lambda k: (0, k, 0, 0)),
            pl.BlockSpec((1, rows, 1), lambda k: (k, 0, 0)),
            pl.BlockSpec((1, 1, rows), lambda k: (k, 0, 0)),
        ],
        out_specs=pl.BlockSpec((1, rows, width), lambda k: (k, 0, 0)),
        out_shape=jax.ShapeDtypeStruct((packs, rows, width), BF),
        compiler_params=pltpu.CompilerParams(vmem_limit_bytes=32 << 20),
    )(qkv, seg_col, seg_row)


def attend_back(qkv, grad, seg_col, seg_row):
    _, packs, rows, width = qkv.shape
    return pl.pallas_call(
        attend_back_kernel,
        grid=(packs,),
        in_specs=[
            pl.BlockSpec((3, 1, rows, width), lambda k: (0, k, 0, 0)),
            pl.BlockSpec((1, rows, width), lambda k: (k, 0, 0)),
            pl.BlockSpec((1, rows, 1), lambda k: (k, 0, 0)),
            pl.BlockSpec((1, 1, rows), lambda k: (k, 0, 0)),
        ],
        out_specs=pl.BlockSpec((3, 1, rows, width), lambda k: (0, k, 0, 0)),
        out_shape=jax.ShapeDtypeStruct((3, packs, rows, width), BF),
        compiler_params=pltpu.CompilerParams(vmem_limit_bytes=32 << 20),
    )(qkv, grad, seg_col, seg_row)


def gather_rows(values):
    return lax.all_gather(values.astype(BF), "tp", axis=1, tiled=True)


def scatter_rows(values):
    return lax.psum_scatter(
        values.astype(BF), "tp", scatter_dimension=1, tiled=True
    ).astype(F32)


def norm_forward(residual, gain, offset):
    mean = jnp.mean(residual, axis=-1, keepdims=True)
    centred = residual - mean
    scale = lax.rsqrt(jnp.mean(centred * centred, axis=-1, keepdims=True) + EPS)
    normed = centred * scale
    return normed * gain + offset, normed, scale


def norm_backward(upstream, normed, scale, gain):
    scaled = upstream * gain
    first = jnp.mean(scaled, axis=-1, keepdims=True)
    second = jnp.mean(scaled * normed, axis=-1, keepdims=True)
    grad = scale * (scaled - first - normed * second)
    return grad, jnp.sum(upstream * normed, axis=(0, 1)), jnp.sum(upstream, axis=(0, 1))


def gelu(values):
    return jax.nn.gelu(values, approximate=False)


def mm(spec, left, right):
    return jnp.einsum(spec, left, right, preferred_element_type=F32)


def layer_forward(resid, act, weights, vectors, seg_col, seg_row):
    w_qkv, w_out, w_up, w_down = weights
    head_bias, full_bias, gain, offset, up_bias = vectors
    proj = mm("ktd,cdh->ckth", act, w_qkv)
    zero = jnp.zeros_like(head_bias[0])
    qkv = (proj + jnp.stack([head_bias[0], zero, head_bias[1]])[:, None, None, :]).astype(BF)
    attended = attend(qkv, seg_col, seg_row)
    mixed = scatter_rows(mm("kth,dh->ktd", attended, w_out))
    hidden, normed1, scale1 = norm_forward(resid + mixed + full_bias[0], gain[0], offset[0])
    hidden_full = gather_rows(hidden)
    upper = mm("ktd,df->ktf", hidden_full, w_up) + up_bias
    gelu_low = gelu(upper).astype(BF)
    lowered = scatter_rows(mm("ktf,df->ktd", gelu_low, w_down))
    out, normed2, scale2 = norm_forward(hidden + lowered + full_bias[1], gain[1], offset[1])
    return out, (act, qkv, attended, normed1, scale1, hidden_full, upper, gelu_low, normed2, scale2)


def layer_backward(upstream, saved, weights, vectors, seg_col, seg_row):
    w_qkv, w_out, w_up, w_down = weights
    head_bias, full_bias, gain, offset, up_bias = vectors
    act, qkv, attended, normed1, scale1, hidden_full, upper, gelu_low, normed2, scale2 = saved
    grad2, gain2, offset2 = norm_backward(upstream, normed2, scale2, gain[1])
    grad_lowered = gather_rows(grad2)
    g_down = mm("ktd,ktf->df", grad_lowered, gelu_low).astype(BF)
    grad_gelu = mm("ktd,df->ktf", grad_lowered, w_down).astype(BF)
    _, pull = jax.vjp(gelu, upper)
    grad_upper = pull(grad_gelu.astype(F32))[0].astype(BF)
    up_grad = jnp.sum(grad_upper, axis=(0, 1), dtype=F32)
    g_up = mm("ktd,ktf->df", hidden_full, grad_upper).astype(BF)
    grad_hidden = scatter_rows(mm("ktf,df->ktd", grad_upper, w_up)) + grad2
    grad1, gain1, offset1 = norm_backward(grad_hidden, normed1, scale1, gain[0])
    grad_mixed = gather_rows(grad1)
    g_out = mm("ktd,kth->dh", grad_mixed, attended).astype(BF)
    grad_attended = mm("ktd,dh->kth", grad_mixed, w_out).astype(BF)
    grad_qkv = attend_back(qkv, grad_attended, seg_col, seg_row)
    g_qkv = mm("ktd,ckth->cdh", act, grad_qkv).astype(BF)
    grad_act = scatter_rows(mm("ckth,cdh->ktd", grad_qkv, w_qkv))
    full_part = jnp.stack(
        [jnp.sum(grad1, axis=(0, 1)), jnp.sum(grad2, axis=(0, 1)), gain1, gain2, offset1, offset2]
    )
    head_part = jnp.sum(grad_qkv, axis=(1, 2), dtype=F32)[0::2]
    return grad_act + grad1, (g_qkv, g_out, g_up, g_down), (full_part, head_part, up_grad)


def local(
    tokens, time_embed, cotangent, segment_ids, to_owner, from_owner,
    w_qkv, w_out, w_up, w_down, biases, norm_gain, norm_bias, up_bias,
):
    micro, rows, width = tokens.shape
    layers = w_qkv.shape[0]
    fs, cx, tp = (lax.axis_size(a) for a in ("fsdp", "ctx", "tp"))
    groups = fs * cx
    mine = micro // cx
    pack = segment_ids.shape[1]
    sends = rows // fs
    my_first = lax.axis_index("ctx") * mine
    tp_index = lax.axis_index("tp")

    weights = []
    for layer in range(layers):
        weights.append(
            (
                lax.all_gather(w_qkv[layer], GRP, axis=1, tiled=True),
                lax.all_gather(w_out[layer], GRP, axis=0, tiled=True),
                lax.all_gather(w_up[layer], GRP, axis=0, tiled=True),
                lax.all_gather(w_down[layer], GRP, axis=0, tiled=True),
            )
        )
    vec = jnp.concatenate([biases[:, 2:], norm_gain, norm_bias], axis=1)
    vec = lax.all_gather(vec, "tp", axis=2, tiled=True)
    vectors = [
        (biases[layer, :2], vec[layer, 0:2], vec[layer, 2:4], vec[layer, 4:6], up_bias[layer])
        for layer in range(layers)
    ]

    to_pack = to_owner // pack
    earlier = jnp.arange(rows)[None, :] < jnp.arange(rows)[:, None]
    rank = jnp.sum((to_pack[:, :, None] == to_pack[:, None, :]) & earlier[None], axis=2)
    out_slot = to_pack * sends + rank
    pick_out = (jnp.arange(rows)[None, :, None] == out_slot[:, None, :]).astype(BF)
    given = lax.all_gather(from_owner, "ctx", axis=1, tiled=True)
    given = lax.dynamic_slice_in_dim(given, my_first, mine)
    source = given // rows
    before = (given[:, None, :] < given[:, :, None]) & (
        given[:, None, :] >= (source * rows)[:, :, None]
    )
    in_slot = source * sends + jnp.sum(before, axis=2)
    pick_in = (jnp.arange(pack)[None, None, :] == in_slot[:, :, None]).astype(BF)

    def to_packs(values):
        slots = mm("msg,mgw->msw", pick_out, values).astype(BF)
        slots = slots.reshape(cx, mine, fs, sends, width).transpose(2, 0, 1, 3, 4)
        slots = slots.reshape(groups, mine, sends, width)
        slots = lax.all_to_all(slots, GRP, split_axis=0, concat_axis=0, tiled=True)
        slots = slots.transpose(1, 0, 2, 3).reshape(mine, pack, width)
        return mm("kps,ksw->kpw", pick_in, slots).astype(BF)

    def from_packs(values):
        values = lax.all_to_all(values.astype(BF), "tp", split_axis=2, concat_axis=1, tiled=True)
        slots = mm("kps,kpw->ksw", pick_in, values).astype(BF)
        slots = slots.reshape(mine, groups, sends, width).transpose(1, 0, 2, 3)
        slots = lax.all_to_all(slots, GRP, split_axis=0, concat_axis=0, tiled=True)
        slots = slots.reshape(fs, cx, mine, sends, width).transpose(1, 2, 0, 3, 4)
        return mm("msg,msw->mgw", pick_out, slots.reshape(micro, rows, width))

    embedded = (tokens.astype(F32) + time_embed.astype(F32)).astype(BF)
    act = lax.all_gather(to_packs(embedded), "tp", axis=2, tiled=True)
    resid = lax.dynamic_slice_in_dim(act, tp_index * (pack // tp), pack // tp, 1).astype(F32)
    upstream = lax.all_to_all(
        to_packs(cotangent), "tp", split_axis=1, concat_axis=2, tiled=True
    ).astype(F32)
    seg = lax.dynamic_slice_in_dim(segment_ids, my_first, mine)
    seg_col, seg_row = seg[:, :, None], seg[:, None, :]

    saved = []
    for layer in range(layers):
        if layer:
            act = gather_rows(resid)
        resid, kept = layer_forward(resid, act, weights[layer], vectors[layer], seg_col, seg_row)
        saved.append(kept)
    outputs = from_packs(resid)
    shards = [None] * layers
    parts = [None] * layers
    for layer in reversed(range(layers)):
        upstream, grads, parts[layer] = layer_backward(
            upstream, saved[layer], weights[layer], vectors[layer], seg_col, seg_row
        )
        shards[layer] = (
            lax.psum_scatter(grads[0], GRP, scatter_dimension=1, tiled=True),
            lax.psum_scatter(grads[1], GRP, scatter_dimension=0, tiled=True),
            lax.psum_scatter(grads[2], GRP, scatter_dimension=0, tiled=True),
            lax.psum_scatter(grads[3], GRP, scatter_dimension=0, tiled=True),
        )
    input_grad = from_packs(upstream)
    full_part, head_part, up_part = (jnp.stack([p[i] for p in parts]) for i in range(3))
    full_part = lax.psum_scatter(full_part, "tp", scatter_dimension=2, tiled=True)
    full_part, head_part, up_part = lax.psum((full_part, head_part, up_part), GRP)
    return (
        outputs,
        input_grad,
        *(jnp.stack([s[i] for s in shards]).astype(F32) for i in range(4)),
        jnp.concatenate([head_part, full_part[:, 0:2]], axis=1),
        full_part[:, 2:4],
        full_part[:, 4:6],
        up_part,
    )


def solution(mesh):
    wide = P(None, GRP, "tp")
    vec = P(None, None, "tp")
    qkv = P(None, None, GRP, "tp")
    owner = P(None, GRP)
    return jax.shard_map(
        local,
        mesh=mesh,
        in_specs=(
            wide, wide, wide, P(None, "fsdp"), owner, owner, qkv, wide, wide, wide,
            vec, vec, vec, P(None, "tp"),
        ),
        out_specs=(wide, wide, qkv, wide, wide, wide, vec, vec, vec, P(None, "tp")),
        check_vma=False,
    )
```

time: 2170 us -> 1500 us (0.69)
  blocking collectives: 500 us -> 166 us
  matrix products: 335 us -> 121 us
  other arithmetic: 156 us -> 69.5 us
  local copies, waits for them, and re-layouts: 132 us -> 52.4 us
  Pallas kernels: 0 us -> 37.1 us
  waiting for transfers between devices: 970 us -> 1000 us
    all_gather x50 -> x4, blocking collectives: 399 us -> 75.7 us  [the longest x2 64 us: local(): lax.all_gather(w_out[layer], GRP, axis=0, tiled=True)]
    reduce_scatter x52 -> x15, waiting for transfers between devices: 850 us -> 562 us  [the longest x8 180 us: scatter_rows(): lax.psum_scatter(values.astype(BF), 'tp', scatter_dimension=1, tiled=True)]
    all_gather x6 -> x14, waiting for transfers between devices: 76.5 us -> 349 us  [the longest x7 159 us: gather_rows(): return lax.all_gather(values.astype(BF), 'tp', axis=1, tiled=True)]
    dot_general x288 -> x32, matrix products: 335 us -> 121 us  [mm(): return jnp.einsum(spec, left, right, preferred_element_type=F32)]
    psum x9 -> x1, blocking collectives: 101 us -> 35 us  [local(): lax.psum((full_part, head_part, up_part), GRP)]
    unnamed x58 -> x33, waiting for transfers between devices: 2.31 us -> 67.9 us
    all_to_all x0 -> x3, blocking collectives: none -> 55.1 us  [the longest x1 25.1 us: from_packs(): slots = lax.all_to_all(slots, GRP, split_axis=0, concat_axis=0, tiled=True)]
    gather x8 -> x0, local copies, waits for them, and re-layouts: 54.3 us -> none  [the longest x4 31.1 us: placed(): return jnp.take_along_axis(flat_rows, row_rank[:, :, None], axis=1)]
  transfers between devices with their start and end apart: 62 -> 35, of which waited for: 38 -> 29; matrix products, arithmetic and copies ran while one was open for 21% -> 10% of each run, Pallas kernels for 0% -> 0%
where the time goes in v1:
time: 1500 us; the launch traced here: 1490 us
  waiting for transfers between devices  1000 us (67%)
  blocking collectives  166 us (11%)
  matrix products  121 us (8%)
  other arithmetic  69.5 us (5%)
  local copies, waits for them, and re-layouts  52.4 us (3%)
  Pallas kernels  37.1 us (2%)
  starting transfers between devices  22.2 us (1%)
  between operations  15.4 us (1%)
    reduce_scatter x8, waiting for transfers between devices, scatter_rows(): lax.psum_scatter(values.astype(BF), 'tp', scatter_dimension=1, tiled=True)  180 us
    all_gather x7, waiting for transfers between devices, gather_rows(): return lax.all_gather(values.astype(BF), 'tp', axis=1, tiled=True)  159 us
    reduce_scatter x2, waiting for transfers between devices, local(): lax.psum_scatter(grads[2], GRP, scatter_dimension=0, tiled=True)  137 us
    reduce_scatter x2, waiting for transfers between devices, local(): lax.psum_scatter(grads[3], GRP, scatter_dimension=0, tiled=True)  132 us
    dot_general x32, matrix products, mm(): return jnp.einsum(spec, left, right, preferred_element_type=F32)  121 us
    reduce_scatter x2, waiting for transfers between devices, local(): lax.psum_scatter(grads[1], GRP, scatter_dimension=0, tiled=True)  93.5 us
    all_gather x2, waiting for transfers between devices, local(): lax.all_gather(w_up[layer], GRP, axis=0, tiled=True)  92.6 us
    unnamed x33, waiting for transfers between devices  67.9 us
  transfers between devices with their start and end apart: 35, of which 29 were waited for; matrix products, arithmetic and copies ran while one was open for 10% of the time, Pallas kernels for 0%

profile of v1, /device:TPU:8, one launch (start us, length us, event | category | flops | bytes accessed | tf_op | source)
XLA Modules:
  0.0 1485.6 jit_solution(16839147924369639642)
XLA Ops:
  13.7 6.3 all-to-all-start
  19.9 6.3 all_gather.54
  26.9 12.5 all-to-all-done
  41.6 32.4 %all-gather.1 = bf16[1,1024,256]{2,1,0:T(8,128)(2,1)} all-gather(bf16[1,128,256]{2,1,0:T(8,128)(2,1)S(1)} %get-tuple-element.105), channel_id=3, replica_groups=mesh['fsdp'=4,'ctx'=2,'tp'=4] {'fsdp','ctx'}, dimensions={1}, use_global_device_ids=true | all-gather | bytes 589824 | tf_op jit(solution)/shard_map/all_gather | solution.py:189
  74.0 16.2 %all-gather.23.cloned.1.call-done = bf16[2,512,1024]{2,1,0:T(8,128)(2,1)} async-done(((bf16[2,512,256]{2,1,0:T(8,128)(2,1)}), bf16[2,512,1024]{2,1,0:T(8,128)(2,1)}) %all-gather.23.cloned.1.call-update) | async-done | bytes 2097168 | tf_op jit(solution)/shard_map/all_gather | solution.py:232
  94.1 9.0 shard_map.213
  112.7 25.1 %reduce-scatter.22.cloned.1.call-done = bf16[2,128,1024]{2,1,0:T(8,128)(2,1)} async-done(((bf16[2,512,1024]{2,1,0:T(8,128)(2,1)}), bf16[2,128,1024]{2,1,0:T(8,128)(2,1)}) %reduce-scatter.22.cloned.1.call-update) | async-done | bytes 524304 | tf_op jit(solution)/shard_map/reduce_scatter | solution.py:97
  144.7 45.2 %all-gather.41.cloned.1.call-done = bf16[1,1024,1024]{2,1,0:T(8,128)(2,1)} async-done(((bf16[1,128,1024]{2,1,0:T(8,128)(2,1)}), bf16[1,1024,1024]{2,1,0:T(8,128)(2,1)}) %all-gather.41.cloned.1.call-update) | async-done | bytes 2097168 | tf_op jit(solution)/shard_map/all_gather | solution.py:190
  190.0 23.2 %all-gather.25.cloned.1.call-done = bf16[2,512,1024]{2,1,0:T(8,128)(2,1)} async-done(((bf16[2,128,1024]{2,1,0:T(8,128)(2,1)}), bf16[2,512,1024]{2,1,0:T(8,128)(2,1)}) %all-gather.25.cloned.1.call-update) | async-done | bytes 2097168 | tf_op jit(solution)/shard_map/all_gather | solution.py:93
  220.8 11.0 multiply_convert_fusion.1
  231.8 33.4 %all-gather.43.cloned.1.call-done = bf16[1,1024,1024]{2,1,0:T(8,128)(2,1)} async-done(((bf16[1,128,1024]{2,1,0:T(8,128)(2,1)}), bf16[1,1024,1024]{2,1,0:T(8,128)(2,1)}) %all-gather.43.cloned.1.call-update) | async-done | bytes 2097168 | tf_op jit(solution)/shard_map/all_gather | solution.py:191
  265.2 6.0 fusion.57
  272.1 29.3 %reduce-scatter.24.cloned.1.call-done = bf16[2,128,1024]{2,1,0:T(8,128)(2,1)} async-done(((bf16[2,512,1024]{2,1,0:T(8,128)(2,1)}), bf16[2,128,1024]{2,1,0:T(8,128)(2,1)}) %reduce-scatter.24.cloned.1.call-update) | async-done | bytes 524304 | tf_op jit(solution)/shard_map/reduce_scatter | solution.py:97
  305.2 31.6 %all-gather.5 = bf16[1,1024,256]{2,1,0:T(8,128)(2,1)} all-gather(bf16[1,128,256]{2,1,0:T(8,128)(2,1)S(1)} %get-tuple-element.104), channel_id=7, replica_groups=mesh['fsdp'=4,'ctx'=2,'tp'=4] {'fsdp','ctx'}, dimensions={1}, use_global_device_ids=true | all-gather | bytes 589824 | tf_op jit(solution)/shard_map/all_gather | solution.py:189
  336.8 14.1 all-gather.45.cloned.1.call-done
  350.9 22.7 %all-gather.27.cloned.1.call-done = bf16[2,512,1024]{2,1,0:T(8,128)(2,1)} async-done(((bf16[2,128,1024]{2,1,0:T(8,128)(2,1)}), bf16[2,512,1024]{2,1,0:T(8,128)(2,1)}) %all-gather.27.cloned.1.call-update) | async-done | bytes 2097168 | tf_op jit(solution)/shard_map/all_gather | solution.py:93
  377.5 8.3 shard_map.214
  389.9 30.8 %reduce-scatter.26.cloned.1.call-done = bf16[2,128,1024]{2,1,0:T(8,128)(2,1)} async-done(((bf16[2,512,1024]{2,1,0:T(8,128)(2,1)}), bf16[2,128,1024]{2,1,0:T(8,128)(2,1)}) %reduce-scatter.26.cloned.1.call-update) | async-done | bytes 524304 | tf_op jit(solution)/shard_map/reduce_scatter | solution.py:97
  425.5 47.3 %all-gather.47.cloned.1.call-done = bf16[1,1024,1024]{2,1,0:T(8,128)(2,1)} async-done(((bf16[1,128,1024]{2,1,0:T(8,128)(2,1)}), bf16[1,1024,1024]{2,1,0:T(8,128)(2,1)}) %all-gather.47.cloned.1.call-update) | async-done | bytes 2097168 | tf_op jit(solution)/shard_map/all_gather | solution.py:190
  472.9 23.2 %all-gather.29.cloned.1.call-done = bf16[2,512,1024]{2,1,0:T(8,128)(2,1)} async-done(((bf16[2,128,1024]{2,1,0:T(8,128)(2,1)}), bf16[2,512,1024]{2,1,0:T(8,128)(2,1)}) %all-gather.29.cloned.1.call-update) | async-done | bytes 2097168 | tf_op jit(solution)/shard_map/all_gather | solution.py:93
  503.8 11.0 multiply_convert_fusion
  514.8 33.6 %all-gather.49.cloned.1.call-done = bf16[1,1024,1024]{2,1,0:T(8,128)(2,1)} async-done(((bf16[1,128,1024]{2,1,0:T(8,128)(2,1)}), bf16[1,1024,1024]{2,1,0:T(8,128)(2,1)}) %all-gather.49.cloned.1.call-update) | async-done | bytes 2097168 | tf_op jit(solution)/shard_map/all_gather | solution.py:191
  554.9 17.0 %all_to_all.65 = bf16[8,2,64,256]{3,2,1,0:T(8,128)(2,1)S(1)} all-to-all(bf16[8,2,64,256]{3,2,1,0:T(8,128)(2,1)S(1)} %bitcast.288), channel_id=1, replica_groups=mesh['fsdp'=4,'ctx'=2,'tp'=4] {'fsdp','ctx'}, dimensions={0} | all-to-all | bytes 1048576 | tf_op jit(solution)/shard_map/all_to_all | solution.py:219
  578.0 10.8 all-to-all-done.4
  601.4 22.7 %all-gather.31.cloned.1.call-done = bf16[2,512,1024]{2,1,0:T(8,128)(2,1)} async-done(((bf16[2,128,1024]{2,1,0:T(8,128)(2,1)}), bf16[2,512,1024]{2,1,0:T(8,128)(2,1)}) %all-gather.31.cloned.1.call-update) | async-done | bytes 2097168 | tf_op jit(solution)/shard_map/all_gather | solution.py:93
  624.1 8.4 convert_reduce_fusion
  637.7 31.5 %reduce-scatter.30.cloned.1.call-done = bf16[2,128,1024]{2,1,0:T(8,128)(2,1)} async-done(((bf16[2,512,1024]{2,1,0:T(8,128)(2,1)}), bf16[2,128,1024]{2,1,0:T(8,128)(2,1)}) %reduce-scatter.30.cloned.1.call-update) | async-done | bytes 524304 | tf_op jit(solution)/shard_map/reduce_scatter | solution.py:97
  675.0 22.5 %all-gather.33.cloned.1.call-done = bf16[2,512,1024]{2,1,0:T(8,128)(2,1)} async-done(((bf16[2,128,1024]{2,1,0:T(8,128)(2,1)}), bf16[2,512,1024]{2,1,0:T(8,128)(2,1)}) %all-gather.33.cloned.1.call-update) | async-done | bytes 2097168 | tf_op jit(solution)/shard_map/all_gather | solution.py:93
  700.1 9.9 shard_map.215
  714.4 31.5 %reduce-scatter.32.cloned.1.call-done = bf16[2,128,1024]{2,1,0:T(8,128)(2,1)} async-done(((bf16[2,512,1024]{2,1,0:T(8,128)(2,1)}), bf16[2,128,1024]{2,1,0:T(8,128)(2,1)}) %reduce-scatter.32.cloned.1.call-update) | async-done | bytes 524304 | tf_op jit(solution)/shard_map/reduce_scatter | solution.py:97
  751.6 22.7 %all-gather.35.cloned.1.call-done = bf16[2,512,1024]{2,1,0:T(8,128)(2,1)} async-done(((bf16[2,128,1024]{2,1,0:T(8,128)(2,1)}), bf16[2,512,1024]{2,1,0:T(8,128)(2,1)}) %all-gather.35.cloned.1.call-update) | async-done | bytes 2097168 | tf_op jit(solution)/shard_map/all_gather | solution.py:93
  774.3 8.4 convert_reduce_fusion.1
  787.8 31.5 %reduce-scatter.34.cloned.1.call-done = bf16[2,128,1024]{2,1,0:T(8,128)(2,1)} async-done(((bf16[2,512,1024]{2,1,0:T(8,128)(2,1)}), bf16[2,128,1024]{2,1,0:T(8,128)(2,1)}) %reduce-scatter.34.cloned.1.call-update) | async-done | bytes 524304 | tf_op jit(solution)/shard_map/reduce_scatter | solution.py:97
  826.1 22.3 %all-gather.37.cloned.1.call-done = bf16[2,512,1024]{2,1,0:T(8,128)(2,1)} async-done(((bf16[2,128,1024]{2,1,0:T(8,128)(2,1)}), bf16[2,512,1024]{2,1,0:T(8,128)(2,1)}) %all-gather.37.cloned.1.call-update) | async-done | bytes 2097168 | tf_op jit(solution)/shard_map/all_gather | solution.py:93
  850.8 9.9 shard_map.216
  877.2 6.0 bitcast_convert_fusion
  883.4 6.0 bitcast_convert_fusion.1
  911.0 13.0 all_to_all.66
  939.6 25.1 %all_to_all.67 = bf16[8,2,64,256]{3,2,1,0:T(8,128)(2,1)S(1)} all-to-all(bf16[8,2,64,256]{3,2,1,0:T(8,128)(2,1)S(1)} %bitcast.291), channel_id=1, replica_groups=mesh['fsdp'=4,'ctx'=2,'tp'=4] {'fsdp','ctx'}, dimensions={0} | all-to-all | bytes 1048576 | tf_op jit(solution)/shard_map/all_to_all | solution.py:227
  976.1 61.4 %reduce-scatter.48.cloned.1.call-done = bf16[128,1024]{1,0:T(8,128)(2,1)} async-done(((bf16[1024,1024]{1,0:T(8,128)(2,1)}), bf16[128,1024]{1,0:T(8,128)(2,1)}) %reduce-scatter.48.cloned.1.call-update) | async-done | bytes 262160 | tf_op jit(solution)/shard_map/reduce_scatter | solution.py:257
  1037.4 70.7 %reduce-scatter.46.cloned.1.call-done = bf16[128,1024]{1,0:T(8,128)(2,1)} async-done(((bf16[1024,1024]{1,0:T(8,128)(2,1)}), bf16[128,1024]{1,0:T(8,128)(2,1)}) %reduce-scatter.46.cloned.1.call-update) | async-done | bytes 262160 | tf_op jit(solution)/shard_map/reduce_scatter | solution.py:257
  1118.0 66.1 %reduce-scatter.44.cloned.1.call-done = bf16[128,1024]{1,0:T(8,128)(2,1)} async-done(((bf16[1024,1024]{1,0:T(8,128)(2,1)}), bf16[128,1024]{1,0:T(8,128)(2,1)}) %reduce-scatter.44.cloned.1.call-update) | async-done | bytes 262160 | tf_op jit(solution)/shard_map/reduce_scatter | solution.py:256
  1184.2 70.7 %reduce-scatter.42.cloned.1.call-done = bf16[128,1024]{1,0:T(8,128)(2,1)} async-done(((bf16[1024,1024]{1,0:T(8,128)(2,1)}), bf16[128,1024]{1,0:T(8,128)(2,1)}) %reduce-scatter.42.cloned.1.call-update) | async-done | bytes 262160 | tf_op jit(solution)/shard_map/reduce_scatter | solution.py:256
  1257.2 19.8 %reduce-scatter.50.cloned.1.call-done = f32[2,6,256]{2,1,0:T(8,128)} async-done(((f32[2,6,1024]{2,1,0:T(8,128)}), f32[2,6,256]{2,1,0:T(8,128)}) %reduce-scatter.50.cloned.1.call-update) | async-done | bytes 12304 | tf_op jit(solution)/shard_map/reduce_scatter | solution.py:261
  1277.0 35.0 %all-reduce = (f32[2,6,256]{2,1,0:T(8,128)S(1)}, f32[2,2,256]{2,1,0:T(2,128)S(1)}, f32[2,1024]{1,0:T(2,128)}) all-reduce(f32[2,6,256]{2,1,0:T(8,128)} %reduce-scatter.50.cloned.1.call-done, f32[2,2,256]{2,1,0:T(2,128)S(1)} %pad_maximum_fusion.6, ...), channel_id=1, replica_groups=mesh['fsdp'=4,'ctx'=2,'tp'=4] {'fsdp','ctx'}, use_global_device_ids=true, to_apply=%region_50.51 | all-reduce | flops 6144 | bytes 49152 | tf_op jit(solution)/shard_map/psum | solution.py:262
  1313.3 29.0 %reduce-scatter.40.cloned.1.call-done = bf16[128,256]{1,0:T(8,128)(2,1)} async-done(((bf16[1024,256]{1,0:T(8,128)(2,1)}), bf16[128,256]{1,0:T(8,128)(2,1)}) %reduce-scatter.40.cloned.1.call-update) | async-done | bytes 65552 | tf_op jit(solution)/shard_map/reduce_scatter | solution.py:255
  1342.3 64.5 %reduce-scatter.38.cloned.1.call-done = bf16[128,256]{1,0:T(8,128)(2,1)} async-done(((bf16[1024,256]{1,0:T(8,128)(2,1)}), bf16[128,256]{1,0:T(8,128)(2,1)}) %reduce-scatter.38.cloned.1.call-update) | async-done | bytes 65552 | tf_op jit(solution)/shard_map/reduce_scatter | solution.py:255
  1408.4 65.3 %reduce-scatter.52.cloned.1.call-done = bf16[128,768]{1,0:T(8,128)(2,1)} async-done(((bf16[1024,768]{1,0:T(8,128)(2,1)}), bf16[128,768]{1,0:T(8,128)(2,1)}) %reduce-scatter.52.cloned.1.call-update) | async-done | bytes 196624
  (268 shorter events, 209.9 us)
Async XLA Ops:
  7.2 547.1 %copy-start = (bf16[4,256,256]{2,1,0:T(8,128)(2,1)S(1)}, bf16[4,256,256]{2,1,0:T(8,128)(2,1)}, u32[]{:S(2)}) copy-start(bf16[4,256,256]{2,1,0:T(8,128)(2,1)} %param.16) | copy-start | bytes 1572868
  7.2 33.9 %copy-start.22 = (s32[4,512]{1,0:T(4,128)S(1)}, s32[4,512]{1,0:T(4,128)}, u32[]{:S(2)}) copy-start(s32[4,512]{1,0:T(4,128)} %param.17) | copy-start | bytes 24580
  7.2 66.8 %all-gather.39.cloned.1.call-start = ((), (), s32[]{:S(2)}) async-start(), calls=%async_computation.47 | async-start | bytes 1769472 | tf_op jit(solution)/shard_map/all_gather | solution.py:188
  9.1 32.4 %copy-start.23 = (f32[2,4,256]{2,1,0:T(4,128)S(1)}, f32[2,4,256]{2,1,0:T(4,128)}, u32[]{:S(2)}) copy-start(f32[2,4,256]{2,1,0:T(4,128)} %param.24) | copy-start | bytes 24580
  9.1 32.5 %copy-start.21 = (bf16[2,128,256]{2,1,0:T(8,128)(2,1)S(1)}, bf16[2,128,256]{2,1,0:T(8,128)(2,1)}, u32[]{:S(2)}) copy-start(bf16[2,128,256]{2,1,0:T(8,128)(2,1)} %param.21) | copy-start | bytes 393220
  13.7 25.8 %all-to-all-start = ((bf16[8,2,64,256]{3,2,1,0:T(8,128)(2,1)}), bf16[8,2,64,256]{3,2,1,0:T(8,128)(2,1)S(1)}, u32[]{:S(2)}, u32[]{:S(2)}) async-start(bf16[8,2,64,256]{3,2,1,0:T(8,128)(2,1)} %bitcast.2), calls=%async_computation | async-start | bytes 1048576 | tf_op jit(solution)/shard_map/all_to_all | solution.py:219
  19.9 70.3 %all-gather.23.cloned.1.call-start = ((), (), s32[]{:S(2)}) async-start(), calls=%async_computation.24 | async-start | bytes 2621440 | tf_op jit(solution)/shard_map/all_gather | solution.py:232
  41.1 96.8 %reduce-scatter.22.cloned.1.call-start = ((), (), s32[]{:S(2)}) async-start(), calls=%async_computation.25 | async-start | bytes 2621440 | tf_op jit(solution)/shard_map/reduce_scatter | solution.py:97
  106.3 38.4 %copy-start.24 = (f32[2,1024]{1,0:T(2,128)S(1)}, f32[2,1024]{1,0:T(2,128)}, u32[]{:S(2)}) copy-start(f32[2,1024]{1,0:T(2,128)} %param.27) | copy-start | bytes 24580
  106.3 83.7 %all-gather.41.cloned.1.call-start = ((), (), s32[]{:S(2)}) async-start(), calls=%async_computation.48 | async-start | bytes 2359296 | tf_op jit(solution)/shard_map/all_gather | solution.py:190
  107.2 36.1 %copy-start.20 = (bf16[2,128,1024]{2,1,0:T(8,128)(2,1)S(1)}, bf16[2,128,1024]{2,1,0:T(8,128)(2,1)}, u32[]{:S(2)}) copy-start(bf16[2,128,1024]{2,1,0:T(8,128)(2,1)} %param.23) | copy-start | bytes 1572868
  107.2 105.9 %all-gather.25.cloned.1.call-start = ((), (), s32[]{:S(2)}) async-start(), calls=%async_computation.26 | async-start | bytes 2621440 | tf_op jit(solution)/shard_map/all_gather | solution.py:93
  143.2 122.0 %all-gather.43.cloned.1.call-start = ((), (), s32[]{:S(2)}) async-start(), calls=%async_computation.49 | async-start | bytes 2359296 | tf_op jit(solution)/shard_map/all_gather | solution.py:191
  144.1 157.2 %reduce-scatter.24.cloned.1.call-start = ((), (), s32[]{:S(2)}) async-start(), calls=%async_computation.27 | async-start | bytes 2621440 | tf_op jit(solution)/shard_map/reduce_scatter | solution.py:97
  265.2 36.1 %copy-start.10 = (bf16[2,128,1024]{2,1,0:T(8,128)(2,1)S(1)}, bf16[2,128,1024]{2,1,0:T(8,128)(2,1)}, u32[]{:S(2)}) copy-start(bf16[2,128,1024]{2,1,0:T(8,128)(2,1)} %reduce-scatter.22.cloned.1.call-done) | copy-start | bytes 1572868
  271.3 79.6 %all-gather.45.cloned.1.call-start = ((), (), s32[]{:S(2)}) async-start(), calls=%async_computation.50 | async-start | bytes 1769472 | tf_op jit(solution)/shard_map/all_gather | solution.py:188
  272.0 101.6 %all-gather.27.cloned.1.call-start = ((), (), s32[]{:S(2)}) async-start(), calls=%async_computation.28 | async-start | bytes 2621440 | tf_op jit(solution)/shard_map/all_gather | solution.py:93
  305.1 115.5 %reduce-scatter.26.cloned.1.call-start = ((), (), s32[]{:S(2)}) async-start(), calls=%async_computation.29 | async-start | bytes 2621440 | tf_op jit(solution)/shard_map/reduce_scatter | solution.py:97
  373.6 13.4 copy-start.18
  389.1 83.8 %all-gather.47.cloned.1.call-start = ((), (), s32[]{:S(2)}) async-start(), calls=%async_computation.51 | async-start | bytes 2359296 | tf_op jit(solution)/shard_map/all_gather | solution.py:190
  389.8 106.3 %all-gather.29.cloned.1.call-start = ((), (), s32[]{:S(2)}) async-start(), calls=%async_computation.30 | async-start | bytes 2621440 | tf_op jit(solution)/shard_map/all_gather | solution.py:93
  424.5 123.8 %all-gather.49.cloned.1.call-start = ((), (), s32[]{:S(2)}) async-start(), calls=%async_computation.52 | async-start | bytes 2359296 | tf_op jit(solution)/shard_map/all_gather | solution.py:191
  425.3 171.7 %reduce-scatter.28.cloned.1.call-start = ((), (), s32[]{:S(2)}) async-start(), calls=%async_computation.31 | async-start | bytes 2621440 | tf_op jit(solution)/shard_map/reduce_scatter | solution.py:97
  574.1 14.8 all-to-all-start.4
  577.5 46.6 %all-gather.31.cloned.1.call-start = ((), (), s32[]{:S(2)}) async-start(), calls=%async_computation.32 | async-start | bytes 2621440 | tf_op jit(solution)/shard_map/all_gather | solution.py:93
  601.4 67.8 %reduce-scatter.30.cloned.1.call-start = ((), (), s32[]{:S(2)}) async-start(), calls=%async_computation.33 | async-start | bytes 2621440 | tf_op jit(solution)/shard_map/reduce_scatter | solution.py:97
  637.6 59.9 %all-gather.33.cloned.1.call-start = ((), (), s32[]{:S(2)}) async-start(), calls=%async_computation.34 | async-start | bytes 2621440 | tf_op jit(solution)/shard_map/all_gather | solution.py:93
  674.8 71.2 %reduce-scatter.32.cloned.1.call-start = ((), (), s32[]{:S(2)}) async-start(), calls=%async_computation.35 | async-start | bytes 2621440 | tf_op jit(solution)/shard_map/reduce_scatter | solution.py:97
  697.5 13.7 copy-start.31
  714.4 59.9 %all-gather.35.cloned.1.call-start = ((), (), s32[]{:S(2)}) async-start(), calls=%async_computation.36 | async-start | bytes 2621440 | tf_op jit(solution)/shard_map/all_gather | solution.py:93
  751.6 67.8 %reduce-scatter.34.cloned.1.call-start = ((), (), s32[]{:S(2)}) async-start(), calls=%async_computation.37 | async-start | bytes 2621440 | tf_op jit(solution)/shard_map/reduce_scatter | solution.py:97
  784.1 35.3 %copy-start.11 = (bf16[2,128,1024]{2,1,0:T(8,128)(2,1)S(1)}, bf16[2,128,1024]{2,1,0:T(8,128)(2,1)}, u32[]{:S(2)}) copy-start(bf16[2,128,1024]{2,1,0:T(8,128)(2,1)} %reduce-scatter.22.cloned.1.call-done) | copy-start | bytes 1572868
  787.8 60.6 %all-gather.37.cloned.1.call-start = ((), (), s32[]{:S(2)}) async-start(), calls=%async_computation.38 | async-start | bytes 2621440 | tf_op jit(solution)/shard_map/all_gather | solution.py:93
  825.6 140.5 %reduce-scatter.36.cloned.1.call-start = ((), (), s32[]{:S(2)}) async-start(), calls=%async_computation.39 | async-start | bytes 2621440 | tf_op jit(solution)/shard_map/reduce_scatter | solution.py:97
  848.3 13.6 copy-start.30
  865.1 109.7 %reduce-scatter.54.cloned.1.call-start = ((), (), s32[]{:S(2)}) async-start(), calls=%async_computation.54 | async-start | bytes 1769472
  877.1 160.3 %reduce-scatter.48.cloned.1.call-start = ((), (), s32[]{:S(2)}) async-start(), calls=%async_computation.45 | async-start | bytes 2359296 | tf_op jit(solution)/shard_map/reduce_scatter | solution.py:257
  883.2 224.9 %reduce-scatter.46.cloned.1.call-start = ((), (), s32[]{:S(2)}) async-start(), calls=%async_computation.44 | async-start | bytes 2359296 | tf_op jit(solution)/shard_map/reduce_scatter | solution.py:257
  889.4 294.7 %reduce-scatter.44.cloned.1.call-start = ((), (), s32[]{:S(2)}) async-start(), calls=%async_computation.43 | async-start | bytes 2359296 | tf_op jit(solution)/shard_map/reduce_scatter | solution.py:256
  895.5 359.4 %reduce-scatter.42.cloned.1.call-start = ((), (), s32[]{:S(2)}) async-start(), calls=%async_computation.42 | async-start | bytes 2359296 | tf_op jit(solution)/shard_map/reduce_scatter | solution.py:256
  901.5 375.6 %reduce-scatter.50.cloned.1.call-start = ((), (), s32[]{:S(2)}) async-start(), calls=%async_computation.46 | async-start | bytes 81920 | tf_op jit(solution)/shard_map/reduce_scatter | solution.py:261
  902.3 439.9 %reduce-scatter.40.cloned.1.call-start = ((), (), s32[]{:S(2)}) async-start(), calls=%async_computation.41 | async-start | bytes 589824 | tf_op jit(solution)/shard_map/reduce_scatter | solution.py:255
  905.6 20.5 %copy-start.5 = (bf16[3,2,512,256]{3,2,1,0:T(8,128)(2,1)S(1)}, bf16[3,2,512,256]{3,2,1,0:T(8,128)(2,1)}, u32[]{:S(2)}) copy-start(bf16[3,2,512,256]{3,2,1,0:T(8,128)(2,1)} %copy-done.4) | copy-start | bytes 4718596
  905.6 501.2 %reduce-scatter.38.cloned.1.call-start = ((), (), s32[]{:S(2)}) async-start(), calls=%async_computation.40 | async-start | bytes 589824 | tf_op jit(solution)/shard_map/reduce_scatter | solution.py:255
  909.0 564.7 %reduce-scatter.52.cloned.1.call-start = ((), (), s32[]{:S(2)}) async-start(), calls=%async_computation.53 | async-start | bytes 1769472
  970.4 139.8 %all-to-all-start.5 = ((bf16[2,128,1024]{1,0,2:T(2,128)(2,1)}), bf16[2,128,1024]{1,0,2:T(2,128)(2,1)}, u32[]{:S(2)}, u32[]{:S(2)}) async-start(bf16[2,128,1024]{1,0,2:T(2,128)(2,1)} %copy.129), calls=%async_computation.13 | async-start | bytes 1048576 | tf_op jit(solution)/shard_map/all_to_all | solution.py:224
  1112.8 363.4 %all-to-all-start.6 = ((bf16[8,2,64,256]{3,2,1,0:T(8,128)(2,1)}), bf16[8,2,64,256]{3,2,1,0:T(8,128)(2,1)}, u32[]{:S(2)}, u32[]{:S(2)}) async-start(bf16[8,2,64,256]{3,2,1,0:T(8,128)(2,1)} %bitcast.278), calls=%async_computation.14 | async-start | bytes 1048576 | tf_op jit(solution)/shard_map/all_to_all | solution.py:227
  1254.8 223.7 %copy-start.1 = (bf16[4,256,256]{2,1,0:T(8,128)(2,1)S(1)}, bf16[4,256,256]{2,1,0:T(8,128)(2,1)}, u32[]{:S(2)}) copy-start(bf16[4,256,256]{2,1,0:T(8,128)(2,1)} %param.16) | copy-start | bytes 1572868
  (21 other events, 96.5 us)
Sparse Core Ops, SparseCore 0:
  10.8 55.4 all-gather.38
  68.5 21.7 all-gather.22
  106.4 31.4 reduce-scatter.21
  140.6 49.2 all-gather.40
  192.0 21.0 all-gather.24
  215.9 49.2 all-gather.42
  271.4 29.9 reduce-scatter.23
  304.1 46.7 all-gather.44
  353.0 20.5 all-gather.26
  389.2 31.4 reduce-scatter.25
  423.6 49.2 all-gather.46
  475.0 21.0 all-gather.28
  499.0 49.2 all-gather.48
  554.4 32.4 reduce-scatter.27
  601.5 22.5 all-gather.30
  637.8 31.4 reduce-scatter.29
  674.9 22.5 all-gather.32
  714.5 31.4 reduce-scatter.31
  751.7 22.5 all-gather.34
  787.9 31.4 reduce-scatter.33
  825.7 22.5 all-gather.36
  865.2 31.3 reduce-scatter.35
  900.1 66.4 reduce-scatter.53
  970.3 67.0 reduce-scatter.47
  1041.4 66.6 reduce-scatter.45
  1111.9 72.2 reduce-scatter.43
  1187.9 66.8 reduce-scatter.41
  1257.9 19.0 reduce-scatter.49
  1280.4 61.8 reduce-scatter.39
  1345.8 60.9 reduce-scatter.37
  1410.2 63.4 reduce-scatter.51

commit v2 on v1

--- a/solution.py
+++ b/solution.py
@@ -89,6 +89,416 @@
     )(qkv, grad, seg_col, seg_row)
 
 
+MESH = pl.DeviceIdType.MESH
+LOG2E = 1.4426950408889634
+
+
+def gelu_pair(values):
+    bell = jnp.exp2(values * values * (-0.5 * LOG2E))
+    t = 1.0 / (1.0 + (0.3275911 * math.sqrt(0.5)) * jnp.abs(values))
+    poly = t * (
+        0.127414796 + t * (-0.142248368 + t * (0.7107068705 + t * (-0.7265760135 + t * 0.5307027145)))
+    )
+    tail = poly * bell
+    phi = jnp.where(values < 0, tail, 1.0 - tail)
+    return values * phi, phi + values * bell * (1.0 / math.sqrt(2.0 * math.pi))
+
+
+class Links:
+    def __init__(self):
+        self.fs, self.cx = lax.axis_size("fsdp"), lax.axis_size("ctx")
+        self.f, self.c, self.t = (lax.axis_index(a) for a in ("fsdp", "ctx", "tp"))
+        self.core, self.chip = lax.rem(self.t, 2), self.t // 2
+        self.sib_t = self.t + 1 - 2 * self.core
+        self.peer_t = lax.rem(self.t + 2, 4)
+        self.sib = (self.f, self.c, self.sib_t)
+        self.peer = (self.f, self.c, self.peer_t)
+        self.across = (self.f, 1 - self.c, self.t)
+
+    def away(self, step):
+        return (lax.rem(self.f + step, self.fs), self.c, self.t)
+
+    def barrier(self):
+        sem = pltpu.get_barrier_semaphore()
+        for target in (self.sib, self.peer, self.across):
+            pl.semaphore_signal(sem, inc=1, device_id=target, device_id_type=MESH)
+
+        def greet(step, carry):
+            pl.semaphore_signal(sem, inc=1, device_id=self.away(step), device_id_type=MESH)
+            return carry
+
+        lax.fori_loop(1, self.fs, greet, 0)
+        pl.semaphore_wait(sem, 2 + self.fs)
+
+
+def remote(src, dst, send, recv, target):
+    return pltpu.make_async_remote_copy(
+        src_ref=src, dst_ref=dst, send_sem=send, recv_sem=recv,
+        device_id=target, device_id_type=MESH,
+    )
+
+
+class RowSum:
+    def __init__(self, lk, part, from_sib, to_peer, from_peer, send, recv):
+        self.lk, self.part, self.from_sib = lk, part, from_sib
+        self.to_peer, self.from_peer, self.send, self.recv = to_peer, from_peer, send, recv
+
+    def sib_copy(self, k):
+        return remote(
+            self.part.at[k, 1 - self.lk.core], self.from_sib.at[k],
+            self.send.at[k, 0], self.recv.at[k, 0], self.lk.sib,
+        )
+
+    def peer_copy(self, k):
+        return remote(
+            self.to_peer.at[k], self.from_peer.at[k],
+            self.send.at[k, 1], self.recv.at[k, 1], self.lk.peer,
+        )
+
+    def first(self, k):
+        self.sib_copy(k).start()
+
+    def second(self, k):
+        self.sib_copy(k).wait_recv()
+        other = 1 - self.lk.chip
+        total = self.part[k, self.lk.core, other].astype(F32) + self.from_sib[k, other].astype(F32)
+        self.to_peer[k] = total.astype(BF)
+        self.peer_copy(k).start()
+
+    def last(self, k):
+        own = self.part[k, self.lk.core, self.lk.chip].astype(F32)
+        own = own + self.from_sib[k, self.lk.chip].astype(F32)
+        self.peer_copy(k).wait_recv()
+        self.sib_copy(k).wait_send()
+        self.peer_copy(k).wait_send()
+        return own + self.from_peer[k].astype(F32)
+
+
+class RowGather:
+    def __init__(self, lk, rows, send, recv):
+        self.lk, self.rows, self.send, self.recv = lk, rows, send, recv
+
+    def block(self, ref, index):
+        return ref.at[pl.ds(pl.multiple_of(index * self.rows, self.rows), self.rows)]
+
+    def copy(self, ref, k, which):
+        index = self.lk.t if which < 2 else self.lk.peer_t
+        part = self.block(ref, index)
+        target = self.lk.peer if which == 0 else self.lk.sib
+        return remote(part, part, self.send.at[k, which], self.recv.at[k, which], target)
+
+    def first(self, ref, k):
+        self.copy(ref, k, 0).start()
+        self.copy(ref, k, 1).start()
+
+    def second(self, ref, k):
+        self.copy(ref, k, 0).wait_recv()
+        self.copy(ref, k, 2).start()
+
+    def last(self, ref, k):
+        self.copy(ref, k, 1).wait_recv()
+        self.copy(ref, k, 2).wait_recv()
+        for which in range(3):
+            self.copy(ref, k, which).wait_send()
+
+
+class WeightGather:
+    def __init__(self, lk, shard, full, z_send, z_recv, x_send, x_recv, own):
+        self.lk, self.shard, self.full = lk, shard, full
+        self.z_send, self.z_recv, self.x_send, self.x_recv = z_send, z_recv, x_send, x_recv
+        self.own = own
+        self.rows = shard.shape[1]
+
+    def block(self, chunk, f, c):
+        first = pl.multiple_of((f * self.lk.cx + c) * self.rows, self.rows)
+        return self.full.at[chunk, pl.ds(first, self.rows)]
+
+    def z_copy(self, chunk, step):
+        return remote(
+            self.shard.at[chunk], self.block(chunk, self.lk.f, self.lk.c),
+            self.z_send.at[chunk, step], self.z_recv.at[chunk, self.lk.fs - step],
+            self.lk.away(step),
+        )
+
+    def x_copy(self, chunk, step):
+        f = lax.rem(self.lk.f + step, self.lk.fs)
+        part = self.block(chunk, f, self.lk.c)
+        return remote(
+            part, part, self.x_send.at[chunk, step], self.x_recv.at[chunk, step], self.lk.across
+        )
+
+    def x_own(self, chunk):
+        return remote(
+            self.shard.at[chunk], self.block(chunk, self.lk.f, self.lk.c),
+            self.x_send.at[chunk, 0], self.x_recv.at[chunk, 0], self.lk.across,
+        )
+
+    def own_copy(self, chunk):
+        return pltpu.make_async_copy(
+            self.shard.at[chunk], self.block(chunk, self.lk.f, self.lk.c), self.own.at[chunk]
+        )
+
+    def each(self, first, work):
+        def body(step, carry):
+            work(step)
+            return carry
+
+        lax.fori_loop(first, self.lk.fs, body, 0)
+
+    def start(self, chunk):
+        self.own_copy(chunk).start()
+        self.x_own(chunk).start()
+        self.each(1, lambda step: self.z_copy(chunk, step).start())
+
+    def forward(self, chunk):
+        def work(step):
+            self.z_copy(chunk, self.lk.fs - step).wait_recv()
+            self.x_copy(chunk, step).start()
+
+        self.each(1, work)
+
+    def finish(self, chunk):
+        self.own_copy(chunk).wait()
+        self.each(0, lambda step: self.x_copy(chunk, step).wait_recv())
+
+    def drain(self, chunk):
+        self.each(1, lambda step: self.z_copy(chunk, step).wait_send())
+        self.each(0, lambda step: self.x_copy(chunk, step).wait_send())
+
+
+def store_part(part, k, cols, values, rows):
+    for block in range(4):
+        part[k, block % 2, block // 2, :, cols] = values[block * rows : (block + 1) * rows].astype(
+            BF
+        )
+
+
+def masked_scores(query, key_rows, same_seq):
+    return jnp.where(
+        same_seq, dot(query, key_rows, NT) * (LOG2E / math.sqrt(HD)), NEG
+    )
+
+
+def forward_kernel(
+    act_in, shard, vec, head_bias, up_bias, seg_col, seg_row,
+    out_w, out_act, out_qkv, out_att, out_nrm, out_std, out_hid, out_glu, out_dglu, out_lse,
+    out_u,
+    w, act, qkv, att, nrm, std, hid, glu, dglu, lse, u, h, part, from_sib, to_peer, from_peer,
+    in_sem, out_sem, rs_send, rs_recv, ag_send, ag_recv, z_send, z_recv, x_send, x_recv, own,
+):
+    layers, packs, rows, width = act.shape
+    mine = rows // 4
+    heads_width = att.shape[3]
+    chunks = shard.shape[0]
+    lk = Links()
+    lk.barrier()
+    rs = RowSum(lk, part, from_sib, to_peer, from_peer, rs_send, rs_recv)
+    ag = RowGather(lk, mine, ag_send, ag_recv)
+    wg = WeightGather(lk, shard, w, z_send, z_recv, x_send, x_recv, own)
+    pending = []
+
+    def save(src, dst):
+        copy = pltpu.make_async_copy(src, dst, out_sem.at[len(pending)])
+        copy.start()
+        pending.append(copy)
+
+    load = pltpu.make_async_copy(act_in, act.at[0], in_sem)
+    load.start()
+    wg.start(0)
+    load.wait()
+    my_rows = pl.ds(pl.multiple_of(lk.t * mine, mine), mine)
+    for k in range(packs):
+        u[k] = act[0, k, my_rows].astype(F32)
+    lse[...] = jnp.zeros_like(lse)
+    wg.forward(0)
+    wg.start(1)
+    wg.finish(0)
+    save(w.at[0], out_w.at[0])
+
+    def project(layer, k):
+        for j in range(3):
+            cols = slice(j * heads_width, (j + 1) * heads_width)
+            acc = dot(act[layer, k], w[3 * layer, :, cols], NN)
+            if j != 1:
+                acc = acc + head_bias[layer, j // 2 : j // 2 + 1]
+            qkv[layer, k, :, cols] = acc.astype(BF)
+        save(qkv.at[layer, k], out_qkv.at[layer, k])
+
+    def attention(layer, k):
+        same_seq = seg_col[k] == seg_row[k]
+        for head in range(heads_width // HD):
+            cols = [slice(j * heads_width + head * HD, j * heads_width + (head + 1) * HD) for j in range(3)]
+            scores = masked_scores(qkv[layer, k, :, cols[0]], qkv[layer, k, :, cols[1]], same_seq)
+            top = jnp.max(scores, axis=1, keepdims=True)
+            weighted = jnp.exp2(scores - top)
+            total = jnp.sum(weighted, axis=1, keepdims=True)
+            lse[layer, k, :, head : head + 1] = top + jnp.log2(total)
+            probs = (weighted * (1.0 / total)).astype(BF)
+            att[layer, k, :, cols[0]] = dot(probs, qkv[layer, k, :, cols[2]], NN).astype(BF)
+        save(lse.at[layer, k], out_lse.at[layer, k])
+        save(att.at[layer, k], out_att.at[layer, k])
+        for j in range(width // 256):
+            cols = slice(j * 256, (j + 1) * 256)
+            acc = dot(att[layer, k], w[3 * layer, cols, 3 * heads_width :], NT)
+            store_part(part, k, cols, acc, mine)
+        rs.first(k)
+
+    def normalize(layer, which, k, resid):
+        mean = jnp.mean(resid, axis=1, keepdims=True)
+        centred = resid - mean
+        scale = lax.rsqrt(jnp.mean(centred * centred, axis=1, keepdims=True) + EPS)
+        normed = centred * scale
+        nrm[layer, which, k] = normed
+        std[layer, which, k] = jnp.broadcast_to(scale, std.shape[3:])
+        save(nrm.at[layer, which, k], out_nrm.at[layer, which, k])
+        save(std.at[layer, which, k], out_std.at[layer, which, k])
+        return normed * vec[layer, 2 + which : 3 + which] + vec[layer, 4 + which : 5 + which]
+
+    def norm_one(layer, k):
+        hidden = normalize(layer, 0, k, u[k] + rs.last(k) + vec[layer, 0:1])
+        h[k] = hidden
+        hid[layer, k, my_rows] = hidden.astype(BF)
+        ag.first(hid.at[layer, k], k)
+
+    def expand(layer, k):
+        def tile(j, carry):
+            cols = pl.ds(pl.multiple_of(j * 256, 256), 256)
+            acc = dot(hid[layer, k], w[3 * layer + 1, :, cols], NN) + up_bias[layer, :, cols]
+            value, slope = gelu_pair(acc)
+            glu[layer, k, :, cols] = value.astype(BF)
+            dglu[layer, k, :, cols] = slope.astype(BF)
+            return carry
+
+        lax.fori_loop(0, width // 256, tile, 0)
+        save(glu.at[layer, k], out_glu.at[layer, k])
+        save(dglu.at[layer, k], out_dglu.at[layer, k])
+
+    def contract(layer, k):
+        def tile(j, carry):
+            cols = pl.ds(pl.multiple_of(j * 256, 256), 256)
+            acc = dot(glu[layer, k], w[3 * layer + 2, cols, :], NT)
+            store_part(part, k, cols, acc, mine)
+            return carry
+
+        lax.fori_loop(0, width // 256, tile, 0)
+        rs.first(k)
+
+    def norm_two(layer, k):
+        out = normalize(layer, 1, k, h[k] + rs.last(k) + vec[layer, 1:2])
+        u[k] = out
+        if layer + 1 < layers:
+            act[layer + 1, k, my_rows] = out.astype(BF)
+            ag.first(act.at[layer + 1, k], k)
+        else:
+            save(u.at[k], out_u.at[k])
+
+    def weights_next(chunk):
+        if chunk < chunks:
+            if chunk + 1 < chunks:
+                wg.start(chunk + 1)
+            wg.forward(chunk)
+
+    def weights_ready(chunk):
+        wg.finish(chunk)
+        save(w.at[chunk], out_w.at[chunk])
+
+    for layer in range(layers):
+        base = 3 * layer
+        more = layer + 1 < layers
+        if layer:
+            weights_ready(base)
+            ag.last(act.at[layer, 0], 0)
+            save(act.at[layer, 0], out_act.at[layer - 1, 0])
+        project(layer, 0)
+        if layer:
+            ag.second(act.at[layer, 1], 1)
+        attention(layer, 0)
+        weights_next(base + 1)
+        if layer:
+            ag.last(act.at[layer, 1], 1)
+            save(act.at[layer, 1], out_act.at[layer - 1, 1])
+        project(layer, 1)
+        rs.second(0)
+        attention(layer, 1)
+        norm_one(layer, 0)
+        rs.second(1)
+        ag.second(hid.at[layer, 0], 0)
+        norm_one(layer, 1)
+        weights_ready(base + 1)
+        weights_next(base + 2)
+        ag.last(hid.at[layer, 0], 0)
+        save(hid.at[layer, 0], out_hid.at[layer, 0])
+        expand(layer, 0)
+        ag.second(hid.at[layer, 1], 1)
+        weights_ready(base + 2)
+        contract(layer, 0)
+        weights_next(base + 3)
+        ag.last(hid.at[layer, 1], 1)
+        save(hid.at[layer, 1], out_hid.at[layer, 1])
+        expand(layer, 1)
+        rs.second(0)
+        contract(layer, 1)
+        norm_two(layer, 0)
+        rs.second(1)
+        if more:
+            ag.second(act.at[layer + 1, 0], 0)
+        norm_two(layer, 1)
+    for chunk in range(chunks):
+        wg.drain(chunk)
+    for copy in pending:
+        copy.wait()
+
+
+def forward(act, shard, vec, head_bias, up_bias, seg_col, seg_row):
+    packs, rows, width = act.shape
+    chunks = shard.shape[0]
+    layers = chunks // 3
+    mine = rows // 4
+    heads = head_bias.shape[2]
+    fs = lax.axis_size("fsdp")
+    shapes = dict(
+        w=((chunks, width, width), BF),
+        act=((layers, packs, rows, width), BF),
+        qkv=((layers, packs, rows, 3 * heads), BF),
+        att=((layers, packs, rows, heads), BF),
+        nrm=((layers, 2, packs, mine, width), F32),
+        std=((layers, 2, packs, mine, 128), F32),
+        hid=((layers, packs, rows, width), BF),
+        glu=((layers, packs, rows, width), BF),
+        dglu=((layers, packs, rows, width), BF),
+        lse=((layers, packs, rows, 128), F32),
+        u=((packs, mine, width), F32),
+    )
+    outs = {name: jax.ShapeDtypeStruct(*shape) for name, shape in shapes.items()}
+    outs["act"] = jax.ShapeDtypeStruct((layers - 1, packs, rows, width), BF)
+    copies = chunks + (layers - 1) * packs + layers * packs * 10 + packs
+    dma = pltpu.SemaphoreType.DMA
+    whole = pl.BlockSpec(memory_space=pl.ANY)
+    vmem = pl.BlockSpec(memory_space=pltpu.VMEM)
+    return pl.pallas_call(
+        forward_kernel,
+        in_specs=[whole, whole, vmem, vmem, vmem, vmem, vmem],
+        out_specs=[whole] * len(outs),
+        out_shape=list(outs.values()),
+        scratch_shapes=[pltpu.VMEM(*shape) for shape in shapes.values()]
+        + [
+            pltpu.VMEM((packs, mine, width), F32),
+            pltpu.VMEM((packs, 2, 2, mine, width), BF),
+            pltpu.VMEM((packs, 2, mine, width), BF),
+            pltpu.VMEM((packs, mine, width), BF),
+            pltpu.VMEM((packs, mine, width), BF),
+            dma(()), dma((copies,)),
+            dma((packs, 2)), dma((packs, 2)), dma((packs, 3)), dma((packs, 3)),
+            dma((chunks, fs)), dma((chunks, fs)), dma((chunks, fs)), dma((chunks, fs)),
+            dma((chunks,)),
+        ],
+        compiler_params=pltpu.CompilerParams(
+            collective_id=0, has_side_effects=True, vmem_limit_bytes=60 << 20
+        ),
+        name="forward",
+    )(act, shard, vec, head_bias, up_bias, seg_col, seg_row)
+
+
 def gather_rows(values):
     return lax.all_gather(values.astype(BF), "tp", axis=1, tiled=True)
 
@@ -121,23 +531,6 @@
 
 def mm(spec, left, right):
     return jnp.einsum(spec, left, right, preferred_element_type=F32)
-
-
-def layer_forward(resid, act, weights, vectors, seg_col, seg_row):
-    w_qkv, w_out, w_up, w_down = weights
-    head_bias, full_bias, gain, offset, up_bias = vectors
-    proj = mm("ktd,cdh->ckth", act, w_qkv)
-    zero = jnp.zeros_like(head_bias[0])
-    qkv = (proj + jnp.stack([head_bias[0], zero, head_bias[1]])[:, None, None, :]).astype(BF)
-    attended = attend(qkv, seg_col, seg_row)
-    mixed = scatter_rows(mm("kth,dh->ktd", attended, w_out))
-    hidden, normed1, scale1 = norm_forward(resid + mixed + full_bias[0], gain[0], offset[0])
-    hidden_full = gather_rows(hidden)
-    upper = mm("ktd,df->ktf", hidden_full, w_up) + up_bias
-    gelu_low = gelu(upper).astype(BF)
-    lowered = scatter_rows(mm("ktf,df->ktd", gelu_low, w_down))
-    out, normed2, scale2 = norm_forward(hidden + lowered + full_bias[1], gain[1], offset[1])
-    return out, (act, qkv, attended, normed1, scale1, hidden_full, upper, gelu_low, normed2, scale2)
 
 
 def layer_backward(upstream, saved, weights, vectors, seg_col, seg_row):
@@ -148,8 +541,7 @@
     grad_lowered = gather_rows(grad2)
     g_down = mm("ktd,ktf->df", grad_lowered, gelu_low).astype(BF)
     grad_gelu = mm("ktd,df->ktf", grad_lowered, w_down).astype(BF)
-    _, pull = jax.vjp(gelu, upper)
-    grad_upper = pull(grad_gelu.astype(F32))[0].astype(BF)
+    grad_upper = (grad_gelu.astype(F32) * upper.astype(F32)).astype(BF)
     up_grad = jnp.sum(grad_upper, axis=(0, 1), dtype=F32)
     g_up = mm("ktd,ktf->df", hidden_full, grad_upper).astype(BF)
     grad_hidden = scatter_rows(mm("ktf,df->ktd", grad_upper, w_up)) + grad2
@@ -181,16 +573,11 @@
     my_first = lax.axis_index("ctx") * mine
     tp_index = lax.axis_index("tp")
 
-    weights = []
-    for layer in range(layers):
-        weights.append(
-            (
-                lax.all_gather(w_qkv[layer], GRP, axis=1, tiled=True),
-                lax.all_gather(w_out[layer], GRP, axis=0, tiled=True),
-                lax.all_gather(w_up[layer], GRP, axis=0, tiled=True),
-                lax.all_gather(w_down[layer], GRP, axis=0, tiled=True),
-            )
-        )
+    shard = jnp.concatenate(
+        [w_qkv[:, 0], w_qkv[:, 1], w_qkv[:, 2], w_out, w_up, w_down], axis=2
+    )
+    shard = shard.reshape(layers, shard.shape[1], 3, -1).transpose(0, 2, 1, 3)
+    shard = shard.reshape(layers * 3, shard.shape[2], -1)
     vec = jnp.concatenate([biases[:, 2:], norm_gain, norm_bias], axis=1)
     vec = lax.all_gather(vec, "tp", axis=2, tiled=True)
     vectors = [
@@ -230,19 +617,34 @@
 
     embedded = (tokens.astype(F32) + time_embed.astype(F32)).astype(BF)
     act = lax.all_gather(to_packs(embedded), "tp", axis=2, tiled=True)
-    resid = lax.dynamic_slice_in_dim(act, tp_index * (pack // tp), pack // tp, 1).astype(F32)
     upstream = lax.all_to_all(
         to_packs(cotangent), "tp", split_axis=1, concat_axis=2, tiled=True
     ).astype(F32)
     seg = lax.dynamic_slice_in_dim(segment_ids, my_first, mine)
     seg_col, seg_row = seg[:, :, None], seg[:, None, :]
 
+    full_w, o_act, o_qkv, o_att, o_nrm, o_std, o_hid, o_glu, o_dglu, o_lse, resid = forward(
+        act, shard, vec, biases[:, :2], up_bias[:, None], seg_col, seg_row
+    )
+    weights = []
     saved = []
+    hw = o_att.shape[3]
     for layer in range(layers):
-        if layer:
-            act = gather_rows(resid)
-        resid, kept = layer_forward(resid, act, weights[layer], vectors[layer], seg_col, seg_row)
-        saved.append(kept)
+        first = full_w[3 * layer]
+        weights.append(
+            (
+                jnp.stack([first[:, c * hw : (c + 1) * hw] for c in range(3)]),
+                first[:, 3 * hw :], full_w[3 * layer + 1], full_w[3 * layer + 2],
+            )
+        )
+        saved.append(
+            (
+                act if layer == 0 else o_act[layer - 1],
+                jnp.stack([o_qkv[layer, :, :, c * hw : (c + 1) * hw] for c in range(3)]),
+                o_att[layer], o_nrm[layer, 0], o_std[layer, 0, :, :, :1], o_hid[layer],
+                o_dglu[layer], o_glu[layer], o_nrm[layer, 1], o_std[layer, 1, :, :, :1],
+            )
+        )
     outputs = from_packs(resid)
     shards = [None] * layers
     parts = [None] * layers

time: 1500 us -> 1170 us (0.78)
  waiting for transfers between devices: 1000 us -> 642 us
  Pallas kernels: 37.1 us -> 218 us
  blocking collectives: 166 us -> 82.7 us
  matrix products: 121 us -> 80.9 us
  other arithmetic: 69.5 us -> 39.3 us
    pallas_call x2 -> x1, Pallas kernels: 17.2 us -> 198 us  [forward(): pl.pallas_call(forward_kernel, in_specs=[whole, whole, vmem, vmem, vmem,...]
    all_gather x6 -> x0, waiting for transfers between devices: 174 us -> none  [the longest x2 92.6 us: local(): lax.all_gather(w_up[layer], GRP, axis=0, tiled=True)]
    reduce_scatter x8 -> x4, waiting for transfers between devices: 180 us -> 94.6 us  [scatter_rows(): lax.psum_scatter(values.astype(BF), 'tp', scatter_dimension=1, tiled=True)]
    all_gather x7 -> x4, waiting for transfers between devices: 159 us -> 78.2 us  [gather_rows(): return lax.all_gather(values.astype(BF), 'tp', axis=1, tiled=True)]
    all_gather x2 -> x0, blocking collectives: 64 us -> none  [local(): lax.all_gather(w_out[layer], GRP, axis=0, tiled=True)]
    dot_general x32 -> x24, matrix products: 121 us -> 80.9 us  [mm(): return jnp.einsum(spec, left, right, preferred_element_type=F32)]
    convert_element_type x2 -> x0, other arithmetic: 22 us -> none  [layer_forward(): gelu_low = gelu(upper).astype(BF)]
    all_to_all x1 -> x0, blocking collectives: 17 us -> none  [to_packs(): slots = lax.all_to_all(slots, GRP, split_axis=0, concat_axis=0, tiled=True)]
  transfers between devices with their start and end apart: 35 -> 23, of which waited for: 29 -> 18; matrix products, arithmetic and copies ran while one was open for 10% -> 9% of each run, Pallas kernels for 0% -> 0%
where the time goes in v2:
time: 1170 us; the launch traced here: 1160 us
  waiting for transfers between devices  642 us (55%)
  Pallas kernels  218 us (19%)
  blocking collectives  82.7 us (7%)
  matrix products  80.9 us (7%)
  local copies, waits for them, and re-layouts  54 us (5%)
  other arithmetic  39.3 us (3%)
  starting transfers between devices  24 us (2%)
  between operations  15.5 us (1%)
    pallas_call x1, Pallas kernels, forward(): pl.pallas_call(forward_kernel, in_specs=[whole, whole, vmem, vmem, vmem,...  198 us
    reduce_scatter x2, waiting for transfers between devices, local(): lax.psum_scatter(grads[2], GRP, scatter_dimension=0, tiled=True)  137 us
    reduce_scatter x2, waiting for transfers between devices, local(): lax.psum_scatter(grads[3], GRP, scatter_dimension=0, tiled=True)  133 us
    reduce_scatter x4, waiting for transfers between devices, scatter_rows(): lax.psum_scatter(values.astype(BF), 'tp', scatter_dimension=1, tiled=True)  94.6 us
    reduce_scatter x2, waiting for transfers between devices, local(): lax.psum_scatter(grads[1], GRP, scatter_dimension=0, tiled=True)  93.3 us
    dot_general x24, matrix products, mm(): return jnp.einsum(spec, left, right, preferred_element_type=F32)  80.9 us
    all_gather x4, waiting for transfers between devices, gather_rows(): return lax.all_gather(values.astype(BF), 'tp', axis=1, tiled=True)  78.2 us
    unnamed x20, waiting for transfers between devices  65.6 us
  transfers between devices with their start and end apart: 23, of which 18 were waited for; matrix products, arithmetic and copies ran while one was open for 9% of the time, Pallas kernels for 0%

profile of v2, /device:TPU:8, one launch (start us, length us, event | category | flops | bytes accessed | tf_op | source)
XLA Modules:
  0.0 1156.8 jit_solution(16455244240107035936)
XLA Ops:
  11.8 6.3 all-to-all-start
  18.0 4.7 all_gather.21
  23.4 7.8 all-to-all-done
  34.4 4.9 all-to-all-start.3
  41.1 5.6 all_gather.23.vec
  47.8 4.9 all-to-all-done.3
  54.9 3.5 all-to-all-start.4
  59.8 7.4 all-to-all-done.4
  72.5 197.8 %forward.1 = (bf16[6,1024,1024]{2,1,0:T(8,128)(2,1)}, bf16[1,2,512,1024]{3,2,1,0:T(8,128)(2,1)}, bf16[2,2,512,768]{3,2,1,0:T(8,128)(2,1)}, bf16[2,2,512,256]{3,2...) custom-call(bf16[2,512,1024]{2,1,0:T(8,128)(2,1)} %all-gather.6.clon, ...), custom_call_target="tpu_custom_call" | custom-call | tf_op jit(solution)/shard_map/forward/pallas_call | solution.py:478
  275.5 25.5 %all-gather.8.cloned.1.call-done = bf16[2,512,1024]{2,1,0:T(8,128)(2,1)} async-done(((bf16[2,128,1024]{2,1,0:T(8,128)(2,1)}), bf16[2,512,1024]{2,1,0:T(8,128)(2,1)}) %all-gather.8.cloned.1.call-update) | async-done | bytes 2097168 | tf_op jit(solution)/shard_map/all_gather | solution.py:503
  301.0 5.2 convert_reduce_fusion
  307.6 5.3 fusion.32
  313.0 31.5 %reduce-scatter.18.cloned.1.call-done = bf16[2,128,1024]{2,1,0:T(8,128)(2,1)} async-done(((bf16[2,512,1024]{2,1,0:T(8,128)(2,1)}), bf16[2,128,1024]{2,1,0:T(8,128)(2,1)}) %reduce-scatter.18.cloned.1.call-update) | async-done | bytes 524304 | tf_op jit(solution)/shard_map/reduce_scatter | solution.py:507
  354.1 4.1 slice_bitcast_fusion
  360.7 11.6 %all-gather.10.cloned.1.call-done = bf16[2,512,1024]{2,1,0:T(8,128)(2,1)} async-done(((bf16[2,128,1024]{2,1,0:T(8,128)(2,1)}), bf16[2,512,1024]{2,1,0:T(8,128)(2,1)}) %all-gather.10.cloned.1.call-update) | async-done | bytes 2097168 | tf_op jit(solution)/shard_map/all_gather | solution.py:503
  374.9 10.3 shard_map.213
  388.5 31.5 %reduce-scatter.20.cloned.1.call-done = bf16[2,128,1024]{2,1,0:T(8,128)(2,1)} async-done(((bf16[2,512,1024]{2,1,0:T(8,128)(2,1)}), bf16[2,128,1024]{2,1,0:T(8,128)(2,1)}) %reduce-scatter.20.cloned.1.call-update) | async-done | bytes 524304 | tf_op jit(solution)/shard_map/reduce_scatter | solution.py:507
  425.1 22.7 %all-gather.12.cloned.1.call-done = bf16[2,512,1024]{2,1,0:T(8,128)(2,1)} async-done(((bf16[2,128,1024]{2,1,0:T(8,128)(2,1)}), bf16[2,512,1024]{2,1,0:T(8,128)(2,1)}) %all-gather.12.cloned.1.call-update) | async-done | bytes 2097168 | tf_op jit(solution)/shard_map/all_gather | solution.py:503
  447.8 5.2 convert_reduce_fusion.1
  454.4 5.4 fusion.37
  459.8 31.5 %reduce-scatter.22.cloned.1.call-done = bf16[2,128,1024]{2,1,0:T(8,128)(2,1)} async-done(((bf16[2,512,1024]{2,1,0:T(8,128)(2,1)}), bf16[2,128,1024]{2,1,0:T(8,128)(2,1)}) %reduce-scatter.22.cloned.1.call-update) | async-done | bytes 524304 | tf_op jit(solution)/shard_map/reduce_scatter | solution.py:507
  501.4 18.4 %all-gather.14.cloned.1.call-done = bf16[2,512,1024]{2,1,0:T(8,128)(2,1)} async-done(((bf16[2,128,1024]{2,1,0:T(8,128)(2,1)}), bf16[2,512,1024]{2,1,0:T(8,128)(2,1)}) %all-gather.14.cloned.1.call-update) | async-done | bytes 2097168 | tf_op jit(solution)/shard_map/all_gather | solution.py:503
  522.4 9.9 shard_map.214
  533.5 3.2 bitcast_convert_fusion.4
  536.8 4.6 fusion.55
  541.3 4.2 copy.161
  545.5 3.2 copy.167
  548.8 5.9 bitcast_convert_fusion
  555.0 6.0 bitcast_convert_fusion.1
  561.0 6.0 bitcast_convert_fusion.2
  567.1 6.0 bitcast_convert_fusion.3
  581.0 3.2 fusion.59
  584.3 3.3 fusion.58
  588.2 11.5 all_to_all.65
  600.2 5.1 fusion.52
  605.3 4.2 copy.159
  613.2 25.9 %all_to_all.66 = bf16[8,2,64,256]{3,2,1,0:T(8,128)(2,1)S(1)} all-to-all(bf16[8,2,64,256]{3,2,1,0:T(8,128)(2,1)S(1)} %bitcast.334), channel_id=1, replica_groups=mesh['fsdp'=4,'ctx'=2,'tp'=4] {'fsdp','ctx'}, dimensions={0} | all-to-all | bytes 1048576 | tf_op jit(solution)/shard_map/all_to_all | solution.py:614
  642.7 3.5 all-to-all-start.5
  647.7 62.4 %reduce-scatter.36.cloned.1.call-done = bf16[128,1024]{1,0:T(8,128)(2,1)} async-done(((bf16[1024,1024]{1,0:T(8,128)(2,1)}), bf16[128,1024]{1,0:T(8,128)(2,1)}) %reduce-scatter.36.cloned.1.call-update) | async-done | bytes 262160 | tf_op jit(solution)/shard_map/reduce_scatter | solution.py:659
  710.1 71.1 %reduce-scatter.34.cloned.1.call-done = bf16[128,1024]{1,0:T(8,128)(2,1)} async-done(((bf16[1024,1024]{1,0:T(8,128)(2,1)}), bf16[128,1024]{1,0:T(8,128)(2,1)}) %reduce-scatter.34.cloned.1.call-update) | async-done | bytes 262160 | tf_op jit(solution)/shard_map/reduce_scatter | solution.py:659
  785.0 4.8 all-to-all-start.6
  789.8 66.7 %reduce-scatter.32.cloned.1.call-done = bf16[128,1024]{1,0:T(8,128)(2,1)} async-done(((bf16[1024,1024]{1,0:T(8,128)(2,1)}), bf16[128,1024]{1,0:T(8,128)(2,1)}) %reduce-scatter.32.cloned.1.call-update) | async-done | bytes 262160 | tf_op jit(solution)/shard_map/reduce_scatter | solution.py:658
  856.5 70.5 %reduce-scatter.30.cloned.1.call-done = bf16[128,1024]{1,0:T(8,128)(2,1)} async-done(((bf16[1024,1024]{1,0:T(8,128)(2,1)}), bf16[128,1024]{1,0:T(8,128)(2,1)}) %reduce-scatter.30.cloned.1.call-update) | async-done | bytes 262160 | tf_op jit(solution)/shard_map/reduce_scatter | solution.py:658
  929.4 19.8 %reduce-scatter.38.cloned.1.call-done = f32[2,6,256]{2,1,0:T(8,128)} async-done(((f32[2,6,1024]{2,1,0:T(8,128)}), f32[2,6,256]{2,1,0:T(8,128)}) %reduce-scatter.38.cloned.1.call-update) | async-done | bytes 12304 | tf_op jit(solution)/shard_map/reduce_scatter | solution.py:663
  949.2 35.1 %all-reduce = (f32[2,6,256]{2,1,0:T(8,128)S(1)}, f32[2,2,256]{2,1,0:T(2,128)S(1)}, f32[2,1024]{1,0:T(2,128)}) all-reduce(f32[2,6,256]{2,1,0:T(8,128)} %reduce-scatter.38.cloned.1.call-done, f32[2,2,256]{2,1,0:T(2,128)S(1)} %pad_maximum_fusion.7, ...), channel_id=1, replica_groups=mesh['fsdp'=4,'ctx'=2,'tp'=4] {'fsdp','ctx'}, use_global_device_ids=true, to_apply=%region_38.39 | all-reduce | flops 6144 | bytes 49152 | tf_op jit(solution)/shard_map/psum | solution.py:664
  985.5 28.8 %reduce-scatter.28.cloned.1.call-done = bf16[128,256]{1,0:T(8,128)(2,1)} async-done(((bf16[1024,256]{1,0:T(8,128)(2,1)}), bf16[128,256]{1,0:T(8,128)(2,1)}) %reduce-scatter.28.cloned.1.call-update) | async-done | bytes 65552 | tf_op jit(solution)/shard_map/reduce_scatter | solution.py:657
  1014.3 64.5 %reduce-scatter.26.cloned.1.call-done = bf16[128,256]{1,0:T(8,128)(2,1)} async-done(((bf16[1024,256]{1,0:T(8,128)(2,1)}), bf16[128,256]{1,0:T(8,128)(2,1)}) %reduce-scatter.26.cloned.1.call-update) | async-done | bytes 65552 | tf_op jit(solution)/shard_map/reduce_scatter | solution.py:657
  1080.4 65.3 %reduce-scatter.40.cloned.1.call-done = bf16[128,768]{1,0:T(8,128)(2,1)} async-done(((bf16[1024,768]{1,0:T(8,128)(2,1)}), bf16[128,768]{1,0:T(8,128)(2,1)}) %reduce-scatter.40.cloned.1.call-update) | async-done | bytes 196624
  (209 shorter events, 95.5 us)
Async XLA Ops:
  7.2 25.7 %copy-start = (bf16[4,256,256]{2,1,0:T(8,128)(2,1)S(1)}, bf16[4,256,256]{2,1,0:T(8,128)(2,1)}, u32[]{:S(2)}) copy-start(bf16[4,256,256]{2,1,0:T(8,128)(2,1)} %param.16) | copy-start | bytes 1572868
  7.2 10.8 copy-start.31
  11.8 19.5 %all-to-all-start = ((bf16[8,2,64,256]{3,2,1,0:T(8,128)(2,1)}), bf16[8,2,64,256]{3,2,1,0:T(8,128)(2,1)S(1)}, u32[]{:S(2)}, u32[]{:S(2)}) async-start(bf16[8,2,64,256]{3,2,1,0:T(8,128)(2,1)} %bitcast.2), calls=%async_computation | async-start | bytes 1048576 | tf_op jit(solution)/shard_map/all_to_all | solution.py:606
  18.0 54.5 %all-gather.6.cloned.1.call-start = ((), (), s32[]{:S(2)}) async-start(), calls=%async_computation.20 | async-start | bytes 2621440 | tf_op jit(solution)/shard_map/all_gather | solution.py:619
  32.8 6.4 copy-start.30
  32.8 7.0 copy-start.28
  32.8 7.6 copy-start.29
  32.9 8.2 copy-start.32
  32.9 8.2 copy-start.33
  34.4 18.3 %all-to-all-start.3 = ((bf16[8,2,64,256]{3,2,1,0:T(8,128)(2,1)}), bf16[8,2,64,256]{3,2,1,0:T(8,128)(2,1)S(1)}, u32[]{:S(2)}, u32[]{:S(2)}) async-start(bf16[8,2,64,256]{3,2,1,0:T(8,128)(2,1)} %bitcast.20), calls=%async_computation.3 | async-start | bytes 1048576 | tf_op jit(solution)/shard_map/all_to_all | solution.py:606
  46.7 8.2 copy-start.26
  52.7 5.7 copy-start.25
  52.7 5.7 copy-start.17
  52.8 5.7 copy-start.18
  52.8 5.7 copy-start.27
  54.9 12.3 %all-to-all-start.4 = ((bf16[2,512,256]{2,0,1:T(2,128)(2,1)}), bf16[2,512,256]{2,0,1:T(2,128)(2,1)S(1)}, u32[]{:S(2)}, u32[]{:S(2)}) async-start(bf16[2,512,256]{2,0,1:T(2,128)(2,1)} %copy.126), calls=%async_computation.4 | async-start | bytes 1048576 | tf_op jit(solution)/shard_map/all_to_all | solution.py:620
  58.4 242.6 %all-gather.8.cloned.1.call-start = ((), (), s32[]{:S(2)}) async-start(), calls=%async_computation.21 | async-start | bytes 2621440 | tf_op jit(solution)/shard_map/all_gather | solution.py:503
  275.4 69.1 %reduce-scatter.18.cloned.1.call-start = ((), (), s32[]{:S(2)}) async-start(), calls=%async_computation.22 | async-start | bytes 2621440 | tf_op jit(solution)/shard_map/reduce_scatter | solution.py:507
  312.9 59.4 %all-gather.10.cloned.1.call-start = ((), (), s32[]{:S(2)}) async-start(), calls=%async_computation.23 | async-start | bytes 2621440 | tf_op jit(solution)/shard_map/all_gather | solution.py:503
  349.6 70.5 %reduce-scatter.20.cloned.1.call-start = ((), (), s32[]{:S(2)}) async-start(), calls=%async_computation.24 | async-start | bytes 2621440 | tf_op jit(solution)/shard_map/reduce_scatter | solution.py:507
  360.7 14.1 %copy-start.2 = (s32[2,512,1]{2,1,0:T(8,128)S(1)}, s32[2,512,1]{2,1,0:T(8,128)}, u32[]{:S(2)}) copy-start(s32[2,512,1]{2,1,0:T(8,128)} %copy.117.seg_col) | copy-start | bytes 12292
  360.7 14.1 %copy-start.7 = (s32[2,1,512]{2,1,0:T(1,128)S(1)}, s32[2,1,512]{2,1,0:T(1,128)}, u32[]{:S(2)}) copy-start(s32[2,1,512]{2,1,0:T(1,128)} %broadcast_in_dim.8.seg_row) | copy-start | bytes 12292
  374.9 10.4 copy-start.22
  374.9 10.4 copy-start.23
  374.9 10.4 copy-start.24
  388.5 59.3 %all-gather.12.cloned.1.call-start = ((), (), s32[]{:S(2)}) async-start(), calls=%async_computation.25 | async-start | bytes 2621440 | tf_op jit(solution)/shard_map/all_gather | solution.py:503
  425.1 66.3 %reduce-scatter.22.cloned.1.call-start = ((), (), s32[]{:S(2)}) async-start(), calls=%async_computation.26 | async-start | bytes 2621440 | tf_op jit(solution)/shard_map/reduce_scatter | solution.py:507
  459.8 60.0 %all-gather.14.cloned.1.call-start = ((), (), s32[]{:S(2)}) async-start(), calls=%async_computation.27 | async-start | bytes 2621440 | tf_op jit(solution)/shard_map/all_gather | solution.py:503
  497.1 143.3 %reduce-scatter.24.cloned.1.call-start = ((), (), s32[]{:S(2)}) async-start(), calls=%async_computation.28 | async-start | bytes 2621440 | tf_op jit(solution)/shard_map/reduce_scatter | solution.py:507
  497.3 2.9 copy-start.12
  522.3 11.1 copy-start.19
  522.3 11.1 copy-start.20
  522.4 11.1 copy-start.21
  536.7 109.8 %reduce-scatter.42.cloned.1.call-start = ((), (), s32[]{:S(2)}) async-start(), calls=%async_computation.37 | async-start | bytes 1769472
  548.8 161.3 %reduce-scatter.36.cloned.1.call-start = ((), (), s32[]{:S(2)}) async-start(), calls=%async_computation.34 | async-start | bytes 2359296 | tf_op jit(solution)/shard_map/reduce_scatter | solution.py:659
  554.7 226.5 %reduce-scatter.34.cloned.1.call-start = ((), (), s32[]{:S(2)}) async-start(), calls=%async_computation.33 | async-start | bytes 2359296 | tf_op jit(solution)/shard_map/reduce_scatter | solution.py:659
  561.0 295.5 %reduce-scatter.32.cloned.1.call-start = ((), (), s32[]{:S(2)}) async-start(), calls=%async_computation.32 | async-start | bytes 2359296 | tf_op jit(solution)/shard_map/reduce_scatter | solution.py:658
  567.0 360.0 %reduce-scatter.30.cloned.1.call-start = ((), (), s32[]{:S(2)}) async-start(), calls=%async_computation.31 | async-start | bytes 2359296 | tf_op jit(solution)/shard_map/reduce_scatter | solution.py:658
  573.1 376.1 %reduce-scatter.38.cloned.1.call-start = ((), (), s32[]{:S(2)}) async-start(), calls=%async_computation.35 | async-start | bytes 81920 | tf_op jit(solution)/shard_map/reduce_scatter | solution.py:663
  581.0 433.3 %reduce-scatter.28.cloned.1.call-start = ((), (), s32[]{:S(2)}) async-start(), calls=%async_computation.30 | async-start | bytes 589824 | tf_op jit(solution)/shard_map/reduce_scatter | solution.py:657
  584.3 3.5 copy-start.16
  584.3 494.5 %reduce-scatter.26.cloned.1.call-start = ((), (), s32[]{:S(2)}) async-start(), calls=%async_computation.29 | async-start | bytes 589824 | tf_op jit(solution)/shard_map/reduce_scatter | solution.py:657
  587.7 558.0 %reduce-scatter.40.cloned.1.call-start = ((), (), s32[]{:S(2)}) async-start(), calls=%async_computation.36 | async-start | bytes 1769472
  613.2 27.3 %copy-start.11 = (f32[2,128,1024]{2,1,0:T(8,128)S(1)}, f32[2,128,1024]{2,1,0:T(8,128)}, u32[]{:S(2)}) copy-start(f32[2,128,1024]{2,1,0:T(8,128)} %copy-done.10) | copy-start | bytes 3145732
  642.7 140.6 %all-to-all-start.5 = ((bf16[2,128,1024]{1,0,2:T(2,128)(2,1)}), bf16[2,128,1024]{1,0,2:T(2,128)(2,1)S(1)}, u32[]{:S(2)}, u32[]{:S(2)}) async-start(bf16[2,128,1024]{1,0,2:T(2,128)(2,1)} %copy.130), calls=%async_computation.9 | async-start | bytes 1048576 | tf_op jit(solution)/shard_map/all_to_all | solution.py:611
  784.2 144.9 %copy-start.4 = (bf16[3,2,512,256]{3,2,1,0:T(8,128)(2,1)S(1)}, bf16[3,2,512,256]{3,2,1,0:T(8,128)(2,1)}, u32[]{:S(2)}) copy-start(bf16[3,2,512,256]{3,2,1,0:T(8,128)(2,1)} %copy-done.3) | copy-start | bytes 4718596
  785.0 363.1 %all-to-all-start.6 = ((bf16[8,2,64,256]{3,2,1,0:T(8,128)(2,1)}), bf16[8,2,64,256]{3,2,1,0:T(8,128)(2,1)S(1)}, u32[]{:S(2)}, u32[]{:S(2)}) async-start(bf16[8,2,64,256]{3,2,1,0:T(8,128)(2,1)} %bitcast.319), calls=%async_computation.10 | async-start | bytes 1048576 | tf_op jit(solution)/shard_map/all_to_all | solution.py:614
  1146.9 2.6 copy-start.1
  (11 other events, 20.3 us)
Sparse Core Ops, SparseCore 0:
  33.0 22.9 all-gather.5
  275.6 25.4 all-gather.7
  313.0 31.4 reduce-scatter.17
  349.7 22.5 all-gather.9
  388.6 31.4 reduce-scatter.19
  425.2 22.5 all-gather.11
  459.9 31.4 reduce-scatter.21
  497.2 22.5 all-gather.13
  536.8 31.4 reduce-scatter.23
  571.6 68.1 reduce-scatter.41
  643.8 66.2 reduce-scatter.35
  713.9 67.2 reduce-scatter.33
  785.1 71.2 reduce-scatter.31
  860.3 66.6 reduce-scatter.29
  930.0 19.1 reduce-scatter.37
  952.4 61.8 reduce-scatter.27
  1017.9 60.8 reduce-scatter.25
  1082.1 63.6 reduce-scatter.39

commit v3 on v2

--- a/solution.py
+++ b/solution.py
@@ -23,71 +23,6 @@
 NN = ((1,), (0,))
 NT = ((1,), (1,))
 TN = ((0,), (0,))
-
-
-def head_probs(query, key_rows, same_seq):
-    scores = jnp.where(same_seq, dot(query, key_rows, NT) * (1.0 / math.sqrt(HD)), NEG)
-    top = jnp.max(scores, axis=1, keepdims=True)
-    weighted = jnp.exp(scores - top)
-    return weighted * (1.0 / jnp.sum(weighted, axis=1, keepdims=True))
-
-
-def attend_kernel(qkv_ref, seg_col, seg_row, out_ref):
-    same_seq = seg_col[0] == seg_row[0]
-    for head in range(qkv_ref.shape[3] // HD):
-        cols = slice(head * HD, (head + 1) * HD)
-        probs = head_probs(qkv_ref[0, 0, :, cols], qkv_ref[1, 0, :, cols], same_seq)
-        out_ref[0, :, cols] = dot(probs.astype(BF), qkv_ref[2, 0, :, cols], NN).astype(BF)
-
-
-def attend_back_kernel(qkv_ref, grad_ref, seg_col, seg_row, out_ref):
-    same_seq = seg_col[0] == seg_row[0]
-    scale = 1.0 / math.sqrt(HD)
-    for head in range(qkv_ref.shape[3] // HD):
-        cols = slice(head * HD, (head + 1) * HD)
-        query, key_rows, value_rows = (qkv_ref[c, 0, :, cols] for c in range(3))
-        grad = grad_ref[0, :, cols]
-        probs = head_probs(query, key_rows, same_seq)
-        grad_probs = dot(grad, value_rows, NT)
-        delta = jnp.sum(probs * grad_probs, axis=1, keepdims=True)
-        grad_scores = (probs * (grad_probs - delta)).astype(BF)
-        out_ref[0, 0, :, cols] = (dot(grad_scores, key_rows, NN) * scale).astype(BF)
-        out_ref[1, 0, :, cols] = (dot(grad_scores, query, TN) * scale).astype(BF)
-        out_ref[2, 0, :, cols] = dot(probs.astype(BF), grad, TN).astype(BF)
-
-
-def attend(qkv, seg_col, seg_row):
-    _, packs, rows, width = qkv.shape
-    return pl.pallas_call(
-        attend_kernel,
-        grid=(packs,),
-        in_specs=[
-            pl.BlockSpec((3, 1, rows, width), lambda k: (0, k, 0, 0)),
-            pl.BlockSpec((1, rows, 1), lambda k: (k, 0, 0)),
-            pl.BlockSpec((1, 1, rows), lambda k: (k, 0, 0)),
-        ],
-        out_specs=pl.BlockSpec((1, rows, width), lambda k: (k, 0, 0)),
-        out_shape=jax.ShapeDtypeStruct((packs, rows, width), BF),
-        compiler_params=pltpu.CompilerParams(vmem_limit_bytes=32 << 20),
-    )(qkv, seg_col, seg_row)
-
-
-def attend_back(qkv, grad, seg_col, seg_row):
-    _, packs, rows, width = qkv.shape
-    return pl.pallas_call(
-        attend_back_kernel,
-        grid=(packs,),
-        in_specs=[
-            pl.BlockSpec((3, 1, rows, width), lambda k: (0, k, 0, 0)),
-            pl.BlockSpec((1, rows, width), lambda k: (k, 0, 0)),
-            pl.BlockSpec((1, rows, 1), lambda k: (k, 0, 0)),
-            pl.BlockSpec((1, 1, rows), lambda k: (k, 0, 0)),
-        ],
-        out_specs=pl.BlockSpec((3, 1, rows, width), lambda k: (0, k, 0, 0)),
-        out_shape=jax.ShapeDtypeStruct((3, packs, rows, width), BF),
-        compiler_params=pltpu.CompilerParams(vmem_limit_bytes=32 << 20),
-    )(qkv, grad, seg_col, seg_row)
-
 
 MESH = pl.DeviceIdType.MESH
 LOG2E = 1.4426950408889634
@@ -499,64 +434,414 @@
     )(act, shard, vec, head_bias, up_bias, seg_col, seg_row)
 
 
-def gather_rows(values):
-    return lax.all_gather(values.astype(BF), "tp", axis=1, tiled=True)
-
-
-def scatter_rows(values):
-    return lax.psum_scatter(
-        values.astype(BF), "tp", scatter_dimension=1, tiled=True
-    ).astype(F32)
-
-
-def norm_forward(residual, gain, offset):
-    mean = jnp.mean(residual, axis=-1, keepdims=True)
-    centred = residual - mean
-    scale = lax.rsqrt(jnp.mean(centred * centred, axis=-1, keepdims=True) + EPS)
-    normed = centred * scale
-    return normed * gain + offset, normed, scale
-
-
-def norm_backward(upstream, normed, scale, gain):
-    scaled = upstream * gain
-    first = jnp.mean(scaled, axis=-1, keepdims=True)
-    second = jnp.mean(scaled * normed, axis=-1, keepdims=True)
-    grad = scale * (scaled - first - normed * second)
-    return grad, jnp.sum(upstream * normed, axis=(0, 1)), jnp.sum(upstream, axis=(0, 1))
-
-
-def gelu(values):
-    return jax.nn.gelu(values, approximate=False)
+class GradScatter:
+    def __init__(self, lk, grad, from_x, from_z, x_send, x_recv, z_send, z_recv):
+        self.lk, self.grad, self.from_x, self.from_z = lk, grad, from_x, from_z
+        self.x_send, self.x_recv, self.z_send, self.z_recv = x_send, x_recv, z_send, z_recv
+        self.rows = from_x.shape[2]
+
+    def block(self, chunk, step, c):
+        f = lax.rem(self.lk.f + step, self.lk.fs)
+        first = pl.multiple_of((f * self.lk.cx + c) * self.rows, self.rows)
+        return self.grad.at[chunk, pl.ds(first, self.rows)]
+
+    def x_copy(self, chunk, step):
+        return remote(
+            self.block(chunk, step, 1 - self.lk.c), self.from_x.at[chunk, step],
+            self.x_send.at[chunk, step], self.x_recv.at[chunk, step], self.lk.across,
+        )
+
+    def z_copy(self, chunk, step):
+        slot = self.lk.fs - step
+        return remote(
+            self.block(chunk, step, self.lk.c), self.from_z.at[chunk, slot - 1],
+            self.z_send.at[chunk, step], self.z_recv.at[chunk, slot], self.lk.away(step),
+        )
+
+    def each(self, first, work):
+        def body(step, carry):
+            work(step)
+            return carry
+
+        lax.fori_loop(first, self.lk.fs, body, 0)
+
+    def first(self, chunk):
+        self.each(1, lambda step: self.x_copy(chunk, step).start())
+        self.x_copy(chunk, 0).start()
+
+    def second(self, chunk):
+        def work(step):
+            self.x_copy(chunk, step).wait_recv()
+            own = self.block(chunk, step, self.lk.c)
+            own[...] = (own[...].astype(F32) + self.from_x[chunk, step].astype(F32)).astype(BF)
+            self.z_copy(chunk, step).start()
+
+        self.each(1, work)
+
+    def last(self, chunk, out):
+        self.x_copy(chunk, 0).wait_recv()
+        out[...] = self.block(chunk, 0, self.lk.c)[...].astype(F32) + self.from_x[chunk, 0].astype(F32)
+
+        def work(step):
+            self.z_copy(chunk, self.lk.fs - step).wait_recv()
+            out[...] = out[...] + self.from_z[chunk, step - 1].astype(F32)
+
+        self.each(1, work)
+
+    def drain(self, chunk):
+        self.each(0, lambda step: self.x_copy(chunk, step).wait_send())
+        self.each(1, lambda step: self.z_copy(chunk, step).wait_send())
+
+
+def backward_kernel(
+    up_in, act_first, act_more, w_in, qkv_in, att_in, nrm_in, std_in, hid_in, glu_in, dglu_in,
+    lse_in, vec, seg_col, seg_row,
+    out_qkv, out_out, out_up, out_down, out_u, out_vec, out_head, out_bias,
+    w, qkv, att, nrm, std, hid, glu, dglu, lse, up, gtwo, gl, gm, gup, gqkv, gatt,
+    part, from_sib, to_peer, from_peer, grad, from_x, from_z, gsum, low,
+    in_sem, out_sem, rs_send, rs_recv, ag_send, ag_recv, x_send, x_recv, z_send, z_recv,
+):
+    packs, rows, width = hid.shape
+    layers = vec.shape[0]
+    mine = rows // 4
+    heads_width = att.shape[2]
+    lk = Links()
+    sources = dict(
+        nrm1=lambda layer: (nrm_in.at[layer, 1], nrm.at[1]),
+        std1=lambda layer: (std_in.at[layer, 1], std.at[1]),
+        nrm0=lambda layer: (nrm_in.at[layer, 0], nrm.at[0]),
+        std0=lambda layer: (std_in.at[layer, 0], std.at[0]),
+        w2=lambda layer: (w_in.at[3 * layer + 2], w.at[2]),
+        dglu=lambda layer: (dglu_in.at[layer], dglu),
+        w1=lambda layer: (w_in.at[3 * layer + 1], w.at[1]),
+        glu=lambda layer: (glu_in.at[layer], glu),
+        hid=lambda layer: (hid_in.at[layer], hid),
+        w0=lambda layer: (w_in.at[3 * layer], w.at[0]),
+        qkv=lambda layer: (qkv_in.at[layer], qkv),
+        lse=lambda layer: (lse_in.at[layer], lse),
+        att=lambda layer: (att_in.at[layer], att),
+        act=lambda layer: (act_more.at[layer - 1] if layer else act_first, hid),
+    )
+    order = {name: index for index, name in enumerate(sources)}
+
+    def fetch(name, layer):
+        if layer >= 0:
+            src, dst = sources[name](layer)
+            pltpu.make_async_copy(src, dst, in_sem.at[order[name]]).start()
+
+    def ready(name, layer):
+        src, dst = sources[name](layer)
+        pltpu.make_async_copy(src, dst, in_sem.at[order[name]]).wait()
+
+    load = pltpu.make_async_copy(up_in, up, in_sem.at[len(order)])
+    load.start()
+    for name in sources:
+        if name != "act":
+            fetch(name, layers - 1)
+    lk.barrier()
+    rs = RowSum(lk, part, from_sib, to_peer, from_peer, rs_send, rs_recv)
+    ag = RowGather(lk, mine, ag_send, ag_recv)
+    gs = GradScatter(lk, grad, from_x, from_z, x_send, x_recv, z_send, z_recv)
+    my_rows = pl.ds(pl.multiple_of(lk.t * mine, mine), mine)
+    pending = []
+    held = {}
+    used = []
+
+    def save(src, dst):
+        copy = pltpu.make_async_copy(src, dst, out_sem.at[len(used)])
+        copy.start()
+        used.append(1)
+        pending.append(copy)
+
+    out_vec[...] = jnp.zeros_like(out_vec)
+    out_head[...] = jnp.zeros_like(out_head)
+    out_bias[...] = jnp.zeros_like(out_bias)
+
+    def norm_back(layer, which, k, upstream):
+        normed = nrm[which, k]
+        scale = std[which, k][:, 0:1]
+        out_vec[layer, 2 + which : 3 + which] += jnp.sum(upstream * normed, axis=0, keepdims=True)
+        out_vec[layer, 4 + which : 5 + which] += jnp.sum(upstream, axis=0, keepdims=True)
+        scaled = upstream * vec[layer, 2 + which : 3 + which]
+        first = jnp.mean(scaled, axis=1, keepdims=True)
+        second = jnp.mean(scaled * normed, axis=1, keepdims=True)
+        result = scale * (scaled - first - normed * second)
+        out_vec[layer, which : which + 1] += jnp.sum(result, axis=0, keepdims=True)
+        return result
+
+    def norm_two(layer, k):
+        result = norm_back(layer, 1, k, up[k])
+        gtwo[k] = result
+        gl[k, my_rows] = result.astype(BF)
+        ag.first(gl.at[k], k)
+
+    def norm_one(layer, k):
+        result = norm_back(layer, 0, k, gtwo[k] + rs.last(k))
+        up[k] = result
+        gm[k, my_rows] = result.astype(BF)
+        ag.first(gm.at[k], k)
+
+    def tiles(work):
+        def body(j, carry):
+            work(pl.ds(pl.multiple_of(j * 256, 256), 256))
+            return carry
+
+        lax.fori_loop(0, width // 256, body, 0)
+
+    def through_down(layer, k):
+        def tile(cols):
+            grad_gelu = dot(gl[k], w[2, :, cols], NN).astype(BF).astype(F32)
+            result = (grad_gelu * dglu[k, :, cols].astype(F32)).astype(BF)
+            gup[k, :, cols] = result
+            out_bias[layer, :, cols] += jnp.sum(result.astype(F32), axis=0, keepdims=True)
+
+        tiles(tile)
+
+    def through_up(layer, k):
+        tiles(lambda cols: store_part(part, k, cols, dot(gup[k], w[1, cols, :], NT), mine))
+        rs.first(k)
+
+    def through_out(k):
+        gatt[k] = dot(gm[k], w[0, :, 3 * heads_width :], NN).astype(BF)
+
+    def attention(layer, k):
+        same_seq = seg_col[k] == seg_row[k]
+        scale = 1.0 / math.sqrt(HD)
+        for head in range(heads_width // HD):
+            cols = [slice(j * heads_width + head * HD, j * heads_width + (head + 1) * HD) for j in range(3)]
+            query, keys, values = (qkv[k, :, c] for c in cols)
+            grads = gatt[k, :, cols[0]]
+            probs = jnp.exp2(masked_scores(query, keys, same_seq) - lse[k, :, head : head + 1])
+            grad_probs = dot(grads, values, NT)
+            delta = jnp.sum(probs * grad_probs, axis=1, keepdims=True)
+            grad_scores = (probs * (grad_probs - delta)).astype(BF)
+            gqkv[k, :, cols[0]] = (dot(grad_scores, keys, NN) * scale).astype(BF)
+            gqkv[k, :, cols[1]] = (dot(grad_scores, query, TN) * scale).astype(BF)
+            gqkv[k, :, cols[2]] = dot(probs.astype(BF), grads, TN).astype(BF)
+        for j in range(2):
+            cols = slice(2 * j * heads_width, (2 * j + 1) * heads_width)
+            out_head[layer, j : j + 1] += jnp.sum(
+                gqkv[k, :, cols].astype(F32), axis=0, keepdims=True
+            )
+
+    def through_qkv(k):
+        tiles(
+            lambda cols: store_part(
+                part, k, cols, dot(gqkv[k], w[0, cols, : 3 * heads_width], NT), mine
+            )
+        )
+        rs.first(k)
+
+    def product(left, right, cols, right_cols=slice(None)):
+        total = dot(left[0, :, cols], right[0, :, right_cols], TN)
+        for k in range(1, packs):
+            total = total + dot(left[k, :, cols], right[k, :, right_cols], TN)
+        return total.astype(BF)
+
+    def down_grad(layer):
+        def tile(cols):
+            grad[3 * layer + 2, cols, :] = product(gl, glu, cols)
+
+        tiles(tile)
+        gs.first(3 * layer + 2)
+
+    def up_grad(layer):
+        def tile(cols):
+            grad[3 * layer + 1, cols, :] = product(hid, gup, cols)
+
+        tiles(tile)
+        gs.first(3 * layer + 1)
+
+    def first_grad(layer):
+        def tile(cols):
+            grad[3 * layer, cols, : 3 * heads_width] = product(hid, gqkv, cols)
+            grad[3 * layer, cols, 3 * heads_width :] = product(gm, att, cols)
+
+        tiles(tile)
+        gs.first(3 * layer)
+
+    def emit(layer, which):
+        chunk = 3 * layer + which
+        out = gsum.at[which]
+        while held.get(which):
+            held[which].pop().wait()
+        gs.last(chunk, out)
+        held[which] = []
+        saved = len(pending)
+        if which == 2:
+            save(out, out_down.at[layer])
+        elif which == 1:
+            save(out, out_up.at[layer])
+        else:
+            for c in range(3):
+                save(out.at[:, c * heads_width : (c + 1) * heads_width], out_qkv.at[layer, c])
+            save(out.at[:, 3 * heads_width :], out_out.at[layer])
+        held[which] = [pending.pop() for _ in range(len(pending) - saved)]
+
+    load.wait()
+    top = layers - 1
+    ready("nrm1", top)
+    ready("std1", top)
+    for k in range(packs):
+        norm_two(top, k)
+    fetch("nrm1", top - 1)
+    fetch("std1", top - 1)
+    for layer in reversed(range(layers)):
+        ag.second(gl.at[0], 0)
+        if layer < top:
+            ready("act", layer + 1)
+            first_grad(layer + 1)
+            fetch("att", layer)
+            fetch("hid", layer)
+        ready("w2", layer)
+        ready("dglu", layer)
+        ag.last(gl.at[0], 0)
+        through_down(layer, 0)
+        ag.second(gl.at[1], 1)
+        ready("w1", layer)
+        through_up(layer, 0)
+        ag.last(gl.at[1], 1)
+        through_down(layer, 1)
+        fetch("w2", layer - 1)
+        fetch("dglu", layer - 1)
+        rs.second(0)
+        through_up(layer, 1)
+        fetch("w1", layer - 1)
+        ready("glu", layer)
+        down_grad(layer)
+        fetch("glu", layer - 1)
+        rs.second(1)
+        ready("nrm0", layer)
+        ready("std0", layer)
+        norm_one(layer, 0)
+        if layer < top:
+            gs.second(3 * (layer + 1) + 1)
+        ready("hid", layer)
+        up_grad(layer)
+        fetch("act", layer)
+        ag.second(gm.at[0], 0)
+        norm_one(layer, 1)
+        fetch("nrm0", layer - 1)
+        fetch("std0", layer - 1)
+        ready("w0", layer)
+        ready("qkv", layer)
+        ready("lse", layer)
+        ag.last(gm.at[0], 0)
+        through_out(0)
+        attention(layer, 0)
+        ag.second(gm.at[1], 1)
+        through_qkv(0)
+        if layer < top:
+            gs.second(3 * (layer + 1))
+        else:
+            gs.second(3 * layer + 2)
+        ag.last(gm.at[1], 1)
+        through_out(1)
+        rs.second(0)
+        attention(layer, 1)
+        fetch("qkv", layer - 1)
+        fetch("lse", layer - 1)
+        through_qkv(1)
+        fetch("w0", layer - 1)
+        ready("att", layer)
+        if layer == 0:
+            ready("act", layer)
+            first_grad(0)
+        for k in range(packs):
+            if k:
+                rs.second(k)
+            up[k] = rs.last(k) + up[k]
+            if layer:
+                if k == 0:
+                    ready("nrm1", layer - 1)
+                    ready("std1", layer - 1)
+                norm_two(layer - 1, k)
+            else:
+                low[k] = up[k].astype(BF)
+                save(low.at[k], out_u.at[k])
+        if layer:
+            fetch("nrm1", layer - 2)
+            fetch("std1", layer - 2)
+        if layer < top:
+            for which in (2, 1, 0):
+                emit(layer + 1, which)
+    gs.second(2)
+    emit(0, 2)
+    gs.second(1)
+    emit(0, 1)
+    gs.second(0)
+    emit(0, 0)
+    for chunk in range(3 * layers):
+        gs.drain(chunk)
+    for copy in pending + sum(held.values(), []):
+        copy.wait()
+
+
+def backward(upstream, act, saved, vec, seg_col, seg_row):
+    full_w, o_act, o_qkv, o_att, o_nrm, o_std, o_hid, o_glu, o_dglu, o_lse = saved
+    packs, rows, width = act.shape
+    layers, mine = vec.shape[0], rows // 4
+    chunks = 3 * layers
+    heads = o_att.shape[3]
+    fs, cx = lax.axis_size("fsdp"), lax.axis_size("ctx")
+    shard = width // (fs * cx)
+    outs = [
+        jax.ShapeDtypeStruct((layers, 3, shard, heads), F32),
+        jax.ShapeDtypeStruct((layers, shard, heads), F32),
+        jax.ShapeDtypeStruct((layers, shard, width), F32),
+        jax.ShapeDtypeStruct((layers, shard, width), F32),
+        jax.ShapeDtypeStruct((packs, mine, width), BF),
+        jax.ShapeDtypeStruct((layers, 6, width), F32),
+        jax.ShapeDtypeStruct((layers, 2, heads), F32),
+        jax.ShapeDtypeStruct((layers, 1, width), F32),
+    ]
+    dma = pltpu.SemaphoreType.DMA
+    whole = pl.BlockSpec(memory_space=pl.ANY)
+    vmem = pl.BlockSpec(memory_space=pltpu.VMEM)
+    full = pltpu.VMEM((packs, rows, width), BF)
+    rowed = pltpu.VMEM((packs, mine, width), F32)
+    return pl.pallas_call(
+        backward_kernel,
+        in_specs=[whole] * 12 + [vmem] * 3,
+        out_specs=[whole] * 5 + [vmem] * 3,
+        out_shape=outs,
+        scratch_shapes=[
+            pltpu.VMEM((3, width, width), BF),
+            pltpu.VMEM((packs, rows, 3 * heads), BF),
+            pltpu.VMEM((packs, rows, heads), BF),
+            pltpu.VMEM((2, packs, mine, width), F32),
+            pltpu.VMEM((2, packs, mine, 128), F32),
+            full, full, full,
+            pltpu.VMEM((packs, rows, 128), F32),
+            rowed, rowed,
+            full, full, full,
+            pltpu.VMEM((packs, rows, 3 * heads), BF),
+            pltpu.VMEM((packs, rows, heads), BF),
+            pltpu.VMEM((packs, 2, 2, mine, width), BF),
+            pltpu.VMEM((packs, 2, mine, width), BF),
+            pltpu.VMEM((packs, mine, width), BF),
+            pltpu.VMEM((packs, mine, width), BF),
+            pltpu.VMEM((chunks, width, width), BF),
+            pltpu.VMEM((chunks, fs, shard, width), BF),
+            pltpu.VMEM((chunks, fs - 1, shard, width), BF),
+            pltpu.VMEM((3, shard, width), F32),
+            pltpu.VMEM((packs, mine, width), BF),
+            dma((15,)), dma((packs + 6 * layers,)),
+            dma((packs, 2)), dma((packs, 2)), dma((packs, 3)), dma((packs, 3)),
+            dma((chunks, fs)), dma((chunks, fs)), dma((chunks, fs)), dma((chunks, fs)),
+        ],
+        compiler_params=pltpu.CompilerParams(
+            collective_id=1, has_side_effects=True, vmem_limit_bytes=60 << 20
+        ),
+        name="backward",
+    )(
+        upstream, act, o_act, full_w, o_qkv, o_att, o_nrm, o_std, o_hid, o_glu, o_dglu, o_lse,
+        vec, seg_col, seg_row,
+    )
 
 
 def mm(spec, left, right):
     return jnp.einsum(spec, left, right, preferred_element_type=F32)
-
-
-def layer_backward(upstream, saved, weights, vectors, seg_col, seg_row):
-    w_qkv, w_out, w_up, w_down = weights
-    head_bias, full_bias, gain, offset, up_bias = vectors
-    act, qkv, attended, normed1, scale1, hidden_full, upper, gelu_low, normed2, scale2 = saved
-    grad2, gain2, offset2 = norm_backward(upstream, normed2, scale2, gain[1])
-    grad_lowered = gather_rows(grad2)
-    g_down = mm("ktd,ktf->df", grad_lowered, gelu_low).astype(BF)
-    grad_gelu = mm("ktd,df->ktf", grad_lowered, w_down).astype(BF)
-    grad_upper = (grad_gelu.astype(F32) * upper.astype(F32)).astype(BF)
-    up_grad = jnp.sum(grad_upper, axis=(0, 1), dtype=F32)
-    g_up = mm("ktd,ktf->df", hidden_full, grad_upper).astype(BF)
-    grad_hidden = scatter_rows(mm("ktf,df->ktd", grad_upper, w_up)) + grad2
-    grad1, gain1, offset1 = norm_backward(grad_hidden, normed1, scale1, gain[0])
-    grad_mixed = gather_rows(grad1)
-    g_out = mm("ktd,kth->dh", grad_mixed, attended).astype(BF)
-    grad_attended = mm("ktd,dh->kth", grad_mixed, w_out).astype(BF)
-    grad_qkv = attend_back(qkv, grad_attended, seg_col, seg_row)
-    g_qkv = mm("ktd,ckth->cdh", act, grad_qkv).astype(BF)
-    grad_act = scatter_rows(mm("ckth,cdh->ktd", grad_qkv, w_qkv))
-    full_part = jnp.stack(
-        [jnp.sum(grad1, axis=(0, 1)), jnp.sum(grad2, axis=(0, 1)), gain1, gain2, offset1, offset2]
-    )
-    head_part = jnp.sum(grad_qkv, axis=(1, 2), dtype=F32)[0::2]
-    return grad_act + grad1, (g_qkv, g_out, g_up, g_down), (full_part, head_part, up_grad)
 
 
 def local(
@@ -623,49 +908,21 @@
     seg = lax.dynamic_slice_in_dim(segment_ids, my_first, mine)
     seg_col, seg_row = seg[:, :, None], seg[:, None, :]
 
-    full_w, o_act, o_qkv, o_att, o_nrm, o_std, o_hid, o_glu, o_dglu, o_lse, resid = forward(
+    *saved, resid = forward(
         act, shard, vec, biases[:, :2], up_bias[:, None], seg_col, seg_row
     )
-    weights = []
-    saved = []
-    hw = o_att.shape[3]
-    for layer in range(layers):
-        first = full_w[3 * layer]
-        weights.append(
-            (
-                jnp.stack([first[:, c * hw : (c + 1) * hw] for c in range(3)]),
-                first[:, 3 * hw :], full_w[3 * layer + 1], full_w[3 * layer + 2],
-            )
-        )
-        saved.append(
-            (
-                act if layer == 0 else o_act[layer - 1],
-                jnp.stack([o_qkv[layer, :, :, c * hw : (c + 1) * hw] for c in range(3)]),
-                o_att[layer], o_nrm[layer, 0], o_std[layer, 0, :, :, :1], o_hid[layer],
-                o_dglu[layer], o_glu[layer], o_nrm[layer, 1], o_std[layer, 1, :, :, :1],
-            )
-        )
     outputs = from_packs(resid)
-    shards = [None] * layers
-    parts = [None] * layers
-    for layer in reversed(range(layers)):
-        upstream, grads, parts[layer] = layer_backward(
-            upstream, saved[layer], weights[layer], vectors[layer], seg_col, seg_row
-        )
-        shards[layer] = (
-            lax.psum_scatter(grads[0], GRP, scatter_dimension=1, tiled=True),
-            lax.psum_scatter(grads[1], GRP, scatter_dimension=0, tiled=True),
-            lax.psum_scatter(grads[2], GRP, scatter_dimension=0, tiled=True),
-            lax.psum_scatter(grads[3], GRP, scatter_dimension=0, tiled=True),
-        )
+    g_qkv, g_out, g_up, g_down, upstream, full_part, head_part, up_part = backward(
+        upstream, act, saved, vec, seg_col, seg_row
+    )
     input_grad = from_packs(upstream)
-    full_part, head_part, up_part = (jnp.stack([p[i] for p in parts]) for i in range(3))
+    up_part = up_part[:, 0]
     full_part = lax.psum_scatter(full_part, "tp", scatter_dimension=2, tiled=True)
     full_part, head_part, up_part = lax.psum((full_part, head_part, up_part), GRP)
     return (
         outputs,
         input_grad,
-        *(jnp.stack([s[i] for s in shards]).astype(F32) for i in range(4)),
+        g_qkv, g_out, g_up, g_down,
         jnp.concatenate([head_part, full_part[:, 0:2]], axis=1),
         full_part[:, 2:4],
         full_part[:, 4:6],

time: 1170 us -> 613 us (0.52)
  waiting for transfers between devices: 642 us -> 68.4 us
  Pallas kernels: 218 us -> 411 us
  matrix products: 80.9 us -> 8.36 us
  blocking collectives: 82.7 us -> 45.8 us
  local copies, waits for them, and re-layouts: 54 us -> 17.9 us
  other arithmetic: 39.3 us -> 4.57 us
    reduce_scatter x10 -> x0, waiting for transfers between devices: 459 us -> none  [the longest x2 137 us: local(): lax.psum_scatter(grads[2], GRP, scatter_dimension=0, tiled=True)]
    pallas_call x2 -> x1, Pallas kernels: 20.3 us -> 214 us  [backward(): pl.pallas_call(backward_kernel, in_specs=[whole] * 12 + [vmem] * 3, out_s...]
    all_gather x4 -> x0, waiting for transfers between devices: 78.2 us -> none  [gather_rows(): return lax.all_gather(values.astype(BF), 'tp', axis=1, tiled=True)]
    dot_general x24 -> x8, matrix products: 80.9 us -> 8.36 us  [mm(): return jnp.einsum(spec, left, right, preferred_element_type=F32)]
    unnamed x20 -> x2, waiting for transfers between devices: 65.6 us -> 0.74 us
    all_to_all x2 -> x0, blocking collectives: 37.4 us -> none  [the longest x1 25.9 us: from_packs(): slots = lax.all_to_all(slots, GRP, split_axis=0, concat_axis=0, tiled=True)]
    unnamed x83 -> x43, local copies, waits for them, and re-layouts: 24.6 us -> 3.62 us
    all_to_all x1 -> x2, waiting for transfers between devices: 0.01 us -> 14.7 us  [from_packs(): lax.all_to_all(values.astype(BF), 'tp', split_axis=2, concat_axis=1, tile...]
  transfers between devices with their start and end apart: 23 -> 9, of which waited for: 18 -> 7; matrix products, arithmetic and copies ran while one was open for 9% -> 3% of each run, Pallas kernels for 0% -> 0%
where the time goes in v3:
time: 613 us; the launch traced here: 604 us
  Pallas kernels  411 us (67%)
  waiting for transfers between devices  68.4 us (11%)
  blocking collectives  45.8 us (7%)
  starting transfers between devices  33.1 us (5%)
  local copies, waits for them, and re-layouts  17.9 us (3%)
  between operations  14.6 us (2%)
  matrix products  8.36 us (1%)
    pallas_call x1, Pallas kernels, backward(): pl.pallas_call(backward_kernel, in_specs=[whole] * 12 + [vmem] * 3, out_s...  214 us
    pallas_call x1, Pallas kernels, forward(): pl.pallas_call(forward_kernel, in_specs=[whole, whole, vmem, vmem, vmem,...  197 us
    psum x1, blocking collectives, local(): lax.psum((full_part, head_part, up_part), GRP)  35 us
    reduce_scatter x1, waiting for transfers between devices, local(): lax.psum_scatter(full_part, 'tp', scatter_dimension=2, tiled=True)  21.9 us
    all_to_all x2, waiting for transfers between devices, from_packs(): lax.all_to_all(values.astype(BF), 'tp', split_axis=2, concat_axis=1, tile...  14.7 us
    all_to_all x2, waiting for transfers between devices, to_packs(): slots = lax.all_to_all(slots, GRP, split_axis=0, concat_axis=0, tiled=True)  12.3 us
  transfers between devices with their start and end apart: 9, of which 7 were waited for; matrix products, arithmetic and copies ran while one was open for 3% of the time, Pallas kernels for 0%

profile of v3, /device:TPU:8, one launch (start us, length us, event | category | flops | bytes accessed | tf_op | source)
XLA Modules:
  0.0 603.6 jit_solution(11111962761560718710)
XLA Ops:
  7.2 0.7 add_select_fusion
  8.4 0.7 multiply_add_fusion.1
  9.1 1.8 convolution_convert_fusion.1
  10.9 0.8 copy.78
  11.8 6.3 %all-to-all-start = ((bf16[8,2,64,256]{3,2,1,0:T(8,128)(2,1)}), bf16[8,2,64,256]{3,2,1,0:T(8,128)(2,1)S(1)}, u32[]{:S(2)}, u32[]{:S(2)}) async-start(bf16[8,2,64,256]{3,2,1,0:T(8,128)(2,1)} %bitcast.2), calls=%async_computation | async-start | bytes 1048576 | tf_op jit(solution)/shard_map/all_to_all | solution.py:891
  18.0 4.7 all_gather.9
  22.7 0.7 convert_reduce_fusion
  23.4 7.8 %all-to-all-done = bf16[8,2,64,256]{3,2,1,0:T(8,128)(2,1)S(1)} async-done(((bf16[8,2,64,256]{3,2,1,0:T(8,128)(2,1)}), bf16[8,2,64,256]{3,2,1,0:T(8,128)(2,1)S(1)}, u32[]{:S(2)}, u32[]{:S(2)}) %all-to-all-start) | async-done | bytes 524320 | tf_op jit(solution)/shard_map/all_to_all | solution.py:891
  31.3 1.6 fusion.4
  32.9 0.6 convolution_convert_fusion
  33.5 0.8 copy.90
  34.4 4.9 all-to-all-start.3
  39.3 0.6 broadcast_in_dim.8.seg_row
  39.9 0.6 broadcast_in_dim.6.up_bias
  40.5 1.0 copy.84.seg_col
  41.5 0.6 fusion.21
  42.1 6.0 %all_gather.11.vec = f32[2,6,1024]{2,1,0:T(8,128)} all-gather(f32[2,6,256]{2,1,0:T(8,128)S(1)} %pad_maximum_fusion.1), channel_id=1, replica_groups=mesh['fsdp'=4,'ctx'=2,'tp'=4] {'tp'}, dimensions={2}, use_global_device_ids=true | all-gather | bytes 61440 | tf_op jit(solution)/shard_map/all_gather | solution.py:867
  48.2 4.5 all-to-all-done.3
  52.8 0.8 fusion.6
  53.5 1.3 copy.93
  54.9 3.8 all-to-all-start.4
  58.7 1.3 pad_maximum_fusion
  60.0 7.4 %all-to-all-done.4 = bf16[2,512,256]{2,0,1:T(2,128)(2,1)S(1)} async-done(((bf16[2,512,256]{2,0,1:T(2,128)(2,1)}), bf16[2,512,256]{2,0,1:T(2,128)(2,1)S(1)}, u32[]{:S(2)}, u32[]{:S(2)}) %all-to-all-start.4) | async-done | bytes 524320 | tf_op jit(solution)/shard_map/all_to_all | solution.py:905
  67.9 1.5 reshape.96.up_in
  69.4 197.4 %forward.1 = (bf16[6,1024,1024]{2,1,0:T(8,128)(2,1)}, bf16[1,2,512,1024]{3,2,1,0:T(8,128)(2,1)}, bf16[2,2,512,768]{3,2,1,0:T(8,128)(2,1)}, bf16[2,2,512,256]{3,2...) custom-call(bf16[2,512,1024]{2,1,0:T(8,128)(2,1)} %all-gather.2.clon, ...), custom_call_target="tpu_custom_call" | custom-call | tf_op jit(solution)/shard_map/forward/pallas_call | solution.py:413
  266.8 213.5 %backward.1 = (f32[2,3,128,256]{3,2,1,0:T(8,128)}, f32[2,128,256]{2,1,0:T(8,128)}, f32[2,128,1024]{2,1,0:T(8,128)}, f32[2,128,1024]{2,1,0:T(8,128)}, bf16[2,128,...) custom-call(f32[2,128,1024]{2,1,0:T(8,128)} %reshape.96.up_in, ...), custom_call_target="tpu_custom_call" | custom-call | tf_op jit(solution)/shard_map/backward/pallas_call | solution.py:803
  480.3 2.1 copy.96
  482.4 3.5 all-to-all-start.5
  486.0 1.1 copy.85
  487.1 7.6 %all-to-all-done.5 = bf16[2,128,1024]{1,0,2:T(2,128)(2,1)S(1)} async-done(((bf16[2,128,1024]{1,0,2:T(2,128)(2,1)}), bf16[2,128,1024]{1,0,2:T(2,128)(2,1)S(1)}, u32[]{:S(2)}, u32[]{:S(2)}) %all-to-all-start.5) | async-done | bytes 524320 | tf_op jit(solution)/shard_map/all_to_all | solution.py:896
  494.7 3.5 all-to-all-start.1
  499.1 0.8 copy.113
  499.9 7.1 %all-to-all-done.1 = bf16[2,128,1024]{1,0,2:T(2,128)(2,1)S(1)} async-done(((bf16[2,128,1024]{1,0,2:T(2,128)(2,1)}), bf16[2,128,1024]{1,0,2:T(2,128)(2,1)S(1)}, u32[]{:S(2)}, u32[]{:S(2)}) %all-to-all-start.1) | async-done | bytes 524320 | tf_op jit(solution)/shard_map/all_to_all | solution.py:896
  507.0 6.4 %all-to-all-start.6 = ((bf16[8,2,64,256]{3,2,1,0:T(8,128)(2,1)}), bf16[8,2,64,256]{3,2,1,0:T(8,128)(2,1)S(1)}, u32[]{:S(2)}, u32[]{:S(2)}) async-start(bf16[8,2,64,256]{3,2,1,0:T(8,128)(2,1)} %bitcast.63), calls=%async_computation.6 | async-start | bytes 1048576 | tf_op jit(solution)/shard_map/all_to_all | solution.py:899
  514.3 0.8 copy.114
  515.1 11.3 %all-to-all-done.6 = bf16[8,2,64,256]{3,2,1,0:T(8,128)(2,1)S(1)} async-done(((bf16[8,2,64,256]{3,2,1,0:T(8,128)(2,1)}), bf16[8,2,64,256]{3,2,1,0:T(8,128)(2,1)S(1)}, u32[]{:S(2)}, u32[]{:S(2)}) %all-to-all-start.6) | async-done | bytes 524320 | tf_op jit(solution)/shard_map/all_to_all | solution.py:899
  526.4 4.9 all-to-all-start.2
  531.3 0.7 reduce-scatter.2.cloned.1.call-update
  532.1 21.9 %reduce-scatter.2.cloned.1.call-done = f32[2,6,256]{2,1,0:T(8,128)} async-done(((f32[2,6,1024]{2,1,0:T(8,128)}), f32[2,6,256]{2,1,0:T(8,128)}) %reduce-scatter.2.cloned.1.call-update) | async-done | bytes 12304 | tf_op jit(solution)/shard_map/reduce_scatter | solution.py:920
  554.0 35.0 %all-reduce = (f32[2,6,256]{2,1,0:T(8,128)S(1)}, f32[2,2,256]{2,1,0:T(2,128)S(1)}, f32[2,1024]{1,0:T(2,128)}) all-reduce(f32[2,6,256]{2,1,0:T(8,128)} %reduce-scatter.2.cloned.1.call-done, f32[2,2,256]{2,1,0:T(2,128)S(1)} %copy-done.18, f32[2,1024]{1,0:T(2,128)S(1)} %bitcast.85), channel_id=1, replica_groups=mesh['fsdp'=4,'ctx'=2,'tp'=4] {'fsdp','ctx'}, use_global_device_ids=true, to_apply=%region_4.5 | all-reduce | flops 6144 | bytes 49152 | tf_op jit(solution)/shard_map/psum | solution.py:921
  589.1 0.6 fusion.20
  589.7 0.6 pad_maximum_fusion.2
  590.4 1.3 fusion.13
  591.7 1.3 fusion.12
  593.1 0.9 copy.120
  593.9 0.7 copy.121
  594.6 1.0 copy.122
  595.6 1.0 copy.123
  (62 shorter events, 3.0 us)
Async XLA Ops:
  7.2 25.7 %copy-start = (bf16[4,256,256]{2,1,0:T(8,128)(2,1)S(1)}, bf16[4,256,256]{2,1,0:T(8,128)(2,1)}, u32[]{:S(2)}) copy-start(bf16[4,256,256]{2,1,0:T(8,128)(2,1)} %param.16) | copy-start | bytes 1572868
  7.2 10.8 %copy-start.15 = (s32[4,256]{1,0:T(4,128)S(1)}, s32[4,256]{1,0:T(4,128)}, u32[]{:S(2)}) copy-start(s32[4,256]{1,0:T(4,128)} %param.19) | copy-start | bytes 12292
  11.8 19.5 %all-to-all-start = ((bf16[8,2,64,256]{3,2,1,0:T(8,128)(2,1)}), bf16[8,2,64,256]{3,2,1,0:T(8,128)(2,1)S(1)}, u32[]{:S(2)}, u32[]{:S(2)}) async-start(bf16[8,2,64,256]{3,2,1,0:T(8,128)(2,1)} %bitcast.2), calls=%async_computation | async-start | bytes 1048576 | tf_op jit(solution)/shard_map/all_to_all | solution.py:891
  18.0 51.4 %all-gather.2.cloned.1.call-start = ((), (), s32[]{:S(2)}) async-start(), calls=%async_computation.8 | async-start | bytes 2621440 | tf_op jit(solution)/shard_map/all_gather | solution.py:904
  32.8 6.4 %copy-start.12 = (s32[4,512]{1,0:T(4,128)S(1)}, s32[4,512]{1,0:T(4,128)}, u32[]{:S(2)}) copy-start(s32[4,512]{1,0:T(4,128)} %param.17) | copy-start | bytes 24580
  32.8 7.0 %copy-start.11 = (f32[2,1024]{1,0:T(2,128)S(1)}, f32[2,1024]{1,0:T(2,128)}, u32[]{:S(2)}) copy-start(f32[2,1024]{1,0:T(2,128)} %param.27) | copy-start | bytes 24580
  32.8 8.7 %copy-start.13 = (f32[2,4,256]{2,1,0:T(4,128)S(1)}, f32[2,4,256]{2,1,0:T(4,128)}, u32[]{:S(2)}) copy-start(f32[2,4,256]{2,1,0:T(4,128)} %param.24) | copy-start | bytes 24580
  32.9 9.3 %copy-start.16 = (f32[2,2,256]{2,1,0:T(2,128)S(1)}, f32[2,2,256]{2,1,0:T(2,128)}, u32[]{:S(2)}) copy-start(f32[2,2,256]{2,1,0:T(2,128)} %param.26) | copy-start | bytes 12292
  32.9 9.3 %copy-start.17 = (f32[2,2,256]{2,1,0:T(2,128)S(1)}, f32[2,2,256]{2,1,0:T(2,128)}, u32[]{:S(2)}) copy-start(f32[2,2,256]{2,1,0:T(2,128)} %param.25) | copy-start | bytes 12292
  34.4 18.3 %all-to-all-start.3 = ((bf16[8,2,64,256]{3,2,1,0:T(8,128)(2,1)}), bf16[8,2,64,256]{3,2,1,0:T(8,128)(2,1)S(1)}, u32[]{:S(2)}, u32[]{:S(2)}) async-start(bf16[8,2,64,256]{3,2,1,0:T(8,128)(2,1)} %bitcast.20), calls=%async_computation.3 | async-start | bytes 1048576 | tf_op jit(solution)/shard_map/all_to_all | solution.py:891
  52.7 5.9 copy-start.8
  52.7 6.0 copy-start.6
  52.7 6.0 copy-start.7
  52.8 6.0 copy-start.10
  54.9 12.6 %all-to-all-start.4 = ((bf16[2,512,256]{2,0,1:T(2,128)(2,1)}), bf16[2,512,256]{2,0,1:T(2,128)(2,1)S(1)}, u32[]{:S(2)}, u32[]{:S(2)}) async-start(bf16[2,512,256]{2,0,1:T(2,128)(2,1)} %copy.93), calls=%async_computation.4 | async-start | bytes 1048576 | tf_op jit(solution)/shard_map/all_to_all | solution.py:905
  480.3 5.6 copy-start.2
  482.4 12.3 %all-to-all-start.5 = ((bf16[2,128,1024]{1,0,2:T(2,128)(2,1)}), bf16[2,128,1024]{1,0,2:T(2,128)(2,1)S(1)}, u32[]{:S(2)}, u32[]{:S(2)}) async-start(bf16[2,128,1024]{1,0,2:T(2,128)(2,1)} %copy.96), calls=%async_computation.5 | async-start | bytes 1048576 | tf_op jit(solution)/shard_map/all_to_all | solution.py:896
  494.7 12.3 %all-to-all-start.1 = ((bf16[2,128,1024]{1,0,2:T(2,128)(2,1)}), bf16[2,128,1024]{1,0,2:T(2,128)(2,1)S(1)}, u32[]{:S(2)}, u32[]{:S(2)}) async-start(bf16[2,128,1024]{1,0,2:T(2,128)(2,1)} %copy.85), calls=%async_computation.1 | async-start | bytes 1048576 | tf_op jit(solution)/shard_map/all_to_all | solution.py:896
  507.0 19.4 %all-to-all-start.6 = ((bf16[8,2,64,256]{3,2,1,0:T(8,128)(2,1)}), bf16[8,2,64,256]{3,2,1,0:T(8,128)(2,1)S(1)}, u32[]{:S(2)}, u32[]{:S(2)}) async-start(bf16[8,2,64,256]{3,2,1,0:T(8,128)(2,1)} %bitcast.63), calls=%async_computation.6 | async-start | bytes 1048576 | tf_op jit(solution)/shard_map/all_to_all | solution.py:899
  513.8 18.2 %copy-start.14 = (f32[2,1,1024]{2,1,0:T(1,128)S(1)}, f32[2,1,1024]{2,1,0:T(1,128)}, u32[]{:S(2)}) copy-start(f32[2,1,1024]{2,1,0:T(1,128)} %get-tuple-element.47) | copy-start | bytes 24580
  513.8 40.2 %copy-start.18 = (f32[2,2,256]{2,1,0:T(2,128)S(1)}, f32[2,2,256]{2,1,0:T(2,128)}, u32[]{:S(2)}) copy-start(f32[2,2,256]{2,1,0:T(2,128)} %get-tuple-element.45) | copy-start | bytes 12292
  526.4 63.9 %all-to-all-start.2 = ((bf16[8,2,64,256]{3,2,1,0:T(8,128)(2,1)}), bf16[8,2,64,256]{3,2,1,0:T(8,128)(2,1)S(1)}, u32[]{:S(2)}, u32[]{:S(2)}) async-start(bf16[8,2,64,256]{3,2,1,0:T(8,128)(2,1)} %bitcast.64), calls=%async_computation.2 | async-start | bytes 1048576 | tf_op jit(solution)/shard_map/all_to_all | solution.py:899
  531.3 22.7 %reduce-scatter.2.cloned.1.call-start = ((), (), s32[]{:S(2)}) async-start(), calls=%async_computation.9 | async-start | bytes 81920 | tf_op jit(solution)/shard_map/reduce_scatter | solution.py:920
  590.3 2.7 copy-start.5
  590.4 3.5 copy-start.9
  591.7 2.9 copy-start.4
  593.1 2.6 copy-start.3
  593.9 2.7 copy-start.1
Sparse Core Ops, SparseCore 0:
  33.0 22.9 all-gather.1
  534.6 19.4 reduce-scatter.1

commit v4 on v3

--- a/solution.py
+++ b/solution.py
@@ -1,4 +1,3 @@
-import functools
 import math
 
 import jax
@@ -48,22 +47,28 @@
         self.peer_t = lax.rem(self.t + 2, 4)
         self.sib = (self.f, self.c, self.sib_t)
         self.peer = (self.f, self.c, self.peer_t)
+        self.diag_t = 3 - self.t
+        self.diag = (self.f, self.c, self.diag_t)
         self.across = (self.f, 1 - self.c, self.t)
-
-    def away(self, step):
-        return (lax.rem(self.f + step, self.fs), self.c, self.t)
+        self.g = self.f * self.cx + self.c
+
+    def away(self, step, c=None):
+        return (lax.rem(self.f + step, self.fs), self.c if c is None else c, self.t)
 
     def barrier(self):
         sem = pltpu.get_barrier_semaphore()
-        for target in (self.sib, self.peer, self.across):
+        for target in (self.sib, self.peer, self.diag, self.across):
             pl.semaphore_signal(sem, inc=1, device_id=target, device_id_type=MESH)
 
         def greet(step, carry):
-            pl.semaphore_signal(sem, inc=1, device_id=self.away(step), device_id_type=MESH)
+            for c in (self.c, 1 - self.c):
+                pl.semaphore_signal(
+                    sem, inc=1, device_id=self.away(step, c), device_id_type=MESH
+                )
             return carry
 
         lax.fori_loop(1, self.fs, greet, 0)
-        pl.semaphore_wait(sem, 2 + self.fs)
+        pl.semaphore_wait(sem, 2 + 2 * self.fs)
 
 
 def remote(src, dst, send, recv, target):
@@ -110,11 +115,13 @@
 
 
 class RowGather:
-    def __init__(self, lk, rows, send, recv):
+    def __init__(self, lk, rows, send, recv, by_columns=False):
         self.lk, self.rows, self.send, self.recv = lk, rows, send, recv
+        self.by_columns = by_columns
 
     def block(self, ref, index):
-        return ref.at[pl.ds(pl.multiple_of(index * self.rows, self.rows), self.rows)]
+        part = part_of(self.rows, index)
+        return ref.at[:, part] if self.by_columns else ref.at[part]
 
     def copy(self, ref, k, which):
         index = self.lk.t if which < 2 else self.lk.peer_t
@@ -135,6 +142,78 @@
         self.copy(ref, k, 2).wait_recv()
         for which in range(3):
             self.copy(ref, k, which).wait_send()
+
+
+class Exchange:
+    def __init__(self, lk, src, dst, send, recv, in_place=False):
+        self.lk, self.src, self.dst, self.send, self.recv = lk, src, dst, send, recv
+        self.in_place = in_place
+
+    def copy(self, other, step):
+        lk = self.lk
+        c = 1 - lk.c if other else lk.c
+        target = lax.rem(lk.f + step, lk.fs) * lk.cx + c
+        return remote(
+            self.src(target), self.dst(lk.g), self.send.at[other, step],
+            self.recv.at[other, lax.rem(lk.fs - step, lk.fs)], lk.away(step, c),
+        )
+
+    def each(self, work):
+        def body(step, carry):
+            work(1, step)
+            work(0, step)
+            return carry
+
+        work(1, 0)
+        lax.fori_loop(1, self.lk.fs, body, 0)
+
+    def first(self):
+        self.each(lambda other, step: self.copy(other, step).start())
+        if not self.in_place:
+            self.dst(self.lk.g)[...] = self.src(self.lk.g)[...]
+
+    def last(self):
+        def work(other, step):
+            self.copy(other, lax.rem(self.lk.fs - step, self.lk.fs)).wait_recv()
+
+        self.each(work)
+
+    def drain(self):
+        self.each(lambda other, step: self.copy(other, step).wait_send())
+
+
+class Trade:
+    def __init__(self, lk, src, dst, send, recv):
+        self.lk, self.src, self.dst, self.send, self.recv = lk, src, dst, send, recv
+
+    def copies(self):
+        lk = self.lk
+        pairs = ((lk.peer_t, lk.peer), (lk.diag_t, lk.diag), (lk.sib_t, lk.sib))
+        return [
+            remote(self.src(index), self.dst(lk.t), self.send.at[i], self.recv.at[i], target)
+            for i, (index, target) in enumerate(pairs)
+        ]
+
+    def first(self):
+        for copy in self.copies():
+            copy.start()
+        self.dst(self.lk.t)[...] = self.src(self.lk.t)[...]
+
+    def last(self):
+        for copy in self.copies():
+            copy.wait_recv()
+            copy.wait_send()
+
+
+def part_of(size, index):
+    return pl.ds(pl.multiple_of(index * size, size), size)
+
+
+def stored_slots(dst, values, first, count, sends, block):
+    for i in range(count):
+        dst(i)[block * sends : (block + 1) * sends] = values[
+            (first + i) * sends : (first + i + 1) * sends
+        ].astype(BF)
 
 
 class WeightGather:
@@ -215,13 +294,17 @@
 
 
 def forward_kernel(
-    act_in, shard, vec, head_bias, up_bias, seg_col, seg_row,
+    tokens, time_embed, cot, pick_out, pick_in, shard, vec, head_bias, up_bias, seg_col, seg_row,
     out_w, out_act, out_qkv, out_att, out_nrm, out_std, out_hid, out_glu, out_dglu, out_lse,
-    out_u,
+    out_u, out_cot,
     w, act, qkv, att, nrm, std, hid, glu, dglu, lse, u, h, part, from_sib, to_peer, from_peer,
-    in_sem, out_sem, rs_send, rs_recv, ag_send, ag_recv, z_send, z_recv, x_send, x_recv, own,
+    slots, arrived, cot_part, cot_rows, u_low,
+    out_sem, rs_send, rs_recv, ag_send, ag_recv, z_send, z_recv, x_send, x_recv, own,
+    ex_send, ex_recv, tr_send, tr_recv,
 ):
     layers, packs, rows, width = act.shape
+    sends = slots.shape[2] // packs
+    local_width = slots.shape[3]
     mine = rows // 4
     heads_width = att.shape[3]
     chunks = shard.shape[0]
@@ -237,16 +320,49 @@
         copy.start()
         pending.append(copy)
 
-    load = pltpu.make_async_copy(act_in, act.at[0], in_sem)
-    load.start()
+    my_rows = part_of(mine, lk.t)
+    my_cols = part_of(local_width, lk.t)
+    swaps = [
+        Exchange(
+            lk, lambda g, i=i: slots.at[i, g], lambda g, i=i: arrived.at[i, g],
+            ex_send.at[i], ex_recv.at[i],
+        )
+        for i in range(2)
+    ]
+
+    def send_slots(which, values):
+        for c in range(2):
+            for k in range(packs):
+                m = c * packs + k
+                picked = dot(pick_out[m], values(m), NN)
+                for f in range(picked.shape[0] // sends):
+                    slots[which, 2 * f + c, k * sends : (k + 1) * sends] = picked[
+                        f * sends : (f + 1) * sends
+                    ].astype(BF)
+        swaps[which].first()
+
+    def placed_rows(which, k):
+        blocks = [
+            arrived[which, g, k * sends : (k + 1) * sends] for g in range(arrived.shape[1])
+        ]
+        return dot(pick_in[k], jnp.concatenate(blocks, axis=0), NN).astype(BF)
+
     wg.start(0)
-    load.wait()
-    my_rows = pl.ds(pl.multiple_of(lk.t * mine, mine), mine)
+    send_slots(0, lambda m: (tokens[m].astype(F32) + time_embed[m].astype(F32)).astype(BF))
+    lse[...] = jnp.zeros_like(lse)
+    first_ag = RowGather(lk, local_width, ag_send, ag_recv, by_columns=True)
+    swaps[0].last()
     for k in range(packs):
-        u[k] = act[0, k, my_rows].astype(F32)
-    lse[...] = jnp.zeros_like(lse)
+        act[0, k, :, my_cols] = placed_rows(0, k)
+        first_ag.first(act.at[0, k], k)
     wg.forward(0)
     wg.start(1)
+    for k in range(packs):
+        first_ag.second(act.at[0, k], k)
+    for k in range(packs):
+        first_ag.last(act.at[0, k], k)
+        u[k] = act[0, k, my_rows].astype(F32)
+        save(act.at[0, k], out_act.at[0, k])
     wg.finish(0)
     save(w.at[0], out_w.at[0])
 
@@ -325,7 +441,8 @@
             act[layer + 1, k, my_rows] = out.astype(BF)
             ag.first(act.at[layer + 1, k], k)
         else:
-            save(u.at[k], out_u.at[k])
+            u_low[k] = out.astype(BF)
+            save(u_low.at[k], out_u.at[k])
 
     def weights_next(chunk):
         if chunk < chunks:
@@ -337,13 +454,17 @@
         wg.finish(chunk)
         save(w.at[chunk], out_w.at[chunk])
 
+    trade = Trade(
+        lk, lambda t: cot_part.at[:, part_of(mine, t)],
+        lambda t: cot_rows.at[:, :, part_of(local_width, t)], tr_send, tr_recv,
+    )
     for layer in range(layers):
         base = 3 * layer
         more = layer + 1 < layers
         if layer:
             weights_ready(base)
             ag.last(act.at[layer, 0], 0)
-            save(act.at[layer, 0], out_act.at[layer - 1, 0])
+            save(act.at[layer, 0], out_act.at[layer, 0])
         project(layer, 0)
         if layer:
             ag.second(act.at[layer, 1], 1)
@@ -351,7 +472,7 @@
         weights_next(base + 1)
         if layer:
             ag.last(act.at[layer, 1], 1)
-            save(act.at[layer, 1], out_act.at[layer - 1, 1])
+            save(act.at[layer, 1], out_act.at[layer, 1])
         project(layer, 1)
         rs.second(0)
         attention(layer, 1)
@@ -368,29 +489,46 @@
         weights_ready(base + 2)
         contract(layer, 0)
         weights_next(base + 3)
+        if not more:
+            send_slots(1, lambda m: cot[m])
         ag.last(hid.at[layer, 1], 1)
         save(hid.at[layer, 1], out_hid.at[layer, 1])
         expand(layer, 1)
         rs.second(0)
         contract(layer, 1)
+        if not more:
+            swaps[1].last()
+            for k in range(packs):
+                cot_part[k] = placed_rows(1, k)
+            trade.first()
         norm_two(layer, 0)
         rs.second(1)
         if more:
             ag.second(act.at[layer + 1, 0], 0)
         norm_two(layer, 1)
+    trade.last()
+    save(cot_rows, out_cot)
     for chunk in range(chunks):
         wg.drain(chunk)
+    for swap in swaps:
+        swap.drain()
     for copy in pending:
         copy.wait()
 
 
-def forward(act, shard, vec, head_bias, up_bias, seg_col, seg_row):
-    packs, rows, width = act.shape
+def forward(
+    tokens, time_embed, cot, pick_out, pick_in, shard, vec, head_bias, up_bias, seg_col, seg_row
+):
+    packs, rows = pick_in.shape[:2]
+    width = shard.shape[2]
+    local_width = tokens.shape[2]
     chunks = shard.shape[0]
     layers = chunks // 3
     mine = rows // 4
     heads = head_bias.shape[2]
-    fs = lax.axis_size("fsdp")
+    fs, cx = lax.axis_size("fsdp"), lax.axis_size("ctx")
+    groups = fs * cx
+    sends = tokens.shape[1] // fs
     shapes = dict(
         w=((chunks, width, width), BF),
         act=((layers, packs, rows, width), BF),
@@ -405,14 +543,15 @@
         u=((packs, mine, width), F32),
     )
     outs = {name: jax.ShapeDtypeStruct(*shape) for name, shape in shapes.items()}
-    outs["act"] = jax.ShapeDtypeStruct((layers - 1, packs, rows, width), BF)
-    copies = chunks + (layers - 1) * packs + layers * packs * 10 + packs
+    outs["u"] = jax.ShapeDtypeStruct((packs, mine, width), BF)
+    outs["cot"] = jax.ShapeDtypeStruct((packs, mine, width), BF)
+    copies = chunks + layers * packs * 11 + packs + 1
     dma = pltpu.SemaphoreType.DMA
     whole = pl.BlockSpec(memory_space=pl.ANY)
     vmem = pl.BlockSpec(memory_space=pltpu.VMEM)
     return pl.pallas_call(
         forward_kernel,
-        in_specs=[whole, whole, vmem, vmem, vmem, vmem, vmem],
+        in_specs=[vmem] * 5 + [whole] + [vmem] * 5,
         out_specs=[whole] * len(outs),
         out_shape=list(outs.values()),
         scratch_shapes=[pltpu.VMEM(*shape) for shape in shapes.values()]
@@ -422,16 +561,25 @@
             pltpu.VMEM((packs, 2, mine, width), BF),
             pltpu.VMEM((packs, mine, width), BF),
             pltpu.VMEM((packs, mine, width), BF),
-            dma(()), dma((copies,)),
+            pltpu.VMEM((2, groups, packs * sends, local_width), BF),
+            pltpu.VMEM((2, groups, packs * sends, local_width), BF),
+            pltpu.VMEM((packs, rows, local_width), BF),
+            pltpu.VMEM((packs, mine, width), BF),
+            pltpu.VMEM((packs, mine, width), BF),
+            dma((copies,)),
             dma((packs, 2)), dma((packs, 2)), dma((packs, 3)), dma((packs, 3)),
             dma((chunks, fs)), dma((chunks, fs)), dma((chunks, fs)), dma((chunks, fs)),
             dma((chunks,)),
+            dma((2, 2, fs)), dma((2, 2, fs)), dma((3,)), dma((3,)),
         ],
         compiler_params=pltpu.CompilerParams(
             collective_id=0, has_side_effects=True, vmem_limit_bytes=60 << 20
         ),
         name="forward",
-    )(act, shard, vec, head_bias, up_bias, seg_col, seg_row)
+    )(
+        tokens, time_embed, cot, pick_out, pick_in, shard, vec, head_bias, up_bias, seg_col,
+        seg_row,
+    )
 
 
 class GradScatter:
@@ -494,12 +642,14 @@
 
 
 def backward_kernel(
-    up_in, act_first, act_more, w_in, qkv_in, att_in, nrm_in, std_in, hid_in, glu_in, dglu_in,
+    up_in, u_in, pick_out, pick_in, act_in, w_in, qkv_in, att_in, nrm_in, std_in, hid_in, glu_in, dglu_in,
     lse_in, vec, seg_col, seg_row,
-    out_qkv, out_out, out_up, out_down, out_u, out_vec, out_head, out_bias,
+    out_qkv, out_out, out_up, out_down, out_ret, out_sums,
     w, qkv, att, nrm, std, hid, glu, dglu, lse, up, gtwo, gl, gm, gup, gqkv, gatt,
-    part, from_sib, to_peer, from_peer, grad, from_x, from_z, gsum, low,
+    part, from_sib, to_peer, from_peer, grad, from_x, from_z, gsum, low, ret_in,
+    out_vec, out_head, out_bias, vec_parts, sums,
     in_sem, out_sem, rs_send, rs_recv, ag_send, ag_recv, x_send, x_recv, z_send, z_recv,
+    ex_send, ex_recv, tr_send, tr_recv, pick_sem,
 ):
     packs, rows, width = hid.shape
     layers = vec.shape[0]
@@ -520,7 +670,7 @@
         qkv=lambda layer: (qkv_in.at[layer], qkv),
         lse=lambda layer: (lse_in.at[layer], lse),
         att=lambda layer: (att_in.at[layer], att),
-        act=lambda layer: (act_more.at[layer - 1] if layer else act_first, hid),
+        act=lambda layer: (act_in.at[layer], hid),
     )
     order = {name: index for index, name in enumerate(sources)}
 
@@ -533,8 +683,12 @@
         src, dst = sources[name](layer)
         pltpu.make_async_copy(src, dst, in_sem.at[order[name]]).wait()
 
-    load = pltpu.make_async_copy(up_in, up, in_sem.at[len(order)])
-    load.start()
+    loads = [
+        pltpu.make_async_copy(up_in, to_peer, in_sem.at[len(order)]),
+        pltpu.make_async_copy(u_in, low, in_sem.at[len(order) + 1]),
+    ]
+    for load in loads:
+        load.start()
     for name in sources:
         if name != "act":
             fetch(name, layers - 1)
@@ -545,6 +699,105 @@
     my_rows = pl.ds(pl.multiple_of(lk.t * mine, mine), mine)
     pending = []
     held = {}
+    local_width = ret_in.shape[1]
+    swap_rows = width // (lk.fs * lk.cx)
+    sends = swap_rows // packs
+    low_cols, next_cols, third_cols, last_cols = (
+        slice(i * local_width, (i + 1) * local_width) for i in range(4)
+    )
+
+    class Return:
+        def __init__(self, index, first, second, landed):
+            self.index, self.first_buf, self.second_buf, self.landed = index, first, second, landed
+            self.trade = Trade(
+                lk, lambda t: low.at[:, :, part_of(local_width, t)],
+                lambda t: gup.at[:, part_of(mine, t), low_cols],
+                tr_send.at[index], tr_recv.at[index],
+            )
+            self.swap = Exchange(
+                lk, lambda g: first.at[part_of(swap_rows, g), low_cols],
+                lambda g: landed.at[part_of(swap_rows, g)], ex_send.at[index], ex_recv.at[index],
+            )
+            self.picks = [
+                pltpu.make_async_copy(
+                    pick_in, second.at[:, : 2 * local_width], pick_sem.at[index, 0]
+                ),
+                pltpu.make_async_copy(pick_out, second.at[:, third_cols], pick_sem.at[index, 1]),
+            ]
+
+        def load(self):
+            for copy in self.picks:
+                copy.start()
+
+        def middle(self):
+            self.trade.last()
+            self.picks[0].wait()
+            for k in range(packs):
+                pick = self.second_buf[k * rows : (k + 1) * rows, : 2 * local_width]
+                values = dot(pick, gup[k, :, low_cols], TN).astype(BF)
+                for g in range(rows // sends):
+                    first = g * swap_rows + k * sends
+                    self.first_buf[first : first + sends, low_cols] = values[
+                        g * sends : (g + 1) * sends
+                    ]
+            self.swap.first()
+
+        def last(self):
+            self.swap.last()
+            self.picks[1].wait()
+            given = pick_out.shape[1]
+            for c in range(2):
+                for k in range(packs):
+                    m = c * packs + k
+                    blocks = [
+                        self.landed[
+                            (2 * f + c) * swap_rows + k * sends :
+                            (2 * f + c) * swap_rows + (k + 1) * sends
+                        ]
+                        for f in range(given // sends)
+                    ]
+                    pick = self.second_buf[m * given : (m + 1) * given, third_cols]
+                    values = dot(pick, jnp.concatenate(blocks, axis=0), TN)
+                    self.second_buf[m * given : (m + 1) * given, last_cols] = values.astype(BF)
+            save(self.second_buf.at[:, last_cols], out_ret.at[self.index])
+            self.saved = pending.pop()
+
+        def finish(self):
+            self.swap.drain()
+            self.saved.wait()
+
+    give_back = [
+        Return(0, grad.at[0], grad.at[1], grad.at[0, :, next_cols]),
+        Return(1, grad.at[3 * layers - 1], grad.at[3 * layers - 2], ret_in),
+    ]
+    vec_trade = Trade(
+        lk, lambda t: out_vec.at[:, :, part_of(local_width, t)], lambda t: vec_parts.at[t],
+        tr_send.at[2], tr_recv.at[2],
+    )
+    vec_swap = Exchange(
+        lk, lambda g: sums.at[lk.g], lambda g: sums.at[g], ex_send.at[2], ex_recv.at[2],
+        in_place=True,
+    )
+
+    def vec_middle():
+        vec_trade.last()
+        total = vec_parts[0]
+        for t in range(1, 4):
+            total = total + vec_parts[t]
+        sums[lk.g, :, 0:6] = total
+        sums[lk.g, :, 6:8] = out_head[...]
+        for j in range(4):
+            sums[lk.g, :, 8 + j : 9 + j] = out_bias[:, :, j * local_width : (j + 1) * local_width]
+        vec_swap.first()
+
+    def vec_last():
+        vec_swap.last()
+
+        def add(g, total):
+            return total + sums[g]
+
+        out_sums[...] = lax.fori_loop(1, sums.shape[0], add, sums[0])
+
     used = []
 
     def save(src, dst):
@@ -678,12 +931,16 @@
             save(out.at[:, 3 * heads_width :], out_out.at[layer])
         held[which] = [pending.pop() for _ in range(len(pending) - saved)]
 
-    load.wait()
+    give_back[0].load()
+    for load in loads:
+        load.wait()
     top = layers - 1
     ready("nrm1", top)
     ready("std1", top)
     for k in range(packs):
+        up[k] = to_peer[k].astype(F32)
         norm_two(top, k)
+    give_back[0].trade.first()
     fetch("nrm1", top - 1)
     fetch("std1", top - 1)
     for layer in reversed(range(layers)):
@@ -693,6 +950,8 @@
             first_grad(layer + 1)
             fetch("att", layer)
             fetch("hid", layer)
+        else:
+            give_back[0].middle()
         ready("w2", layer)
         ready("dglu", layer)
         ag.last(gl.at[0], 0)
@@ -758,42 +1017,56 @@
                 norm_two(layer - 1, k)
             else:
                 low[k] = up[k].astype(BF)
-                save(low.at[k], out_u.at[k])
+        if layer == top:
+            give_back[0].last()
+            give_back[0].finish()
         if layer:
             fetch("nrm1", layer - 2)
             fetch("std1", layer - 2)
         if layer < top:
             for which in (2, 1, 0):
                 emit(layer + 1, which)
+    for chunk in (3 * layers - 1, 3 * layers - 2):
+        gs.drain(chunk)
+    give_back[1].load()
+    give_back[1].trade.first()
+    vec_trade.first()
     gs.second(2)
+    give_back[1].middle()
+    vec_middle()
+    gs.second(1)
     emit(0, 2)
-    gs.second(1)
+    gs.second(0)
+    give_back[1].last()
+    vec_last()
     emit(0, 1)
-    gs.second(0)
     emit(0, 0)
-    for chunk in range(3 * layers):
+    for chunk in range(3 * layers - 2):
         gs.drain(chunk)
+    give_back[1].finish()
+    vec_swap.drain()
     for copy in pending + sum(held.values(), []):
         copy.wait()
 
 
-def backward(upstream, act, saved, vec, seg_col, seg_row):
+def backward(upstream, u, pick_out, pick_in, saved, vec, seg_col, seg_row):
     full_w, o_act, o_qkv, o_att, o_nrm, o_std, o_hid, o_glu, o_dglu, o_lse = saved
-    packs, rows, width = act.shape
-    layers, mine = vec.shape[0], rows // 4
+    layers, packs, rows, width = o_act.shape
+    mine = rows // 4
     chunks = 3 * layers
     heads = o_att.shape[3]
+    local_width = width // 4
     fs, cx = lax.axis_size("fsdp"), lax.axis_size("ctx")
-    shard = width // (fs * cx)
+    groups = fs * cx
+    shard = width // groups
+    given = pick_out.shape[0]
     outs = [
         jax.ShapeDtypeStruct((layers, 3, shard, heads), F32),
         jax.ShapeDtypeStruct((layers, shard, heads), F32),
         jax.ShapeDtypeStruct((layers, shard, width), F32),
         jax.ShapeDtypeStruct((layers, shard, width), F32),
-        jax.ShapeDtypeStruct((packs, mine, width), BF),
-        jax.ShapeDtypeStruct((layers, 6, width), F32),
-        jax.ShapeDtypeStruct((layers, 2, heads), F32),
-        jax.ShapeDtypeStruct((layers, 1, width), F32),
+        jax.ShapeDtypeStruct((2, given, local_width), BF),
+        jax.ShapeDtypeStruct((layers, 12, local_width), F32),
     ]
     dma = pltpu.SemaphoreType.DMA
     whole = pl.BlockSpec(memory_space=pl.ANY)
@@ -802,8 +1075,8 @@
     rowed = pltpu.VMEM((packs, mine, width), F32)
     return pl.pallas_call(
         backward_kernel,
-        in_specs=[whole] * 12 + [vmem] * 3,
-        out_specs=[whole] * 5 + [vmem] * 3,
+        in_specs=[whole] * 14 + [vmem] * 3,
+        out_specs=[whole] * 5 + [vmem],
         out_shape=outs,
         scratch_shapes=[
             pltpu.VMEM((3, width, width), BF),
@@ -826,22 +1099,25 @@
             pltpu.VMEM((chunks, fs - 1, shard, width), BF),
             pltpu.VMEM((3, shard, width), F32),
             pltpu.VMEM((packs, mine, width), BF),
-            dma((15,)), dma((packs + 6 * layers,)),
+            pltpu.VMEM((given, local_width), BF),
+            pltpu.VMEM((layers, 6, width), F32),
+            pltpu.VMEM((layers, 2, heads), F32),
+            pltpu.VMEM((layers, 1, width), F32),
+            pltpu.VMEM((4, layers, 6, local_width), F32),
+            pltpu.VMEM((groups, layers, 12, local_width), F32),
+            dma((16,)), dma((packs + 6 * layers + 2,)),
             dma((packs, 2)), dma((packs, 2)), dma((packs, 3)), dma((packs, 3)),
             dma((chunks, fs)), dma((chunks, fs)), dma((chunks, fs)), dma((chunks, fs)),
+            dma((3, 2, fs)), dma((3, 2, fs)), dma((3, 3)), dma((3, 3)), dma((2, 2)),
         ],
         compiler_params=pltpu.CompilerParams(
-            collective_id=1, has_side_effects=True, vmem_limit_bytes=60 << 20
+            collective_id=1, has_side_effects=True, vmem_limit_bytes=62 << 20
         ),
         name="backward",
     )(
-        upstream, act, o_act, full_w, o_qkv, o_att, o_nrm, o_std, o_hid, o_glu, o_dglu, o_lse,
-        vec, seg_col, seg_row,
-    )
-
-
-def mm(spec, left, right):
-    return jnp.einsum(spec, left, right, preferred_element_type=F32)
+        upstream, u, pick_out, pick_in, o_act, full_w, o_qkv, o_att, o_nrm, o_std, o_hid,
+        o_glu, o_dglu, o_lse, vec, seg_col, seg_row,
+    )
 
 
 def local(
@@ -850,13 +1126,11 @@
 ):
     micro, rows, width = tokens.shape
     layers = w_qkv.shape[0]
-    fs, cx, tp = (lax.axis_size(a) for a in ("fsdp", "ctx", "tp"))
-    groups = fs * cx
+    fs, cx = lax.axis_size("fsdp"), lax.axis_size("ctx")
     mine = micro // cx
     pack = segment_ids.shape[1]
     sends = rows // fs
     my_first = lax.axis_index("ctx") * mine
-    tp_index = lax.axis_index("tp")
 
     shard = jnp.concatenate(
         [w_qkv[:, 0], w_qkv[:, 1], w_qkv[:, 2], w_out, w_up, w_down], axis=2
@@ -865,10 +1139,6 @@
     shard = shard.reshape(layers * 3, shard.shape[2], -1)
     vec = jnp.concatenate([biases[:, 2:], norm_gain, norm_bias], axis=1)
     vec = lax.all_gather(vec, "tp", axis=2, tiled=True)
-    vectors = [
-        (biases[layer, :2], vec[layer, 0:2], vec[layer, 2:4], vec[layer, 4:6], up_bias[layer])
-        for layer in range(layers)
-    ]
 
     to_pack = to_owner // pack
     earlier = jnp.arange(rows)[None, :] < jnp.arange(rows)[:, None]
@@ -884,49 +1154,26 @@
     in_slot = source * sends + jnp.sum(before, axis=2)
     pick_in = (jnp.arange(pack)[None, None, :] == in_slot[:, :, None]).astype(BF)
 
-    def to_packs(values):
-        slots = mm("msg,mgw->msw", pick_out, values).astype(BF)
-        slots = slots.reshape(cx, mine, fs, sends, width).transpose(2, 0, 1, 3, 4)
-        slots = slots.reshape(groups, mine, sends, width)
-        slots = lax.all_to_all(slots, GRP, split_axis=0, concat_axis=0, tiled=True)
-        slots = slots.transpose(1, 0, 2, 3).reshape(mine, pack, width)
-        return mm("kps,ksw->kpw", pick_in, slots).astype(BF)
-
-    def from_packs(values):
-        values = lax.all_to_all(values.astype(BF), "tp", split_axis=2, concat_axis=1, tiled=True)
-        slots = mm("kps,kpw->ksw", pick_in, values).astype(BF)
-        slots = slots.reshape(mine, groups, sends, width).transpose(1, 0, 2, 3)
-        slots = lax.all_to_all(slots, GRP, split_axis=0, concat_axis=0, tiled=True)
-        slots = slots.reshape(fs, cx, mine, sends, width).transpose(1, 2, 0, 3, 4)
-        return mm("msg,msw->mgw", pick_out, slots.reshape(micro, rows, width))
-
-    embedded = (tokens.astype(F32) + time_embed.astype(F32)).astype(BF)
-    act = lax.all_gather(to_packs(embedded), "tp", axis=2, tiled=True)
-    upstream = lax.all_to_all(
-        to_packs(cotangent), "tp", split_axis=1, concat_axis=2, tiled=True
-    ).astype(F32)
     seg = lax.dynamic_slice_in_dim(segment_ids, my_first, mine)
     seg_col, seg_row = seg[:, :, None], seg[:, None, :]
 
-    *saved, resid = forward(
-        act, shard, vec, biases[:, :2], up_bias[:, None], seg_col, seg_row
-    )
-    outputs = from_packs(resid)
-    g_qkv, g_out, g_up, g_down, upstream, full_part, head_part, up_part = backward(
-        upstream, act, saved, vec, seg_col, seg_row
-    )
-    input_grad = from_packs(upstream)
-    up_part = up_part[:, 0]
-    full_part = lax.psum_scatter(full_part, "tp", scatter_dimension=2, tiled=True)
-    full_part, head_part, up_part = lax.psum((full_part, head_part, up_part), GRP)
+    *saved, u, upstream = forward(
+        tokens, time_embed, cotangent, pick_out, pick_in, shard, vec, biases[:, :2],
+        up_bias[:, None], seg_col, seg_row,
+    )
+    g_qkv, g_out, g_up, g_down, returned, sums = backward(
+        upstream, u, pick_out.reshape(micro * rows, rows), pick_in.reshape(mine * pack, pack),
+        saved, vec, seg_col, seg_row,
+    )
+    returned = returned.reshape(2, micro, rows, width).astype(F32)
     return (
-        outputs,
-        input_grad,
+        returned[0],
+        returned[1],
         g_qkv, g_out, g_up, g_down,
-        jnp.concatenate([head_part, full_part[:, 0:2]], axis=1),
-        full_part[:, 2:4],
-        full_part[:, 4:6],
-        up_part,
+        jnp.concatenate([sums[:, 6:8], sums[:, 0:2]], axis=1),
+        sums[:, 2:4],
+        sums[:, 4:6],
+        sums[:, 8:12].reshape(layers, -1),
     )
 
 

time: 613 us -> 487 us (0.79); the launches traced: 604 us -> 484 us
  waiting for transfers between devices: 68.4 us -> 0 us
  Pallas kernels: 411 us -> 448 us
  blocking collectives: 45.8 us -> 10.3 us
  starting transfers between devices: 33.1 us -> 0 us
  between operations: 14.6 us -> 1.04 us
  matrix products: 8.36 us -> 0 us
    all_to_all x7 -> x0, waiting for transfers between devices: 45.7 us -> none  [the longest x2 14.7 us: from_packs(): lax.all_to_all(values.astype(BF), 'tp', split_axis=2, concat_axis=1, tile...]
    pallas_call x2, Pallas kernels: 411 us -> 448 us  [the longest x1 234 us: backward(): pl.pallas_call(backward_kernel, in_specs=[whole] * 14 + [vmem] * 3, out_s...]
    psum x1 -> x0, blocking collectives: 35 us -> none  [local(): lax.psum((full_part, head_part, up_part), GRP)]
    all_to_all x7 -> x0, starting transfers between devices: 33.1 us -> none  [the longest x2 11.3 us: from_packs(): slots = lax.all_to_all(slots, GRP, split_axis=0, concat_axis=0, tiled=True)]
    reduce_scatter x1 -> x0, waiting for transfers between devices: 21.9 us -> none  [local(): lax.psum_scatter(full_part, 'tp', scatter_dimension=2, tiled=True)]
    dot_general x8 -> x0, matrix products: 8.36 us -> none  [mm(): return jnp.einsum(spec, left, right, preferred_element_type=F32)]
  transfers between devices with their start and end apart: 9 -> 0, of which waited for: 7 -> 0; matrix products, arithmetic and copies ran while one was open for 3% -> 0% of each run, Pallas kernels for 0% -> 0%
where the time goes in v4:
time: 487 us; the launch traced here: 484 us
  Pallas kernels  448 us (92%)
  local copies, waits for them, and re-layouts  15.2 us (3%)
  blocking collectives  10.3 us (2%)
  other arithmetic  9.51 us (2%)
    pallas_call x1, Pallas kernels, backward(): pl.pallas_call(backward_kernel, in_specs=[whole] * 14 + [vmem] * 3, out_s...  234 us
    pallas_call x1, Pallas kernels, forward(): pl.pallas_call(forward_kernel, in_specs=[vmem] * 5 + [whole] + [vmem] * 5...  214 us

profile of v4, /device:TPU:8, one launch (start us, length us, event | category | flops | bytes accessed | tf_op | source)
XLA Modules:
  0.0 483.8 jit_solution(6267555168173122793)
XLA Ops:
  0.6 0.0 copy-start
  0.7 0.0 copy-start.4
  0.7 0.0 copy-start.5
  0.7 0.0 copy-start.7
  0.7 0.7 copy-done
  1.4 0.6 broadcast_in_dim.8.seg_row
  2.0 0.7 add_select_fusion
  2.7 4.5 all_gather.6
  7.2 0.7 convert_reduce_fusion
  7.9 1.3 broadcast_in_dim.6.up_bias
  9.2 1.4 fusion.8
  10.5 0.7 pad_maximum_fusion.1
  11.3 5.8 %all_gather.7.vec = f32[2,6,1024]{2,1,0:T(8,128)} all-gather(f32[2,6,256]{2,1,0:T(8,128)S(1)} %pad_maximum_fusion.1), channel_id=1, replica_groups=mesh['fsdp'=4,'ctx'=2,'tp'=4] {'tp'}, dimensions={2}, use_global_device_ids=true | all-gather | bytes 61440 | tf_op jit(solution)/shard_map/all_gather | solution.py:1141
  17.1 0.4 convert_reduce_fusion.1
  17.5 0.7 multiply_add_fusion.1
  18.2 1.1 slice_bitcast_fusion.2
  19.2 1.0 copy.35.seg_col
  20.3 1.0 fusion.3.pick_out
  21.3 0.9 fusion.2.pick_out
  22.2 1.2 fusion.1.pick_in
  23.4 1.2 fusion.pick_in
  24.6 0.0 copy-done.4
  24.6 0.0 copy-done.5
  24.6 0.0 copy-done.7
  24.6 1.3 pad_maximum_fusion
  25.9 214.0 %forward.1 = (bf16[6,1024,1024]{2,1,0:T(8,128)(2,1)}, bf16[2,2,512,1024]{3,2,1,0:T(8,128)(2,1)}, bf16[2,2,512,768]{3,2,1,0:T(8,128)(2,1)}, bf16[2,2,512,256]{3,2...) custom-call(bf16[4,256,256]{2,1,0:T(8,128)(2,1)} %tokens.1, ...), custom_call_target="tpu_custom_call" | custom-call | tf_op jit(solution)/shard_map/forward/pallas_call | solution.py:552
  240.0 233.7 %backward.1 = (f32[2,3,128,256]{3,2,1,0:T(8,128)}, f32[2,128,256]{2,1,0:T(8,128)}, f32[2,128,1024]{2,1,0:T(8,128)}, f32[2,128,1024]{2,1,0:T(8,128)}, bf16[2,1024...) custom-call(bf16[2,128,1024]{2,1,0:T(8,128)(2,1)} %get-tuple-element.28.up_in, bf16[2,128,1024]{2,1,0:T(8,128)(2,1)} %get-tuple-element.29.u_in, ...), custom_call_target="tpu_custom_call" | custom-call | tf_op jit(solution)/shard_map/backward/pallas_call | solution.py:1076
  473.7 0.0 copy-start.3
  473.7 0.0 copy-start.6
  473.7 0.8 slice_bitcast_fusion.3
  474.5 1.5 fusion.7
  476.0 0.6 copy.42
  476.6 0.6 pad_maximum_fusion.2
  477.2 0.0 copy-start.2
  477.2 2.8 fusion.6
  480.0 0.0 copy-start.1
  480.0 0.0 copy-done.3
  480.0 0.9 copy.47
  480.8 0.0 copy-done.6
  480.8 0.7 copy.48
  481.6 0.0 copy-done.2
  481.6 1.0 copy.49
  482.5 0.0 copy-done.1
  482.5 1.0 copy.50
  (8 shorter events, 0.1 us)
Async XLA Ops:
  0.6 0.7 copy-start
  0.7 24.0 %copy-start.4 = (bf16[2,128,1024]{2,1,0:T(8,128)(2,1)S(1)}, bf16[2,128,1024]{2,1,0:T(8,128)(2,1)}, u32[]{:S(2)}) copy-start(bf16[2,128,1024]{2,1,0:T(8,128)(2,1)} %param.23) | copy-start | bytes 1572868
  0.7 24.0 %copy-start.5 = (bf16[2,128,1024]{2,1,0:T(8,128)(2,1)S(1)}, bf16[2,128,1024]{2,1,0:T(8,128)(2,1)}, u32[]{:S(2)}) copy-start(bf16[2,128,1024]{2,1,0:T(8,128)(2,1)} %param.22) | copy-start | bytes 1572868
  0.7 23.9 %copy-start.7 = (bf16[2,128,256]{2,1,0:T(8,128)(2,1)S(1)}, bf16[2,128,256]{2,1,0:T(8,128)(2,1)}, u32[]{:S(2)}) copy-start(bf16[2,128,256]{2,1,0:T(8,128)(2,1)} %param.21) | copy-start | bytes 393220
  473.7 6.3 %copy-start.3 = (f32[2,3,128,256]{3,2,1,0:T(8,128)S(1)}, f32[2,3,128,256]{3,2,1,0:T(8,128)}, u32[]{:S(2)}) copy-start(f32[2,3,128,256]{3,2,1,0:T(8,128)} %get-tuple-element.72) | copy-start | bytes 2359300
  473.7 7.1 %copy-start.6 = (f32[2,128,256]{2,1,0:T(8,128)S(1)}, f32[2,128,256]{2,1,0:T(8,128)}, u32[]{:S(2)}) copy-start(f32[2,128,256]{2,1,0:T(8,128)} %get-tuple-element.73) | copy-start | bytes 786436
  477.2 4.4 copy-start.2
  480.0 2.6 copy-start.1

commit v5 on v4

--- a/solution.py
+++ b/solution.py
@@ -25,6 +25,7 @@
 
 MESH = pl.DeviceIdType.MESH
 LOG2E = 1.4426950408889634
+HALVES = 1
 
 
 def gelu_pair(values):
@@ -205,6 +206,10 @@
             copy.wait_send()
 
 
+def third(count, part):
+    return 1 + (count - 1) * part // 3, 1 + (count - 1) * (part + 1) // 3
+
+
 def part_of(size, index):
     return pl.ds(pl.multiple_of(index * size, size), size)
 
@@ -214,6 +219,39 @@
         dst(i)[block * sends : (block + 1) * sends] = values[
             (first + i) * sends : (first + i + 1) * sends
         ].astype(BF)
+
+
+def one_hot(rows, values):
+    return (lax.broadcasted_iota(jnp.int32, (rows, values.shape[1]), 0) == values).astype(BF)
+
+
+def counts_before(present):
+    size = present.shape[1]
+    earlier = lax.broadcasted_iota(jnp.int32, (size, size), 0) < lax.broadcasted_iota(
+        jnp.int32, (size, size), 1
+    )
+    return dot(present, earlier.astype(BF), NN)
+
+
+def leaving_slots(to_row, packs_total, pack, sends):
+    groups = one_hot(packs_total, to_row // pack)
+    base = lax.broadcasted_iota(jnp.int32, groups.shape, 0) * sends
+    slot = (counts_before(groups) + base.astype(F32)) * groups.astype(F32)
+    return one_hot(to_row.shape[1], jnp.sum(slot, axis=0, keepdims=True).astype(jnp.int32))
+
+
+def coming_slots(given, groups, rows, sends):
+    source = one_hot(groups, given // rows)
+    within = one_hot(rows, lax.rem(given, rows))
+    ranks = counts_before(dot(source, within, NT).astype(BF)).astype(BF)
+    base = lax.broadcasted_iota(jnp.int32, source.shape, 0) * sends
+    slot = (dot(ranks, within, NN) + base.astype(F32)) * source.astype(F32)
+    return one_hot(groups * sends, jnp.sum(slot, axis=0, keepdims=True).astype(jnp.int32))
+
+
+def same_sequence(seg_ref, row):
+    member = one_hot(8, lax.rem(seg_ref[pl.ds(row, 1)], 8))
+    return dot(member, member, TN) > 0.5
 
 
 class WeightGather:
@@ -222,14 +260,21 @@
         self.z_send, self.z_recv, self.x_send, self.x_recv = z_send, z_recv, x_send, x_recv
         self.own = own
         self.rows = shard.shape[1]
+        self.cols = shard.shape[2] // HALVES
+
+    def part(self, chunk):
+        return slice(chunk % HALVES * self.cols, (chunk % HALVES + 1) * self.cols)
+
+    def mine(self, chunk):
+        return self.shard.at[chunk // HALVES, :, self.part(chunk)]
 
     def block(self, chunk, f, c):
-        first = pl.multiple_of((f * self.lk.cx + c) * self.rows, self.rows)
-        return self.full.at[chunk, pl.ds(first, self.rows)]
+        rows = part_of(self.rows, f * self.lk.cx + c)
+        return self.full.at[chunk // HALVES, rows, self.part(chunk)]
 
     def z_copy(self, chunk, step):
         return remote(
-            self.shard.at[chunk], self.block(chunk, self.lk.f, self.lk.c),
+            self.mine(chunk), self.block(chunk, self.lk.f, self.lk.c),
             self.z_send.at[chunk, step], self.z_recv.at[chunk, self.lk.fs - step],
             self.lk.away(step),
         )
@@ -243,13 +288,13 @@
 
     def x_own(self, chunk):
         return remote(
-            self.shard.at[chunk], self.block(chunk, self.lk.f, self.lk.c),
+            self.mine(chunk), self.block(chunk, self.lk.f, self.lk.c),
             self.x_send.at[chunk, 0], self.x_recv.at[chunk, 0], self.lk.across,
         )
 
     def own_copy(self, chunk):
         return pltpu.make_async_copy(
-            self.shard.at[chunk], self.block(chunk, self.lk.f, self.lk.c), self.own.at[chunk]
+            self.mine(chunk), self.block(chunk, self.lk.f, self.lk.c), self.own.at[chunk]
         )
 
     def each(self, first, work):
@@ -294,13 +339,14 @@
 
 
 def forward_kernel(
-    tokens, time_embed, cot, pick_out, pick_in, shard, vec, head_bias, up_bias, seg_col, seg_row,
+    tokens, time_embed, cot, to_owner, from_owner, seg, shard, biases, gain, offset, up_bias,
     out_w, out_act, out_qkv, out_att, out_nrm, out_std, out_hid, out_glu, out_dglu, out_lse,
-    out_u, out_cot,
+    out_u, out_cot, out_gain, out_pick_out, out_pick_in,
     w, act, qkv, att, nrm, std, hid, glu, dglu, lse, u, h, part, from_sib, to_peer, from_peer,
     slots, arrived, cot_part, cot_rows, u_low,
+    bias_full, gain_full, offset_full, pick_out, pick_in, given,
     out_sem, rs_send, rs_recv, ag_send, ag_recv, z_send, z_recv, x_send, x_recv, own,
-    ex_send, ex_recv, tr_send, tr_recv,
+    ex_send, ex_recv, tr_send, tr_recv, given_sem,
 ):
     layers, packs, rows, width = act.shape
     sends = slots.shape[2] // packs
@@ -334,7 +380,7 @@
         for c in range(2):
             for k in range(packs):
                 m = c * packs + k
-                picked = dot(pick_out[m], values(m), NN)
+                picked = dot(pick_out[m * held : (m + 1) * held], values(m), NN)
                 for f in range(picked.shape[0] // sends):
                     slots[which, 2 * f + c, k * sends : (k + 1) * sends] = picked[
                         f * sends : (f + 1) * sends
@@ -345,38 +391,87 @@
         blocks = [
             arrived[which, g, k * sends : (k + 1) * sends] for g in range(arrived.shape[1])
         ]
-        return dot(pick_in[k], jnp.concatenate(blocks, axis=0), NN).astype(BF)
-
-    wg.start(0)
+        return dot(
+            pick_in[k * rows : (k + 1) * rows], jnp.concatenate(blocks, axis=0), TN
+        ).astype(BF)
+
+    def weights_next(chunk):
+        if chunk < chunks:
+            for part in range(chunk * HALVES, (chunk + 1) * HALVES):
+                if part + HALVES < chunks * HALVES:
+                    wg.start(part + HALVES)
+                wg.forward(part)
+
+    def weights_ready(chunk):
+        for part in range(chunk * HALVES, (chunk + 1) * HALVES):
+            wg.finish(part)
+        save(w.at[chunk], out_w.at[chunk])
+
+    for half in range(HALVES):
+        wg.start(half)
+    give = remote(
+        from_owner, given.at[lk.c], given_sem.at[0], given_sem.at[1], lk.across
+    )
+    give.start()
+    params = [
+        Trade(
+            lk, lambda t, src=src: src, lambda t, full=full: full.at[:, :, part_of(local_width, t)],
+            tr_send.at[1 + i], tr_recv.at[1 + i],
+        )
+        for i, (src, full) in enumerate(
+            ((biases, bias_full), (gain, gain_full), (offset, offset_full))
+        )
+    ]
+    for param in params:
+        param.first()
+    held = tokens.shape[1]
+    for m in range(tokens.shape[0]):
+        pick_out[m * held : (m + 1) * held] = leaving_slots(
+            to_owner[m : m + 1], held // sends, rows, sends
+        )
     send_slots(0, lambda m: (tokens[m].astype(F32) + time_embed[m].astype(F32)).astype(BF))
     lse[...] = jnp.zeros_like(lse)
     first_ag = RowGather(lk, local_width, ag_send, ag_recv, by_columns=True)
+    given[lk.c] = from_owner[...]
+    give.wait_recv()
+    give.wait_send()
+    for k in range(packs):
+        m = pl.ds(lk.c * packs + k, 1)
+        row = jnp.concatenate([given[c, m] for c in range(2)], axis=1)
+        pick_in[k * rows : (k + 1) * rows] = coming_slots(
+            row, arrived.shape[1], held, sends
+        )
+    for param in params:
+        param.last()
+    save(gain_full, out_gain)
+    save(pick_out, out_pick_out)
+    save(pick_in, out_pick_in)
     swaps[0].last()
     for k in range(packs):
         act[0, k, :, my_cols] = placed_rows(0, k)
         first_ag.first(act.at[0, k], k)
-    wg.forward(0)
-    wg.start(1)
+    for half in range(HALVES):
+        wg.forward(half)
+        wg.start(HALVES + half)
     for k in range(packs):
         first_ag.second(act.at[0, k], k)
     for k in range(packs):
         first_ag.last(act.at[0, k], k)
         u[k] = act[0, k, my_rows].astype(F32)
         save(act.at[0, k], out_act.at[0, k])
-    wg.finish(0)
-    save(w.at[0], out_w.at[0])
+    weights_ready(0)
 
     def project(layer, k):
         for j in range(3):
             cols = slice(j * heads_width, (j + 1) * heads_width)
             acc = dot(act[layer, k], w[3 * layer, :, cols], NN)
             if j != 1:
-                acc = acc + head_bias[layer, j // 2 : j // 2 + 1]
+                acc = acc + biases[layer, j // 2 : j // 2 + 1]
             qkv[layer, k, :, cols] = acc.astype(BF)
         save(qkv.at[layer, k], out_qkv.at[layer, k])
 
     def attention(layer, k):
-        same_seq = seg_col[k] == seg_row[k]
+        same_seq = same_sequence(seg, lk.c * packs + k)
         for head in range(heads_width // HD):
             cols = [slice(j * heads_width + head * HD, j * heads_width + (head + 1) * HD) for j in range(3)]
             scores = masked_scores(qkv[layer, k, :, cols[0]], qkv[layer, k, :, cols[1]], same_seq)
@@ -403,10 +498,12 @@
         std[layer, which, k] = jnp.broadcast_to(scale, std.shape[3:])
         save(nrm.at[layer, which, k], out_nrm.at[layer, which, k])
         save(std.at[layer, which, k], out_std.at[layer, which, k])
-        return normed * vec[layer, 2 + which : 3 + which] + vec[layer, 4 + which : 5 + which]
+        return (
+            normed * gain_full[layer, which : which + 1] + offset_full[layer, which : which + 1]
+        )
 
     def norm_one(layer, k):
-        hidden = normalize(layer, 0, k, u[k] + rs.last(k) + vec[layer, 0:1])
+        hidden = normalize(layer, 0, k, u[k] + rs.last(k) + bias_full[layer, 2:3])
         h[k] = hidden
         hid[layer, k, my_rows] = hidden.astype(BF)
         ag.first(hid.at[layer, k], k)
@@ -414,7 +511,7 @@
     def expand(layer, k):
         def tile(j, carry):
             cols = pl.ds(pl.multiple_of(j * 256, 256), 256)
-            acc = dot(hid[layer, k], w[3 * layer + 1, :, cols], NN) + up_bias[layer, :, cols]
+            acc = dot(hid[layer, k], w[3 * layer + 1, :, cols], NN) + up_bias[layer : layer + 1, cols]
             value, slope = gelu_pair(acc)
             glu[layer, k, :, cols] = value.astype(BF)
             dglu[layer, k, :, cols] = slope.astype(BF)
@@ -435,7 +532,7 @@
         rs.first(k)
 
     def norm_two(layer, k):
-        out = normalize(layer, 1, k, h[k] + rs.last(k) + vec[layer, 1:2])
+        out = normalize(layer, 1, k, h[k] + rs.last(k) + bias_full[layer, 3:4])
         u[k] = out
         if layer + 1 < layers:
             act[layer + 1, k, my_rows] = out.astype(BF)
@@ -444,19 +541,9 @@
             u_low[k] = out.astype(BF)
             save(u_low.at[k], out_u.at[k])
 
-    def weights_next(chunk):
-        if chunk < chunks:
-            if chunk + 1 < chunks:
-                wg.start(chunk + 1)
-            wg.forward(chunk)
-
-    def weights_ready(chunk):
-        wg.finish(chunk)
-        save(w.at[chunk], out_w.at[chunk])
-
     trade = Trade(
         lk, lambda t: cot_part.at[:, part_of(mine, t)],
-        lambda t: cot_rows.at[:, :, part_of(local_width, t)], tr_send, tr_recv,
+        lambda t: cot_rows.at[:, :, part_of(local_width, t)], tr_send.at[0], tr_recv.at[0],
     )
     for layer in range(layers):
         base = 3 * layer
@@ -508,8 +595,8 @@
         norm_two(layer, 1)
     trade.last()
     save(cot_rows, out_cot)
-    for chunk in range(chunks):
-        wg.drain(chunk)
+    for part in range(chunks * HALVES):
+        wg.drain(part)
     for swap in swaps:
         swap.drain()
     for copy in pending:
@@ -517,18 +604,20 @@
 
 
 def forward(
-    tokens, time_embed, cot, pick_out, pick_in, shard, vec, head_bias, up_bias, seg_col, seg_row
+    tokens, time_embed, cot, to_owner, from_owner, seg, shard, biases, gain, offset, up_bias
 ):
-    packs, rows = pick_in.shape[:2]
+    rows = seg.shape[1]
+    packs = tokens.shape[0] // lax.axis_size("ctx")
     width = shard.shape[2]
     local_width = tokens.shape[2]
     chunks = shard.shape[0]
     layers = chunks // 3
     mine = rows // 4
-    heads = head_bias.shape[2]
+    heads = biases.shape[2]
     fs, cx = lax.axis_size("fsdp"), lax.axis_size("ctx")
     groups = fs * cx
     sends = tokens.shape[1] // fs
+    parts = chunks * HALVES
     shapes = dict(
         w=((chunks, width, width), BF),
         act=((layers, packs, rows, width), BF),
@@ -545,13 +634,17 @@
     outs = {name: jax.ShapeDtypeStruct(*shape) for name, shape in shapes.items()}
     outs["u"] = jax.ShapeDtypeStruct((packs, mine, width), BF)
     outs["cot"] = jax.ShapeDtypeStruct((packs, mine, width), BF)
-    copies = chunks + layers * packs * 11 + packs + 1
+    outs["gain"] = jax.ShapeDtypeStruct((layers, 2, width), F32)
+    given = tokens.shape[0] * tokens.shape[1]
+    outs["pick_out"] = jax.ShapeDtypeStruct((given, tokens.shape[1]), BF)
+    outs["pick_in"] = jax.ShapeDtypeStruct((packs * rows, rows), BF)
+    copies = chunks + layers * packs * 11 + packs + 4
     dma = pltpu.SemaphoreType.DMA
     whole = pl.BlockSpec(memory_space=pl.ANY)
     vmem = pl.BlockSpec(memory_space=pltpu.VMEM)
     return pl.pallas_call(
         forward_kernel,
-        in_specs=[vmem] * 5 + [whole] + [vmem] * 5,
+        in_specs=[vmem] * 6 + [whole] + [vmem] * 4,
         out_specs=[whole] * len(outs),
         out_shape=list(outs.values()),
         scratch_shapes=[pltpu.VMEM(*shape) for shape in shapes.values()]
@@ -566,19 +659,24 @@
             pltpu.VMEM((packs, rows, local_width), BF),
             pltpu.VMEM((packs, mine, width), BF),
             pltpu.VMEM((packs, mine, width), BF),
+            pltpu.VMEM((layers, 4, width), F32),
+            pltpu.VMEM((layers, 2, width), F32),
+            pltpu.VMEM((layers, 2, width), F32),
+            pltpu.VMEM((given, tokens.shape[1]), BF),
+            pltpu.VMEM((packs * rows, rows), BF),
+            pltpu.VMEM((2,) + from_owner.shape, jnp.int32),
             dma((copies,)),
             dma((packs, 2)), dma((packs, 2)), dma((packs, 3)), dma((packs, 3)),
-            dma((chunks, fs)), dma((chunks, fs)), dma((chunks, fs)), dma((chunks, fs)),
-            dma((chunks,)),
-            dma((2, 2, fs)), dma((2, 2, fs)), dma((3,)), dma((3,)),
+            dma((parts, fs)), dma((parts, fs)), dma((parts, fs)), dma((parts, fs)),
+            dma((parts,)),
+            dma((2, 2, fs)), dma((2, 2, fs)), dma((4, 3)), dma((4, 3)), dma((2,)),
         ],
         compiler_params=pltpu.CompilerParams(
             collective_id=0, has_side_effects=True, vmem_limit_bytes=60 << 20
         ),
         name="forward",
     )(
-        tokens, time_embed, cot, pick_out, pick_in, shard, vec, head_bias, up_bias, seg_col,
-        seg_row,
+        tokens, time_embed, cot, to_owner, from_owner, seg, shard, biases, gain, offset, up_bias
     )
 
 
@@ -606,25 +704,26 @@
             self.z_send.at[chunk, step], self.z_recv.at[chunk, slot], self.lk.away(step),
         )
 
-    def each(self, first, work):
+    def each(self, first, work, last=None):
         def body(step, carry):
             work(step)
             return carry
 
-        lax.fori_loop(first, self.lk.fs, body, 0)
+        lax.fori_loop(first, self.lk.fs if last is None else last, body, 0)
 
     def first(self, chunk):
         self.each(1, lambda step: self.x_copy(chunk, step).start())
         self.x_copy(chunk, 0).start()
 
-    def second(self, chunk):
+    def second(self, chunk, part):
         def work(step):
             self.x_copy(chunk, step).wait_recv()
             own = self.block(chunk, step, self.lk.c)
             own[...] = (own[...].astype(F32) + self.from_x[chunk, step].astype(F32)).astype(BF)
             self.z_copy(chunk, step).start()
 
-        self.each(1, work)
+        first, last = third(self.lk.fs, part)
+        self.each(first, work, last)
 
     def last(self, chunk, out):
         self.x_copy(chunk, 0).wait_recv()
@@ -643,7 +742,7 @@
 
 def backward_kernel(
     up_in, u_in, pick_out, pick_in, act_in, w_in, qkv_in, att_in, nrm_in, std_in, hid_in, glu_in, dglu_in,
-    lse_in, vec, seg_col, seg_row,
+    lse_in, gain, seg,
     out_qkv, out_out, out_up, out_down, out_ret, out_sums,
     w, qkv, att, nrm, std, hid, glu, dglu, lse, up, gtwo, gl, gm, gup, gqkv, gatt,
     part, from_sib, to_peer, from_peer, grad, from_x, from_z, gsum, low, ret_in,
@@ -652,7 +751,7 @@
     ex_send, ex_recv, tr_send, tr_recv, pick_sem,
 ):
     packs, rows, width = hid.shape
-    layers = vec.shape[0]
+    layers = gain.shape[0]
     mine = rows // 4
     heads_width = att.shape[2]
     lk = Links()
@@ -734,7 +833,7 @@
             self.picks[0].wait()
             for k in range(packs):
                 pick = self.second_buf[k * rows : (k + 1) * rows, : 2 * local_width]
-                values = dot(pick, gup[k, :, low_cols], TN).astype(BF)
+                values = dot(pick, gup[k, :, low_cols], NN).astype(BF)
                 for g in range(rows // sends):
                     first = g * swap_rows + k * sends
                     self.first_buf[first : first + sends, low_cols] = values[
@@ -815,7 +914,7 @@
         scale = std[which, k][:, 0:1]
         out_vec[layer, 2 + which : 3 + which] += jnp.sum(upstream * normed, axis=0, keepdims=True)
         out_vec[layer, 4 + which : 5 + which] += jnp.sum(upstream, axis=0, keepdims=True)
-        scaled = upstream * vec[layer, 2 + which : 3 + which]
+        scaled = upstream * gain[layer, which : which + 1]
         first = jnp.mean(scaled, axis=1, keepdims=True)
         second = jnp.mean(scaled * normed, axis=1, keepdims=True)
         result = scale * (scaled - first - normed * second)
@@ -858,7 +957,7 @@
         gatt[k] = dot(gm[k], w[0, :, 3 * heads_width :], NN).astype(BF)
 
     def attention(layer, k):
-        same_seq = seg_col[k] == seg_row[k]
+        same_seq = same_sequence(seg, lk.c * packs + k)
         scale = 1.0 / math.sqrt(HD)
         for head in range(heads_width // HD):
             cols = [slice(j * heads_width + head * HD, j * heads_width + (head + 1) * HD) for j in range(3)]
@@ -944,14 +1043,13 @@
     fetch("nrm1", top - 1)
     fetch("std1", top - 1)
     for layer in reversed(range(layers)):
+        base = 3 * layer
+        later = layer < top
         ag.second(gl.at[0], 0)
-        if layer < top:
-            ready("act", layer + 1)
-            first_grad(layer + 1)
-            fetch("att", layer)
-            fetch("hid", layer)
+        if layer == top:
+            give_back[0].middle()
         else:
-            give_back[0].middle()
+            gs.second(base + 3 + 1, 1)
         ready("w2", layer)
         ready("dglu", layer)
         ag.last(gl.at[0], 0)
@@ -966,6 +1064,8 @@
         rs.second(0)
         through_up(layer, 1)
         fetch("w1", layer - 1)
+        if later:
+            gs.second(base + 3 + 1, 2)
         ready("glu", layer)
         down_grad(layer)
         fetch("glu", layer - 1)
@@ -973,8 +1073,8 @@
         ready("nrm0", layer)
         ready("std0", layer)
         norm_one(layer, 0)
-        if layer < top:
-            gs.second(3 * (layer + 1) + 1)
+        if later:
+            gs.second(base + 3, 0)
         ready("hid", layer)
         up_grad(layer)
         fetch("act", layer)
@@ -982,18 +1082,21 @@
         norm_one(layer, 1)
         fetch("nrm0", layer - 1)
         fetch("std0", layer - 1)
+        if later:
+            gs.second(base + 3, 1)
         ready("w0", layer)
         ready("qkv", layer)
         ready("lse", layer)
         ag.last(gm.at[0], 0)
         through_out(0)
+        ag.second(gm.at[1], 1)
         attention(layer, 0)
-        ag.second(gm.at[1], 1)
         through_qkv(0)
-        if layer < top:
-            gs.second(3 * (layer + 1))
+        if later:
+            gs.second(base + 3, 2)
         else:
-            gs.second(3 * layer + 2)
+            gs.second(base + 2, 0)
+            gs.second(base + 2, 1)
         ag.last(gm.at[1], 1)
         through_out(1)
         rs.second(0)
@@ -1002,13 +1105,19 @@
         fetch("lse", layer - 1)
         through_qkv(1)
         fetch("w0", layer - 1)
+        if later:
+            gs.second(base + 2, 0)
+        else:
+            gs.second(base + 2, 2)
+            gs.second(base + 1, 0)
+        rs.second(1)
         ready("att", layer)
-        if layer == 0:
-            ready("act", layer)
-            first_grad(0)
+        ready("act", layer)
+        first_grad(layer)
+        if layer:
+            fetch("att", layer - 1)
+            fetch("hid", layer - 1)
         for k in range(packs):
-            if k:
-                rs.second(k)
             up[k] = rs.last(k) + up[k]
             if layer:
                 if k == 0:
@@ -1023,22 +1132,27 @@
         if layer:
             fetch("nrm1", layer - 2)
             fetch("std1", layer - 2)
-        if layer < top:
-            for which in (2, 1, 0):
-                emit(layer + 1, which)
+    give_back[1].trade.first()
+    vec_trade.first()
+    gs.second(2, 1)
+    emit(1, 2)
+    emit(1, 1)
     for chunk in (3 * layers - 1, 3 * layers - 2):
         gs.drain(chunk)
     give_back[1].load()
-    give_back[1].trade.first()
-    vec_trade.first()
-    gs.second(2)
+    gs.second(2, 2)
     give_back[1].middle()
     vec_middle()
-    gs.second(1)
+    emit(1, 0)
+    gs.second(1, 0)
+    gs.second(1, 1)
+    gs.second(1, 2)
     emit(0, 2)
-    gs.second(0)
+    gs.second(0, 0)
     give_back[1].last()
     vec_last()
+    gs.second(0, 1)
+    gs.second(0, 2)
     emit(0, 1)
     emit(0, 0)
     for chunk in range(3 * layers - 2):
@@ -1049,7 +1163,7 @@
         copy.wait()
 
 
-def backward(upstream, u, pick_out, pick_in, saved, vec, seg_col, seg_row):
+def backward(upstream, u, pick_out, pick_in, saved, gain, seg):
     full_w, o_act, o_qkv, o_att, o_nrm, o_std, o_hid, o_glu, o_dglu, o_lse = saved
     layers, packs, rows, width = o_act.shape
     mine = rows // 4
@@ -1075,7 +1189,7 @@
     rowed = pltpu.VMEM((packs, mine, width), F32)
     return pl.pallas_call(
         backward_kernel,
-        in_specs=[whole] * 14 + [vmem] * 3,
+        in_specs=[whole] * 14 + [vmem] * 2,
         out_specs=[whole] * 5 + [vmem],
         out_shape=outs,
         scratch_shapes=[
@@ -1116,7 +1230,7 @@
         name="backward",
     )(
         upstream, u, pick_out, pick_in, o_act, full_w, o_qkv, o_att, o_nrm, o_std, o_hid,
-        o_glu, o_dglu, o_lse, vec, seg_col, seg_row,
+        o_glu, o_dglu, o_lse, gain, seg,
     )
 
 
@@ -1126,44 +1240,17 @@
 ):
     micro, rows, width = tokens.shape
     layers = w_qkv.shape[0]
-    fs, cx = lax.axis_size("fsdp"), lax.axis_size("ctx")
-    mine = micro // cx
-    pack = segment_ids.shape[1]
-    sends = rows // fs
-    my_first = lax.axis_index("ctx") * mine
-
     shard = jnp.concatenate(
         [w_qkv[:, 0], w_qkv[:, 1], w_qkv[:, 2], w_out, w_up, w_down], axis=2
     )
     shard = shard.reshape(layers, shard.shape[1], 3, -1).transpose(0, 2, 1, 3)
     shard = shard.reshape(layers * 3, shard.shape[2], -1)
-    vec = jnp.concatenate([biases[:, 2:], norm_gain, norm_bias], axis=1)
-    vec = lax.all_gather(vec, "tp", axis=2, tiled=True)
-
-    to_pack = to_owner // pack
-    earlier = jnp.arange(rows)[None, :] < jnp.arange(rows)[:, None]
-    rank = jnp.sum((to_pack[:, :, None] == to_pack[:, None, :]) & earlier[None], axis=2)
-    out_slot = to_pack * sends + rank
-    pick_out = (jnp.arange(rows)[None, :, None] == out_slot[:, None, :]).astype(BF)
-    given = lax.all_gather(from_owner, "ctx", axis=1, tiled=True)
-    given = lax.dynamic_slice_in_dim(given, my_first, mine)
-    source = given // rows
-    before = (given[:, None, :] < given[:, :, None]) & (
-        given[:, None, :] >= (source * rows)[:, :, None]
-    )
-    in_slot = source * sends + jnp.sum(before, axis=2)
-    pick_in = (jnp.arange(pack)[None, None, :] == in_slot[:, :, None]).astype(BF)
-
-    seg = lax.dynamic_slice_in_dim(segment_ids, my_first, mine)
-    seg_col, seg_row = seg[:, :, None], seg[:, None, :]
-
-    *saved, u, upstream = forward(
-        tokens, time_embed, cotangent, pick_out, pick_in, shard, vec, biases[:, :2],
-        up_bias[:, None], seg_col, seg_row,
+    *saved, u, upstream, gain, pick_out, pick_in = forward(
+        tokens, time_embed, cotangent, to_owner, from_owner, segment_ids, shard, biases,
+        norm_gain, norm_bias, up_bias,
     )
     g_qkv, g_out, g_up, g_down, returned, sums = backward(
-        upstream, u, pick_out.reshape(micro * rows, rows), pick_in.reshape(mine * pack, pack),
-        saved, vec, seg_col, seg_row,
+        upstream, u, pick_out, pick_in, saved, gain, segment_ids
     )
     returned = returned.reshape(2, micro, rows, width).astype(F32)
     return (

time: 487 us -> 470 us (0.965); the launches traced: 484 us -> 461 us
  blocking collectives: 10.3 us -> 0 us
  other arithmetic: 9.51 us -> 3.13 us
  local copies, waits for them, and re-layouts: 15.2 us -> 10.2 us
    all_gather x2 -> x0, blocking collectives: 10.3 us -> none  [the longest x1 5.79 us: local(): vec = lax.all_gather(vec, 'tp', axis=2, tiled=True)]
where the time goes in v5:
time: 470 us; the launch traced here: 461 us
  Pallas kernels  446 us (95%)
  local copies, waits for them, and re-layouts  10.2 us (2%)
    pallas_call x1, Pallas kernels, backward(): pl.pallas_call(backward_kernel, in_specs=[whole] * 14 + [vmem] * 2, out_s...  224 us
    pallas_call x1, Pallas kernels, forward(): pl.pallas_call(forward_kernel, in_specs=[vmem] * 6 + [whole] + [vmem] * 4...  223 us

profile of v5, /device:TPU:8, one launch (start us, length us, event | category | flops | bytes accessed | tf_op | source)
XLA Modules:
  0.0 460.8 jit_solution(18015830248232840629)
XLA Ops:
  0.6 1.1 slice_bitcast_fusion.2
  1.7 2.5 pad_maximum_fusion
  4.2 222.5 %forward.1 = (bf16[6,1024,1024]{2,1,0:T(8,128)(2,1)}, bf16[2,2,512,1024]{3,2,1,0:T(8,128)(2,1)}, bf16[2,2,512,768]{3,2,1,0:T(8,128)(2,1)}, bf16[2,2,512,256]{3,2...) custom-call(bf16[4,256,256]{2,1,0:T(8,128)(2,1)} %tokens.1, ...), custom_call_target="tpu_custom_call" | custom-call | tf_op jit(solution)/shard_map/forward/pallas_call | solution.py:645
  226.8 223.8 %backward.1 = (f32[2,3,128,256]{3,2,1,0:T(8,128)}, f32[2,128,256]{2,1,0:T(8,128)}, f32[2,128,1024]{2,1,0:T(8,128)}, f32[2,128,1024]{2,1,0:T(8,128)}, bf16[2,1024...) custom-call(bf16[2,128,1024]{2,1,0:T(8,128)(2,1)} %get-tuple-element.31.up_in, bf16[2,128,1024]{2,1,0:T(8,128)(2,1)} %get-tuple-element.32.u_in, ...), custom_call_target="tpu_custom_call" | custom-call | tf_op jit(solution)/shard_map/backward/pallas_call | solution.py:1190
  450.5 0.0 copy-start.2
  450.6 0.0 copy-start.3
  450.6 0.8 slice_bitcast_fusion.3
  451.4 1.5 fusion.1
  452.8 0.6 copy.30
  453.4 0.6 pad_maximum_fusion.1
  454.1 0.0 copy-start.1
  454.1 2.8 fusion
  456.8 0.0 copy-start
  456.8 0.0 copy-done.2
  456.8 0.9 copy.35
  457.7 0.0 copy-done.3
  457.7 0.7 copy.36
  458.4 0.0 copy-done.1
  458.4 1.0 copy.37
  459.4 0.0 copy-done
  459.4 1.0 copy.38
Async XLA Ops:
  450.5 6.3 %copy-start.2 = (f32[2,3,128,256]{3,2,1,0:T(8,128)S(1)}, f32[2,3,128,256]{3,2,1,0:T(8,128)}, u32[]{:S(2)}) copy-start(f32[2,3,128,256]{3,2,1,0:T(8,128)} %get-tuple-element.73) | copy-start | bytes 2359300
  450.6 7.1 %copy-start.3 = (f32[2,128,256]{2,1,0:T(8,128)S(1)}, f32[2,128,256]{2,1,0:T(8,128)}, u32[]{:S(2)}) copy-start(f32[2,128,256]{2,1,0:T(8,128)} %get-tuple-element.74) | copy-start | bytes 786436
  454.1 4.4 copy-start.1
  456.8 2.6 copy-start
